TPU v7x, 128 devices: a whole 4x4x4 slice. The times are simulated.
128 devices in a mesh: seq: 32 (over z, x, y_hi), ffn: 4 (over y_lo, core).
Axes of the slice: x: 4, y: 4 (y_hi: 2, y_lo: 2; y = y_hi * 2 + y_lo), z: 4, core: 2. Of those that a mesh axis runs over, the one named last changes fastest.
Arguments:
- hidden_in: bfloat16 [4, 2048, 2048], P(None, 'seq'), may hold values from -6 to 6
- cotangent: bfloat16 [4, 2048, 2048], P(None, ('seq', 'ffn')), may hold values from -6 to 6
- doc_lengths: int32 [4, 8], replicated, may hold values from 0 to 2048, as said below
- inward: float32 [2048, 3, 2048], P('seq', None, 'ffn'), may hold values from -0.125 to 0.125
- inward_moment: float32 [2048, 3, 2048], P('seq', None, 'ffn'), may hold values from -0.00024414062 to 0.00024414062
- inward_squares: float32 [2048, 3, 2048], P('seq', None, 'ffn'), may hold values from 9.934108e-10 to 3.973643e-09
- outward: float32 [2048, 2048], P('ffn', 'seq'), may hold values from -0.125 to 0.125
- outward_moment: float32 [2048, 2048], P('ffn', 'seq'), may hold values from -0.00024414062 to 0.00024414062
- outward_squares: float32 [2048, 2048], P('ffn', 'seq'), may hold values from 9.934108e-10 to 3.973643e-09
- upward: float32 [2048, 4, 2048], P('seq', None, 'ffn'), may hold values from -0.125 to 0.125
- upward_moment: float32 [2048, 4, 2048], P('seq', None, 'ffn'), may hold values from -0.00024414062 to 0.00024414062
- upward_squares: float32 [2048, 4, 2048], P('seq', None, 'ffn'), may hold values from 9.934108e-10 to 3.973643e-09
- downward: float32 [4, 2048, 2048], P(None, 'ffn', 'seq'), may hold values from -0.0625 to 0.0625
- downward_moment: float32 [4, 2048, 2048], P(None, 'ffn', 'seq'), may hold values from -0.00024414062 to 0.00024414062
- downward_squares: float32 [4, 2048, 2048], P(None, 'ffn', 'seq'), may hold values from 9.934108e-10 to 3.973643e-09
- prenorm: float32 [4, 2048], replicated, may hold values from -0.9 to 2.5
- prenorm_moment: float32 [4, 2048], replicated, may hold values from -0.00024414062 to 0.00024414062
- prenorm_squares: float32 [4, 2048], replicated, may hold values from 9.934108e-10 to 3.973643e-09
- subnorm: float32 [2, 5, 2048], P(None, None, 'ffn'), may hold values from -0.9 to 2.5
- subnorm_moment: float32 [2, 5, 2048], P(None, None, 'ffn'), may hold values from -0.00024414062 to 0.00024414062
- subnorm_squares: float32 [2, 5, 2048], P(None, None, 'ffn'), may hold values from 9.934108e-10 to 3.973643e-09
Outputs:
- hidden_out: bfloat16 [4, 2048, 2048], P(None, ('seq', 'ffn'))
- input_grad: bfloat16 [4, 2048, 2048], P(None, 'seq')
- updated_inward: float32 [2048, 3, 2048], P('seq', None, 'ffn')
- moment_inward: float32 [2048, 3, 2048], P('seq', None, 'ffn')
- squares_inward: float32 [2048, 3, 2048], P('seq', None, 'ffn')
- updated_outward: float32 [2048, 2048], P('ffn', 'seq')
- moment_outward: float32 [2048, 2048], P('ffn', 'seq')
- squares_outward: float32 [2048, 2048], P('ffn', 'seq')
- updated_upward: float32 [2048, 4, 2048], P('seq', None, 'ffn')
- moment_upward: float32 [2048, 4, 2048], P('seq', None, 'ffn')
- squares_upward: float32 [2048, 4, 2048], P('seq', None, 'ffn')
- updated_downward: float32 [4, 2048, 2048], P(None, 'ffn', 'seq')
- moment_downward: float32 [4, 2048, 2048], P(None, 'ffn', 'seq')
- squares_downward: float32 [4, 2048, 2048], P(None, 'ffn', 'seq')
- updated_prenorm: float32 [4, 2048], replicated
- moment_prenorm: float32 [4, 2048], replicated
- squares_prenorm: float32 [4, 2048], replicated
- updated_subnorm: float32 [2, 5, 2048], P(None, None, 'ffn')
- moment_subnorm: float32 [2, 5, 2048], P(None, None, 'ffn')
- squares_subnorm: float32 [2, 5, 2048], P(None, None, 'ffn')
- grad_norm: float32 [], replicated
Inputs may be any that keep to these rules, and one draw needn't show every extreme that they name: `doc_lengths`: each row holds whole documents from its first slot on, in order; a 0 marks an unused entry and all entries after it are 0; every other entry is at least 100; a row's lengths sum to at most 2048, the rest of the row being padding. In each micro-batch of 2 consecutive rows one row is a single document of 2048 tokens.
All inputs are finite; a program needn't handle non-finite values.
Results may differ from a plain program's by a relative error of at most 0.035.
Values may be sent and summed in bfloat16 or wider, within the bound.
No kernel may reach another device: no remote copies, remote signals or barrier semaphores. Data moves between devices by JAX's collectives and lax.ppermute only.
A program may use at most 256 MiB of HBM per device.

v0:
```python
import math

import jax
import jax.numpy as jnp
import numpy as np
from jax import lax
from jax.experimental import pallas as pl
from jax.experimental.pallas import tpu as pltpu
from jax.sharding import Mesh
from jax.sharding import PartitionSpec as P

HDIM = 64
HALF = 32
FF = 8192
STEP = 10
Z, X, YH, YL, C = "seq_0", "seq_1", "seq_2", "ffn_0", "ffn_1"
FFN = (YL, C)
SEQ = (Z, X, YH)
SEQ_FFN = (Z, X, YH, YL, C)
ZX = (Z, X)
YY = (YH, YL)
EIGHT = (YH, YL, C)
TILE = 256

norm_eps = 1e-05
rope_base = 10000.0
xpos_base = 512.0
clip_limit = 1.0
beta_first = 0.9
beta_second = 0.95
adam_eps = 1e-08
decay_rate = 0.1
matrix_rate = 0.04
norm_rate = 0.6

F32 = jnp.float32
BF16 = jnp.bfloat16
SWAP = [(0, 1), (1, 0)]
MIB = 1024 * 1024


def xor_pairs(count, k):
    return [(i, i ^ k) for i in range(count)]


def dot(a, b, da, db):
    return lax.dot_general(a, b, (((da,), (db,)), ((), ())), preferred_element_type=F32)


def shape(dims, kind=F32):
    return jax.ShapeDtypeStruct(dims, kind)


def bytes_of(dims, kind):
    size = math.prod(dims[:-2]) * jnp.dtype(kind).itemsize
    tall = dims[-2] if len(dims) > 1 else 1
    return size * (-(-tall // 8) * 8) * (-(-dims[-1] // 128) * 128)


def in_hbm(out):
    return pltpu.HBM(out.shape, out.dtype)


def local_call(kernel, name, outs, ins, scratch=(), flops=0, moved=0, spare=4, far=(), stay=()):
    need = sum(bytes_of(a.shape, a.dtype) for a in (*ins, *outs))
    need += sum(bytes_of(s.shape, s.dtype) for s in scratch)
    scalar, vector = pltpu.SMEM, pltpu.VMEM
    return pl.pallas_call(
        kernel,
        out_shape=tuple(in_hbm(o) if n in far else o for n, o in enumerate(outs)),
        in_specs=[
            pl.BlockSpec(memory_space=scalar if a.dtype == jnp.int32 else vector) for a in ins
        ],
        out_specs=tuple(pl.BlockSpec(memory_space=vector) for _ in outs),
        scratch_shapes=list(scratch),
        compiler_params=pltpu.CompilerParams(vmem_limit_bytes=need + spare * MIB),
        cost_estimate=pl.CostEstimate(flops=flops, bytes_accessed=moved, transcendentals=0),
        name=name,
    )(*(pltpu.with_memory_space_constraint(a, pltpu.HBM) if n in stay else a for n, a in enumerate(ins)))


def turned(tile):
    return jnp.transpose(tile.astype(F32)).astype(BF16)


def forward_kernel(qkv_ref, start_ref, out_ref, low_ref, top_ref, q_s, k_s, v_s, s_s):
    blocks = q_s.shape[0]
    pieces = TILE // 128
    for i in range(blocks):
        for j in range(pieces):
            part = slice(j * 128, (j + 1) * 128)
            q_s[i, :, part] = qkv_ref[i * pieces + j, 0]
            k_s[i, part, :] = turned(qkv_ref[i * pieces + j, 1])
            v_s[i, :, part] = qkv_ref[i * pieces + j, 2]
    factor = math.log2(math.e) / math.sqrt(HDIM)
    key_line = lax.broadcasted_iota(jnp.int32, (TILE, TILE), 0)
    query_line = lax.broadcasted_iota(jnp.int32, (TILE, TILE), 1)
    for i in range(blocks):
        query = q_s[i]
        begin = start_ref[:, i * TILE : (i + 1) * TILE]
        peak = None
        for b in range(i + 1):
            s = dot(k_s[b], query, 1, 0) * factor
            keep = key_line >= begin - b * TILE
            if b == i:
                keep = keep & (key_line <= query_line)
            s = jnp.where(keep, s, -1e30)
            s_s[b] = s
            high = jnp.max(s, axis=0, keepdims=True)
            peak = high if peak is None else jnp.maximum(peak, high)
        total = jnp.zeros((1, TILE), F32)
        acc = jnp.zeros((HDIM, TILE), F32)
        for b in range(i + 1):
            e = jnp.exp2(s_s[b] - peak)
            total = total + jnp.sum(e, axis=0, keepdims=True)
            acc = acc + dot(v_s[b], e.astype(BF16), 1, 0)
        out = acc / total
        for j in range(pieces):
            out_ref[i * pieces + j] = out[:, j * 128 : (j + 1) * 128]
            low_ref[i * pieces + j] = out[:, j * 128 : (j + 1) * 128].astype(BF16)
        top_ref[:, i * TILE : (i + 1) * TILE] = peak + jnp.log2(total)


def backward_kernel(
    qkv_ref, do_ref, o_ref, top_ref, start_ref, rot_ref, out_ref,
    qt_s, kt_s, dot_s, q_s, k_s, v_s, do_s, dq_s, dk_s, dv_s,
):
    blocks = qt_s.shape[0]
    pieces = TILE // 128
    for i in range(blocks):
        for j in range(pieces):
            part = slice(j * 128, (j + 1) * 128)
            c = i * pieces + j
            qt_s[i, :, part] = qkv_ref[c, 0]
            kt_s[i, :, part] = qkv_ref[c, 1]
            dot_s[i, :, part] = do_ref[c]
            q_s[i, part, :] = turned(qkv_ref[c, 0])
            k_s[i, part, :] = turned(qkv_ref[c, 1])
            v_s[i, part, :] = turned(qkv_ref[c, 2])
            do_s[i, part, :] = turned(do_ref[c])
    scale = 1.0 / math.sqrt(HDIM)
    factor = math.log2(math.e) * scale
    key_line = lax.broadcasted_iota(jnp.int32, (TILE, TILE), 0)
    query_line = lax.broadcasted_iota(jnp.int32, (TILE, TILE), 1)
    for i in range(blocks):
        span = slice(i * TILE, (i + 1) * TILE)
        begin = start_ref[:, span]
        top = top_ref[:, span]
        delta = jnp.concatenate(
            [
                jnp.sum(
                    do_ref[i * pieces + j].astype(F32) * o_ref[i * pieces + j],
                    axis=0,
                    keepdims=True,
                )
                for j in range(pieces)
            ],
            axis=1,
        )
        dq = jnp.zeros((HDIM, TILE), F32)
        for b in range(i + 1):
            s = dot(k_s[b], qt_s[i], 1, 0) * factor
            keep = key_line >= begin - b * TILE
            if b == i:
                keep = keep & (key_line <= query_line)
            p = jnp.where(keep, jnp.exp2(s - top), 0.0)
            dp = dot(v_s[b], dot_s[i], 1, 0)
            ds = (p * (dp - delta)).astype(BF16)
            dq = dq + dot(kt_s[b], ds, 1, 0)
            dk = dot(ds, q_s[i], 1, 0)
            dv = dot(p.astype(BF16), do_s[i], 1, 0)
            if b == i:
                dk_s[b] = dk
                dv_s[b] = dv
            else:
                dk_s[b] += dk
                dv_s[b] += dv
        dq_s[i] = dq
    for i in range(blocks):
        span = slice(i * TILE, (i + 1) * TILE)
        dq = dq_s[i] * scale
        dk = jnp.transpose(dk_s[i]) * scale
        dv = jnp.transpose(dv_s[i])
        results = []
        for n, g in enumerate((dq, dk)):
            co, si = rot_ref[2 * n, :, span], rot_ref[2 * n + 1, :, span]
            front, back = g[:HALF], g[HALF:]
            results.append(
                jnp.concatenate([front * co + back * si, back * co - front * si], axis=0)
            )
        results.append(dv)
        for n, g in enumerate(results):
            for j in range(pieces):
                out_ref[i * pieces + j, n] = g[:, j * 128 : (j + 1) * 128].astype(BF16)


def attend(qkv, start):
    count = qkv.shape[0]
    blocks = count * 128 // TILE
    return pl.pallas_call(
        forward_kernel,
        out_shape=(
            pltpu.HBM((count, HDIM, 128), F32),
            pltpu.HBM((count, HDIM, 128), BF16),
            jax.ShapeDtypeStruct((1, count * 128), F32),
        ),
        scratch_shapes=[
            pltpu.VMEM((blocks, HDIM, TILE), BF16),
            pltpu.VMEM((blocks, TILE, HDIM), BF16),
            pltpu.VMEM((blocks, HDIM, TILE), BF16),
            pltpu.VMEM((blocks, TILE, TILE), F32),
        ],
        compiler_params=pltpu.CompilerParams(vmem_limit_bytes=20 * MIB),
        cost_estimate=pl.CostEstimate(
            flops=2000000000, bytes_accessed=4000000, transcendentals=2400000
        ),
        name="attend",
    )(qkv, start)


def attend_back(qkv, d_out, out, top, start, tables):
    count = qkv.shape[0]
    blocks = count * 128 // TILE
    wide = pltpu.VMEM((blocks, HDIM, TILE), BF16)
    tall = pltpu.VMEM((blocks, TILE, HDIM), BF16)
    return pl.pallas_call(
        backward_kernel,
        out_shape=pltpu.HBM((count, 3, HDIM, 128), BF16),
        scratch_shapes=[
            wide, wide, wide, tall, tall, tall, tall,
            pltpu.VMEM((blocks, HDIM, TILE), F32),
            pltpu.VMEM((blocks, TILE, HDIM), F32),
            pltpu.VMEM((blocks, TILE, HDIM), F32),
        ],
        compiler_params=pltpu.CompilerParams(vmem_limit_bytes=28 * MIB),
        cost_estimate=pl.CostEstimate(
            flops=6000000000, bytes_accessed=6000000, transcendentals=2400000
        ),
        name="attend_back",
    )(qkv, d_out, out, top, start, tables)


def rotation_tables(row_slots):
    index_half = np.arange(HALF, dtype=np.float64)
    places = np.arange(row_slots, dtype=np.float64) - row_slots // 2
    inverse = rope_base ** (-2.0 * index_half / HDIM)
    angles = inverse[:, None] * places[None, :]
    zeta = (2.0 * index_half + 0.4 * HDIM) / (1.4 * HDIM)
    stretch = zeta[:, None] ** (places[None, :] / xpos_base)
    cosine, sine = np.cos(angles), np.sin(angles)
    tables = [cosine * stretch, sine * stretch, cosine / stretch, sine / stretch]
    return np.stack(tables).astype(np.float32)


def moments(values):
    center = jnp.mean(values, axis=-1, keepdims=True)
    spread = jnp.mean(jnp.square(values - center), axis=-1, keepdims=True)
    inverse = lax.rsqrt(spread + norm_eps)
    return (values - center) * inverse, inverse


def norm_back(upstream, gain, normed, inverse):
    scaled = upstream * gain
    return inverse * (
        scaled
        - jnp.mean(scaled, axis=-1, keepdims=True)
        - normed * jnp.mean(scaled * normed, axis=-1, keepdims=True)
    )


def place_parts(parts, target, me):
    share = parts[0].shape[0]
    for k, part in enumerate(parts):
        target[pl.ds(pl.multiple_of((me ^ k) * share, share), share), :] = part[...]


def take_for_scatter(source, target, me):
    share = source.shape[0] // 8
    for side in range(2):
        for j in range(4):
            at = pl.multiple_of((me ^ (2 * j + side)) * share, share)
            target[pl.ds((side * 4 + j) * share, share), :] = source[pl.ds(at, share), :]


def scatter_product(left, right, keep_ref, send_ref, width=None):
    half = left.shape[0] // 2
    width = width or keep_ref.shape[1]
    step = 256

    def body(i, _):
        at = pl.ds(pl.multiple_of(i * step, step), step)
        product = dot(left[...], right[at, : left.shape[1]], 1, 1)
        keep_ref[:, at] = product[:half]
        send_ref[:, at] = product[half:].astype(BF16)
        return 0

    lax.fori_loop(0, width // step, body, 0)


def project_kernel(
    ids, here_ref, near_ref, far_ref, pre_ref, rot_ref, w_ref, qkv_ref, hat_ref, a_ref, x_s, y_s
):
    half, core = ids[1], ids[2]
    rows, slots, width = here_ref.shape
    other = (1 - half) * slots
    for r in range(rows):
        x_s[pl.ds(pl.multiple_of(half * slots, slots), slots), :] = here_ref[r]
        x_s[pl.ds(pl.multiple_of(other + core * 32, 32), 32), :] = near_ref[r]
        x_s[pl.ds(pl.multiple_of(other + (1 - core) * 32, 32), 32), :] = far_ref[r]
        normed, _ = moments(x_s[...].astype(F32))
        low = normed * pre_ref[0:1] + pre_ref[1:2]
        hat_ref[r * 2 * slots : (r + 1) * 2 * slots, :] = normed.astype(BF16)
        a_ref[r * 2 * slots : (r + 1) * 2 * slots, :] = low.astype(BF16)
    span = 2 * slots
    heads = y_s.shape[1] // HDIM
    for n in range(3):
        y_s[...] = dot(a_ref[...], w_ref[:, n * heads * HDIM : (n + 1) * heads * HDIM], 1, 0)
        for r in range(rows):
            for pair in range(heads // 2):
                t = jnp.transpose(
                    y_s[r * span : (r + 1) * span, pair * 128 : (pair + 1) * 128]
                )
                for e in range(2):
                    g = t[e * HDIM : (e + 1) * HDIM]
                    if n < 2:
                        co, si = rot_ref[2 * n], rot_ref[2 * n + 1]
                        front, back = g[:HALF], g[HALF:]
                        g = jnp.concatenate(
                            [front * co - back * si, front * si + back * co], axis=0
                        )
                    qkv_ref[r * heads + pair * 2 + e, n] = g.astype(BF16)


def inner_moments(sums_ref, width, row=0):
    sums = sums_ref[0]
    for k in range(1, 8):
        sums = sums + sums_ref[k]
    center = sums[row : row + 1] / width
    inverse = lax.rsqrt(sums[row + 1 : row + 2] / width - center * center + norm_eps)
    return sums, center, inverse


def high_low(value):
    high = value.astype(BF16).astype(F32)
    return [high, value - high]


def out_kernel(
    ids, o_ref, gain_ref, w_ref, keep_ref, send_ref, line_ref, c_s, sum_s, l_s, k_s
):
    count, _, span = o_ref.shape
    heads = count // 4
    width = w_ref.shape[0]
    half = keep_ref.shape[0]
    for r in range(4):
        o = jnp.concatenate([o_ref[r * heads + h] for h in range(heads)], axis=0).astype(F32)
        first = jnp.sum(o, axis=0, keepdims=True)
        second = jnp.sum(o * o, axis=0, keepdims=True)
        line_ref[0:1, r * span : (r + 1) * span] = first
        line_ref[1:2, r * span : (r + 1) * span] = second
        lines = [first, second, *high_low(first), *high_low(second)]
        lines.append(jnp.zeros((128 - len(lines), span), F32))
        sums = jnp.transpose(jnp.concatenate(lines, axis=0))
        c = jnp.transpose(o * gain_ref[...]).astype(BF16)
        for s in range(8):
            at = slice(s * 64 + r * 16, s * 64 + (r + 1) * 16)
            c_s[at, :] = c[s * 16 : (s + 1) * 16]
            sum_s[at, :] = sums[s * 16 : (s + 1) * 16]
    take_for_scatter(c_s, l_s, ids[0])
    take_for_scatter(sum_s, k_s, ids[0])
    scatter_product(l_s, w_ref, keep_ref, send_ref, width)
    keep_ref[:, width:] = k_s[:half]
    send_ref[:, width:] = k_s[half:].astype(BF16)


def normed_heads_kernel(o_ref, sums_ref, gain_ref, shift_ref, c_ref, *, width):
    count, _, span = o_ref.shape
    heads = count // 4
    _, center, inverse = inner_moments(sums_ref, width, 4)
    for r in range(4):
        at = slice(r * span, (r + 1) * span)
        o = jnp.concatenate([o_ref[r * heads + h] for h in range(heads)], axis=0).astype(F32)
        c = (o - center[:, at]) * inverse[:, at] * gain_ref[...] + shift_ref[...]
        c = jnp.transpose(c).astype(BF16)
        for s in range(8):
            c_ref[s * 64 + r * 16 : s * 64 + (r + 1) * 16, :] = c[s * 16 : (s + 1) * 16]


def gain_product_kernel(gain_ref, shift_ref, w_ref, out_ref):
    rows = [*high_low(gain_ref[...]), *high_low(shift_ref[...])]
    rows = jnp.concatenate(rows + [jnp.zeros((12, rows[0].shape[1]), F32)], axis=0).astype(BF16)
    product = dot(rows, w_ref[...], 1, 1)
    both = [product[0:1] + product[1:2], product[2:3] + product[3:4]]
    out_ref[...] = jnp.concatenate(both + [jnp.zeros((6, product.shape[1]), F32)], axis=0)


def two_sums(stats, other):
    first = stats[:, 0:1] + (other[:, 2:3] + other[:, 3:4])
    second = stats[:, 1:2] + (other[:, 4:5] + other[:, 5:6])
    return first, second


def core_sum_stats_kernel(keep_ref, got_ref, own_ref, one_ref, two_ref, three_ref):
    share = own_ref.shape[0]
    width = own_ref.shape[1] - 128
    both = keep_ref[:, :width] + got_ref[:, :width].astype(F32)
    first, second = two_sums(keep_ref[:, width:], got_ref[:, width:].astype(F32))
    lane = lax.broadcasted_iota(jnp.int32, (keep_ref.shape[0], 128), 1)
    stats = jnp.zeros(lane.shape, F32)
    for n, v in enumerate([first, second, *high_low(first), *high_low(second)]):
        stats = jnp.where(lane == n, v, stats)
    own_ref[:, :width] = both[:share]
    own_ref[:, width:] = stats[:share]
    for j, ref in ((1, one_ref), (2, two_ref), (3, three_ref)):
        ref[:, :width] = both[j * share : (j + 1) * share].astype(BF16)
        ref[:, width:] = stats[j * share : (j + 1) * share].astype(BF16)


def core_sum_kernel(keep_ref, got_ref, own_ref, one_ref, two_ref, three_ref):
    share = own_ref.shape[0]
    both = keep_ref[...] + got_ref[...].astype(F32)
    own_ref[...] = both[:share]
    for j, ref in ((1, one_ref), (2, two_ref), (3, three_ref)):
        ref[...] = both[j * share : (j + 1) * share].astype(BF16)


def summed(own_ref, refs):
    total = own_ref[...]
    for ref in refs:
        total = total + ref[...].astype(F32)
    return total


def middle_kernel(
    own_ref, one, two, three, x_ref, usable_ref, pre_ref, g_ref, g_one, g_two, g_three,
    r1_ref, bb_ref,
):
    width = r1_ref.shape[1]
    total = own_ref[...]
    product, stats = total[:, :width], total[:, width:]
    for ref in (one, two, three):
        product = product + ref[:, :width].astype(F32)
        first, second = two_sums(stats, ref[:, width:].astype(F32))
        lane = lax.broadcasted_iota(jnp.int32, stats.shape, 1)
        stats = jnp.where(lane == 0, first, jnp.where(lane == 1, second, 0.0))
    center = stats[:, 0:1] / width
    inverse = lax.rsqrt(stats[:, 1:2] / width - center * center + norm_eps)
    g = (g_ref[...] + g_one[...]) + (g_two[...] + g_three[...])
    attn = inverse * (product - center * g[0:1]) + g[1:2]
    r1 = x_ref[...].astype(F32) + usable_ref[...] * attn
    normed, _ = moments(r1)
    r1_ref[...] = r1
    bb_ref[...] = (normed * pre_ref[2:3] + pre_ref[3:4]).astype(BF16)


def result_kernel(own_ref, one, two, three, r1_ref, usable_ref, out_ref):
    f = summed(own_ref, (one, two, three))
    out_ref[...] = (r1_ref[...] + usable_ref[...] * f).astype(BF16)


def down_back_kernel(ids, *refs):
    parts, (w_ref, df_ref, dhn_ref) = refs[:8], refs[8:]
    place_parts(parts, df_ref, ids[0])

    def body(i, _):
        at = pl.ds(pl.multiple_of(i * 256, 256), 256)
        dhn_ref[:, at] = dot(df_ref[...], w_ref[:, at], 1, 0)
        return 0

    lax.fori_loop(0, dhn_ref.shape[1] // 256, body, 0)


def up_kernel(ids, *refs):
    parts, refs = refs[:8], refs[8:]
    w_ref, dhn_ref, gain_ref, o_ref, bb_ref, h_ref, slope_ref, sums_ref = refs
    place_parts(parts, bb_ref, ids[0])
    tokens, units = h_ref.shape
    step = 256

    def body(i, carry):
        at = pl.ds(pl.multiple_of(i * step, step), step)
        u = dot(bb_ref[...], w_ref[:, at], 1, 0)
        cdf = 0.5 * (1.0 + lax.erf(u * (1.0 / math.sqrt(2.0))))
        h = u * cdf
        h_ref[:, at] = h
        slope_ref[:, at] = cdf + u * (
            jnp.exp(-0.5 * u * u) * (1.0 / math.sqrt(2.0 * math.pi))
        )
        scaled = dhn_ref[:, at] * gain_ref[:, at]
        terms = (h, h * h, scaled, scaled * h)
        return tuple(c + jnp.sum(t, axis=1, keepdims=True) for c, t in zip(carry, terms))

    zero = jnp.zeros((tokens, 1), F32)
    sums = lax.fori_loop(0, units // step, body, (zero,) * 4)
    lane = lax.broadcasted_iota(jnp.int32, (tokens, 128), 1)
    wide = jnp.zeros((tokens, 128), F32)
    for n, s in enumerate(sums):
        wide = jnp.where(lane == n, s, wide)
    line = jnp.transpose(wide)
    line = jnp.concatenate([line[:4], o_ref[...], line[6:8]], axis=0)
    for k in range(8):
        sums_ref[k] = line


def inner_back_kernel(
    ids, h_ref, slope_ref, dhn_ref, sums_ref, gain_ref, shift_ref, w_ref,
    keep_ref, send_ref, hn_ref, du_ref, sub_ref, l_s,
):
    sums, center, inverse = inner_moments(sums_ref, FF)
    mean_scaled = sums[2:3] / FF
    mean_both = inverse * (sums[3:4] / FF - center * mean_scaled)
    rows = jnp.concatenate([center, inverse, mean_scaled, mean_both, sums[4:8]], axis=0)
    columns = jnp.transpose(jnp.concatenate([rows] * 16, axis=0))
    tokens = h_ref.shape[0]
    center, inverse, mean_scaled, mean_both = (columns[:, n : n + 1] for n in range(4))
    units = h_ref.shape[1]

    def body(i, _):
        at = pl.ds(pl.multiple_of(i * 256, 256), 256)
        hat = (h_ref[:, at] - center) * inverse
        dhn = dhn_ref[:, at]
        gain = gain_ref[:, at]
        hn_ref[:, at] = (hat * gain + shift_ref[:, at]).astype(BF16)
        du = inverse * (dhn * gain - mean_scaled - hat * mean_both) * slope_ref[:, at]
        du_ref[:, at] = du.astype(BF16)
        sub_ref[0:1, at] = jnp.sum(dhn * hat, axis=0, keepdims=True)
        sub_ref[1:2, at] = jnp.sum(dhn, axis=0, keepdims=True)
        return 0

    lax.fori_loop(0, units // 256, body, 0)
    take_for_scatter(du_ref, l_s, ids[0])
    scatter_product(l_s, w_ref, keep_ref, send_ref)


def down_kernel(ids, hn_ref, w_ref, keep_ref, send_ref, l_s):
    take_for_scatter(hn_ref, l_s, ids[0])
    scatter_product(l_s, w_ref, keep_ref, send_ref)


def mlp_grad_kernel(df_ref, hn_ref, bb_ref, du_ref, out_ref):
    units = hn_ref.shape[1]
    out_ref[:, :units] = dot(jnp.transpose(bb_ref[...]), du_ref[...], 1, 0).astype(BF16)
    out_ref[:, units:] = dot(jnp.transpose(df_ref[...]), hn_ref[...], 1, 0).astype(BF16)


def mlp_grad(df, hn, bb, du):
    tokens, width = df.shape
    units = hn.shape[1]
    step = 256
    narrow = pl.BlockSpec((tokens, step), lambda i: (0, i))
    whole = pl.BlockSpec((tokens, units), lambda i: (0, 0))
    return pl.pallas_call(
        mlp_grad_kernel,
        grid=(width // step,),
        out_shape=pltpu.HBM((width, 2 * units), BF16),
        in_specs=[narrow, whole, narrow, whole],
        out_specs=pl.BlockSpec((step, 2 * units), lambda i: (i, 0)),
        compiler_params=pltpu.CompilerParams(vmem_limit_bytes=20 * MIB),
        cost_estimate=pl.CostEstimate(
            flops=4 * tokens * width * units, bytes_accessed=14 * MIB, transcendentals=0
        ),
        name="mlp_grad",
    )(df, hn, bb, du)


def middle_back_kernel(
    own_ref, one, two, three, r1_ref, cot_ref, usable_ref, pre_ref, dr1_ref, dattn_ref, grad_ref
):
    dbb = summed(own_ref, (one, two, three))
    hat, inverse = moments(r1_ref[...])
    dr1 = cot_ref[...].astype(F32) + norm_back(dbb, pre_ref[2:3], hat, inverse)
    dr1_ref[...] = dr1
    dattn_ref[...] = (usable_ref[...] * dr1).astype(BF16)
    grad_ref[0:1] = jnp.sum(dbb * hat, axis=0, keepdims=True)
    grad_ref[1:2] = jnp.sum(dbb, axis=0, keepdims=True)


def out_back_kernel(ids, *refs):
    parts, refs = refs[:8], refs[8:]
    w_ref, o_ref, sums_ref, gain_ref, dattn_ref, dc_ref, out_ref, sub_ref, y_s = refs
    place_parts(parts, dattn_ref, ids[0])
    y_s[...] = dot(dattn_ref[...], w_ref[...], 1, 0)
    count, _, span = o_ref.shape
    heads = count // 4
    _, center, inverse = inner_moments(sums_ref, dattn_ref.shape[1], 4)
    gain_grad, shift_grad, lines = 0.0, 0.0, []
    for r in range(4):
        at = slice(r * span, (r + 1) * span)
        dc = jnp.concatenate(
            [y_s[s * 64 + r * 16 : s * 64 + (r + 1) * 16, :] for s in range(8)], axis=0
        )
        dc = jnp.transpose(dc)
        dc_ref[:, at] = dc
        o = jnp.concatenate([o_ref[r * heads + h] for h in range(heads)], axis=0).astype(F32)
        hat = (o - center[:, at]) * inverse[:, at]
        gain_grad = gain_grad + jnp.sum(dc * hat, axis=1, keepdims=True)
        shift_grad = shift_grad + jnp.sum(dc, axis=1, keepdims=True)
        scaled = dc * gain_ref[...]
        lines.append(
            jnp.concatenate(
                [
                    jnp.sum(scaled, axis=0, keepdims=True),
                    jnp.sum(scaled * hat, axis=0, keepdims=True),
                    jnp.zeros((6, span), F32),
                ],
                axis=0,
            )
        )
    line = jnp.concatenate(lines, axis=1)
    for k in range(8):
        out_ref[k] = line
    sub_ref[...] = jnp.concatenate(
        [
            jnp.transpose(jnp.broadcast_to(g, (g.shape[0], 128)))[0:1]
            for g in (gain_grad, shift_grad)
        ],
        axis=0,
    )


def head_grad_kernel(dc_ref, o_ref, sums_ref, back_ref, gain_ref, out_ref, *, width):
    count, _, span = o_ref.shape
    heads = count // 4
    _, center, inverse = inner_moments(sums_ref, width, 4)
    back = back_ref[0]
    for k in range(1, 8):
        back = back + back_ref[k]
    for r in range(4):
        at = slice(r * span, (r + 1) * span)
        first, second = back[0:1, at] / width, back[1:2, at] / width
        for h in range(heads):
            part = slice(h * HDIM, (h + 1) * HDIM)
            hat = (o_ref[r * heads + h].astype(F32) - center[:, at]) * inverse[:, at]
            scaled = dc_ref[part, at] * gain_ref[part]
            out_ref[r * heads + h] = (
                inverse[:, at] * (scaled - first - hat * second)
            ).astype(BF16)


def out_grad_kernel(dattn_ref, c_ref, out_ref):
    out_ref[...] = dot(jnp.transpose(dattn_ref[...]), c_ref[...], 1, 0).astype(BF16)


def out_grad(dattn, c):
    tokens, width = dattn.shape
    units = c.shape[1]
    step = 512
    return pl.pallas_call(
        out_grad_kernel,
        grid=(width // step,),
        out_shape=pltpu.HBM((width, units), BF16),
        in_specs=[
            pl.BlockSpec((tokens, step), lambda i: (0, i)),
            pl.BlockSpec((tokens, units), lambda i: (0, 0)),
        ],
        out_specs=pl.BlockSpec((step, units), lambda i: (i, 0)),
        compiler_params=pltpu.CompilerParams(vmem_limit_bytes=16 * MIB),
        cost_estimate=pl.CostEstimate(
            flops=2 * tokens * width * units, bytes_accessed=4 * MIB, transcendentals=0
        ),
        name="out_grad",
    )(dattn, c)


def turn_kernel(ids, a_ref, out_ref):
    for r in range(16):
        at = pl.ds(pl.multiple_of((ids[3] ^ r) * 128, 128), 128)
        to = (r % 4) * 4 + r // 4
        out_ref[to * 128 : (to + 1) * 128, :] = jnp.transpose(a_ref[:, at])


def column(row):
    return jnp.transpose(jnp.broadcast_to(row, (128, row.shape[1])))[:, 0:1]


def row_of(col):
    return jnp.transpose(jnp.broadcast_to(col, (col.shape[0], 128)))[0:1]


def in_grad_kernel(
    ids, dqkv_ref, xt_ref, w_ref, pre_ref, out_ref, three_ref, o_ref, h_ref, *refs
):
    lines, (tokens_ref, d_s, one_s) = refs[:8], refs[8:]
    count = dqkv_ref.shape[0]
    heads = count // 4
    units = d_s.shape[0]
    for r in range(4):
        for n in range(3):
            for h in range(heads):
                base = (n * heads + h) * HDIM
                d_s[base : base + HDIM, r * 128 : (r + 1) * 128] = dqkv_ref[r * heads + h, n]
    sums = []
    for n in range(0, units, 128):
        total = jnp.zeros((1, 128), F32)
        for r in range(4):
            t = jnp.transpose(d_s[n : n + 128, r * 128 : (r + 1) * 128].astype(F32))
            total = total + jnp.sum(t, axis=0, keepdims=True)
            t = t.astype(BF16)
            for s in range(8):
                tokens_ref[s * 64 + r * 16 : s * 64 + (r + 1) * 16, n : n + 128] = t[
                    s * 16 : (s + 1) * 16
                ]
        sums.append(total)
    sums = jnp.concatenate(sums, axis=1)
    for j in range(4):
        products = dot(xt_ref[j * 512 : (j + 1) * 512, :], d_s[...], 1, 1)
        for i in range(4):
            at = pl.ds(pl.multiple_of((ids[3] ^ (4 * i + j)) * 128, 128), 128)
            product = products[i * 128 : (i + 1) * 128]
            gradient = product * column(pre_ref[0:1, at]) + column(pre_ref[1:2, at]) * sums
            gradient = gradient.astype(BF16)
            lines[j][i * 64 : (i + 1) * 64, :units] = gradient[:64]
            lines[4 + i][j * 64 : (j + 1) * 64, :units] = gradient[64:]
            outward = out_ref[at, :]
            lines[j][i * 64 : (i + 1) * 64, units:] = outward[:64]
            lines[4 + i][j * 64 : (j + 1) * 64, units:] = outward[64:]
            w = w_ref[at, :units].astype(F32)
            one_s[0:1, at] = row_of(jnp.sum(w * product, axis=1, keepdims=True))
            one_s[1:2, at] = row_of(jnp.sum(w * sums, axis=1, keepdims=True))
    width = lines[0].shape[1]
    half = o_ref.shape[1]
    small = []
    for ref in (one_s, three_ref):
        for n in range(2):
            small += [ref[n : n + 1, :width], ref[n : n + 1, width:]]
    for n in range(2):
        first = [o_ref[n : n + 1], h_ref[n : n + 1, : width - half]]
        last = [h_ref[n : n + 1, width - half :], jnp.zeros((1, width - half), F32)]
        small += [jnp.concatenate(first, axis=1), jnp.concatenate(last, axis=1)]
    small.append(jnp.zeros((16 - len(small), width), F32))
    small = jnp.concatenate(small, axis=0).astype(BF16)
    for j in range(4):
        lines[j][256:272, :] = small


def in_back_kernel(ids, d_ref, w_ref, keep_ref, send_ref, l_s):
    take_for_scatter(d_ref, l_s, ids[0])
    scatter_product(l_s, w_ref, keep_ref, send_ref)


def summed_low(refs):
    total = refs[0][...].astype(F32)
    for ref in refs[1:]:
        total = total + ref[...].astype(F32)
    return total


def line_sum_kernel(*refs):
    first, second, outs = refs[:4], refs[4:8], refs[8:]
    total = summed_low(first)
    small = total[256:272]
    outs[0][0:64, :] = total[0:64]
    outs[0][64:80, :] = small
    for k in (1, 2, 3):
        outs[k][0:64, :] = total[k * 64 : (k + 1) * 64].astype(BF16)
        outs[k][64:80, :] = small.astype(BF16)
    total = summed_low(second)
    outs[4][...] = total[0:64]
    for k in (1, 2, 3):
        outs[4 + k][...] = total[k * 64 : (k + 1) * 64].astype(BF16)


def last_sum_kernel(ids, *refs):
    ins, (mlp_ref, keep_ref, give_ref, out_ref) = refs[:8], refs[8:]
    width = keep_ref.shape[1]
    low = ids[1] == 0
    second = summed_low(ins[4:])
    slots = second.shape[0]
    total = summed_low(ins[:4])
    first, small = total[:slots], total[slots:]
    keep_ref[:slots, :] = jnp.where(low, first, second).astype(BF16)
    give_ref[:slots, :] = jnp.where(low, second, first).astype(BF16)
    keep_ref[slots:, :] = small.astype(BF16)
    give_ref[slots:, :] = small.astype(BF16)
    squares = whole_sum(first * first + second * second) + mlp_ref[0:1, 0:1]

    def joined(begin):
        return jnp.concatenate([small[begin : begin + 1], small[begin + 1 : begin + 2]], axis=1)

    sub = jnp.concatenate([joined(8), joined(10)], axis=0)
    lane = lax.broadcasted_iota(jnp.int32, (4, 2 * width), 1)
    scalars = jnp.zeros(lane.shape, F32)
    for n, term in enumerate([*high_low(squares), *high_low(whole_sum(sub * sub))]):
        scalars = jnp.where(lane // 128 == n, term, scalars)
    lines = jnp.concatenate([joined(2 * n) for n in range(4)] + [scalars], axis=0).astype(BF16)
    for k in range(out_ref.shape[0]):
        out_ref[k] = lines


def group_total_kernel(small_ref, total_ref, out_ref):
    total = small_ref[0].astype(F32)
    for k in range(1, small_ref.shape[0]):
        total = total + small_ref[k].astype(F32)
    total_ref[...] = total
    squares = total[4:5, 0:128] + total[4:5, 128:256]
    for k in range(out_ref.shape[0]):
        out_ref[k] = jnp.broadcast_to(squares, out_ref.shape[1:])


def input_back_kernel(own_ref, one, two, three, x_ref, dr1_ref, pre_ref, out_ref):
    da = summed(own_ref, (one, two, three))
    hat, inverse = moments(x_ref[...].astype(F32))
    out_ref[...] = (dr1_ref[...] + norm_back(da, pre_ref[0:1], hat, inverse)).astype(BF16)


def whole_sum(values):
    return jnp.sum(jnp.sum(values, axis=1, keepdims=True), axis=0, keepdims=True)


def rest_kernel(ids, g_ref, keep_ref, give_ref, sum_ref):
    slots = keep_ref.shape[0]
    half = ids[1]
    keep_ref[...] = g_ref[pl.ds(pl.multiple_of(half * slots, slots), slots), :]
    give_ref[...] = g_ref[pl.ds(pl.multiple_of((1 - half) * slots, slots), slots), :]
    total = jnp.zeros((1, 1), F32)
    for k in range(g_ref.shape[0] // 32):
        g = g_ref[k * 32 : (k + 1) * 32, :].astype(F32)
        total = total + whole_sum(g * g)
    sum_ref[...] = jnp.broadcast_to(total, sum_ref.shape)


def adam_step(weight, moment, squares, gradient, factor, step_rate, decay_weight):
    clipped = gradient * factor
    moment_new = beta_first * moment + (1.0 - beta_first) * clipped
    squares_new = beta_second * squares + (1.0 - beta_second) * clipped * clipped
    moment_hat = moment_new * (1.0 / (1.0 - beta_first**STEP))
    squares_hat = squares_new * (1.0 / (1.0 - beta_second**STEP))
    updated = weight - step_rate * (
        moment_hat / (jnp.sqrt(squares_hat) + adam_eps) + decay_weight * weight
    )
    return updated, moment_new, squares_new


def adam_kernel(
    ids, small_ref, norm_part, sub_own, sub_take, att_keep, att_take, mlp_keep, mlp_take, *refs
):
    states, outs, norm_out = refs[:18], refs[18:36], refs[36]
    low = ids[1] == 0
    squares = norm_part[0, 0:1, 0:1]
    for k in range(1, norm_part.shape[0]):
        squares = squares + norm_part[k, 0:1, 0:1]
    pre = small_ref[0:4]
    squares = squares + small_ref[4:5, 256:257] + small_ref[4:5, 384:385] + whole_sum(pre * pre)
    norm = jnp.sqrt(squares)
    factor = jnp.minimum(1.0, clip_limit / (norm + 1e-06))
    half = att_keep.shape[1] // 4

    def pair(mine, theirs, at):
        mine = mine[:, at * half : (at + 1) * half].astype(F32)
        theirs = theirs[:, at * half : (at + 1) * half].astype(F32)
        return jnp.concatenate(
            [jnp.where(low, mine, theirs), jnp.where(low, theirs, mine)], axis=1
        )

    def step(which, index, gradient, rate, decay):
        state = [states[3 * which + n][index] for n in range(3)]
        for n, value in enumerate(adam_step(*state, gradient, factor, rate, decay)):
            outs[3 * which + n][index] = value

    everything = slice(None)
    for k in range(3):
        step(0, (k,), pair(att_keep, att_take, k), matrix_rate, decay_rate)
    step(1, (everything,), pair(att_keep, att_take, 3), matrix_rate, decay_rate)
    for b in range(4):
        step(2, (everything, b), pair(mlp_keep, mlp_take, b), matrix_rate, decay_rate)
        step(3, (b,), pair(mlp_keep, mlp_take, 4 + b), matrix_rate, decay_rate)

    @pl.when(pl.program_id(0) == 0)
    def _():
        step(4, (everything,), pre, norm_rate, 0.0)
        for b in range(5):
            row, at = (0, b) if b < 4 else (1, 0)
            both = pair(sub_own, sub_take, at)
            both = jnp.concatenate([both[8 + row : 9 + row], both[10 + row : 11 + row]], axis=0)
            step(5, (b,), both, norm_rate, 0.0)
        norm_out[...] = jnp.broadcast_to(norm, norm_out.shape)


def adam(ids, small, norm_part, gradients, states):
    flat = [a for state in states for a in state]
    step = 32

    def whole(a):
        return pl.BlockSpec(a.shape, lambda i, nd=a.ndim: (0,) * nd)

    def blocks(which, a):
        if which > 3:
            return whole(a)
        dim = (1, 0, 0, 1)[which]
        block = tuple(step if n == dim else d for n, d in enumerate(a.shape))
        return pl.BlockSpec(
            block, lambda i, nd=a.ndim, dim=dim: tuple(i if n == dim else 0 for n in range(nd))
        )

    specs = [blocks(n // 3, a) for n, a in enumerate(flat)]
    rows = [pl.BlockSpec((step, g.shape[1]), lambda i: (i, 0)) for g in gradients]
    a_rows = gradients[2].shape[0] // 16
    norm = shape((8, 128))
    return pl.pallas_call(
        adam_kernel,
        grid=(gradients[2].shape[0] // step,),
        out_shape=tuple(shape(a.shape) for a in flat) + (norm,),
        in_specs=[
            pl.BlockSpec(memory_space=pltpu.SMEM),
            whole(small),
            whole(norm_part),
            *(pl.BlockSpec((16, a.shape[1]), lambda i: (a_rows, 0)) for a in gradients[:2]),
            *rows,
            *specs,
        ],
        out_specs=tuple(specs) + (whole(norm),),
        compiler_params=pltpu.CompilerParams(vmem_limit_bytes=56 * MIB),
        cost_estimate=pl.CostEstimate(flops=0, bytes_accessed=12 * MIB, transcendentals=0),
        name="adam",
    )(ids, small, norm_part, *gradients[:2], *gradients, *flat)


def eight_parts(own, *meanwhile):
    lines = [lax.ppermute(own, YY, xor_pairs(4, k)) for k in (1, 2, 3)]
    if meanwhile:
        lines = [after(line, *meanwhile) for line in lines]
    lines = [own] + lines
    parts = []
    for line in lines:
        parts += [line, lax.ppermute(line, C, SWAP)]
    return parts


def core_scatter(keep, send, kernel=core_sum_kernel):
    share, width = keep.shape[0] // 4, keep.shape[1]
    got = lax.ppermute(send, C, SWAP)
    return local_call(
        kernel,
        "core_sum",
        [shape((share, width))] + [shape((share, width), BF16)] * 3,
        [keep, got],
        moved=5 * MIB,
    )


def line_scatter(own, *sent):
    return [own] + [lax.ppermute(s, YY, xor_pairs(4, k)) for k, s in zip((1, 2, 3), sent)]


def finish_scatter(keep, send, work=None, kernel=core_sum_kernel):
    own, *sent = core_scatter(keep, send, kernel)
    lines = line_scatter(own, *sent)
    if work is None:
        return lines
    done = work(own)
    return lines[:1] + [after(line, *done) for line in lines[1:]], done


def crossing(lines, first_axis, second_axis):
    first, second = list(lines[:4]), list(lines[4:])
    for k in (2, 1, 3):
        first[k] = lax.ppermute(first[k], first_axis, xor_pairs(4, k))
        second[k] = lax.ppermute(second[k], second_axis, xor_pairs(4, k))
    return first, second


def each_to_all(copies, axis):
    return lax.all_to_all(copies, axis, split_axis=0, concat_axis=0, tiled=True)


def after(value, *others):
    return lax.optimization_barrier((value, *others))[0]


def shards(
    hidden_in, cotangent, doc_lengths,
    inward, inward_moment, inward_squares,
    outward, outward_moment, outward_squares,
    upward, upward_moment, upward_squares,
    downward, downward_moment, downward_squares,
    prenorm, prenorm_moment, prenorm_squares,
    subnorm, subnorm_moment, subnorm_squares,
):
    rows, seq_slots, width = hidden_in.shape
    quarter = cotangent.shape[1]
    group_slots = 2 * seq_slots
    row_slots = group_slots * lax.axis_size(ZX)
    half = inward.shape[2] // 2
    heads = half // HDIM
    units = 4 * half
    tokens = rows * group_slots
    share = rows * quarter
    zx = lax.axis_index(ZX)
    row_index = lax.axis_index(Z)
    yh = lax.axis_index(YH)
    core = lax.axis_index(C)
    ffn = lax.axis_index(FFN)
    me = lax.axis_index(EIGHT)
    low_side = yh == 0
    first_core = core == 0
    ids = jnp.stack([me, yh, core, zx]).astype(jnp.int32)

    def mine_theirs(array, axis):
        low = array.astype(BF16)
        mine = lax.dynamic_slice_in_dim(low, yh * half, half, axis)
        theirs = lax.dynamic_slice_in_dim(low, (1 - yh) * half, half, axis)
        return mine, theirs

    def in_order(own, other):
        return jnp.concatenate(
            [jnp.where(low_side, own, other), jnp.where(low_side, other, own)], axis=0
        )

    def both_halves(pairs):
        other = lax.ppermute(jnp.concatenate([t for _, t in pairs], axis=1), YH, SWAP)
        own = jnp.concatenate([m for m, _ in pairs], axis=1)
        return in_order(own, other)

    def rows_of(pair, order):
        return tuple(jnp.transpose(t, order).reshape(seq_slots, -1) for t in pair)

    in_pair = rows_of(mine_theirs(inward, 2), (0, 1, 2))
    out_pair = rows_of(mine_theirs(outward, 0), (1, 0))
    up_pair = rows_of(mine_theirs(upward, 2), (0, 1, 2))
    down_pair = rows_of(mine_theirs(downward, 1), (2, 0, 1))
    w_att = both_halves([in_pair, out_pair])
    w_att = lax.all_gather(w_att, ZX, axis=0, tiled=True)
    w_out = w_att[:, 3 * half :]
    w_mlp = both_halves([up_pair, down_pair])
    w_mlp = lax.all_gather(w_mlp, ZX, axis=0, tiled=True)
    w_up, w_down = w_mlp[:, :units], w_mlp[:, units:]

    doc_ends = jnp.cumsum(doc_lengths, axis=1)
    places = jnp.arange(row_slots, dtype=jnp.int32)
    my_ends = lax.dynamic_slice_in_dim(doc_ends, row_index, 1, 0)
    start = jnp.max(
        jnp.where(places[None, :] >= my_ends.reshape(-1, 1), my_ends.reshape(-1, 1), 0),
        axis=0,
        keepdims=True,
    )
    own_places = zx * group_slots + me * quarter + jnp.arange(quarter, dtype=jnp.int32)
    own_usable = (own_places[None, :] < doc_ends[:, -1:]).astype(F32).reshape(share, 1)

    half_slots = seq_slots // 2
    sent = lax.dynamic_slice_in_dim(hidden_in, core * half_slots, half_slots, 1)
    got_near = lax.ppermute(sent, YY, [(i, 3 - i) for i in range(4)])
    got_far = lax.ppermute(got_near, C, SWAP)
    own_hidden = lax.dynamic_slice_in_dim(hidden_in, ffn * quarter, quarter, 1)
    own_hidden = own_hidden.reshape(share, width)
    own_cot = cotangent.reshape(share, width)
    df_own = (own_usable * own_cot.astype(F32)).astype(BF16)
    df_parts = eight_parts(after(df_own, got_near))

    tables = jnp.asarray(rotation_tables(row_slots))
    near = lax.dynamic_slice_in_dim(tables, zx * group_slots, group_slots, 2)
    qkv, x_hat = local_call(
        project_kernel,
        "project",
        [
            shape((rows * heads, 3, HDIM, group_slots), BF16),
            shape((tokens, width), BF16),
        ],
        [ids, hidden_in, got_near, got_far, after(prenorm, *df_parts), near, w_att],
        [
            pltpu.VMEM((tokens, width), BF16),
            pltpu.VMEM((group_slots, width), BF16),
            pltpu.VMEM((tokens, half), F32),
        ],
        flops=2 * tokens * width * 3 * half,
        moved=8 * MIB,
        far=(0, 1),
    )
    sub = lax.dynamic_slice_in_dim(subnorm, yh * half, half, 2)
    gain_o, shift_o = sub[0, 0].reshape(half, 1), sub[1, 0].reshape(half, 1)
    gain_h, shift_h = sub[0, 1:].reshape(1, units), sub[1, 1:].reshape(1, units)
    (gains,) = local_call(
        gain_product_kernel,
        "gain_product",
        [shape((8, width))],
        [sub[0, 0].reshape(1, half), sub[1, 0].reshape(1, half), after(w_out, x_hat)],
    )
    gains = gains + lax.ppermute(gains, C, SWAP)
    gains = [gains] + [lax.ppermute(gains, YY, xor_pairs(4, k)) for k in (2, 1, 3)]
    qkv = after(each_to_all(qkv, ZX), *gains)
    o_head, o_low, top = attend(qkv, start)
    o = each_to_all(o_low, ZX)
    (x_turned,) = local_call(
        turn_kernel, "turn", [shape((width, tokens), BF16)], [ids, x_hat], moved=4 * MIB, far=(0,)
    )

    stat = shape((8, 8, tokens))
    pieces = [shape((tokens // 2, width)), shape((tokens // 2, width), BF16)]
    wide = [shape((tokens // 2, width + 128)), shape((tokens // 2, width + 128), BF16)]
    keep, send, sums_o = local_call(
        out_kernel,
        "out",
        wide + [shape((2, tokens))],
        [ids, o, gain_o, w_out],
        [
            pltpu.VMEM((tokens, half), BF16),
            pltpu.VMEM((tokens, 128), F32),
            pltpu.VMEM((tokens, half), BF16),
            pltpu.VMEM((tokens, 128), F32),
        ],
        flops=2 * tokens * width * half,
        moved=4 * MIB,
    )
    scattered = finish_scatter(keep, send, kernel=core_sum_stats_kernel)
    r1, bb_own = local_call(
        middle_kernel,
        "middle",
        [shape((share, width)), shape((share, width), BF16)],
        scattered + [own_hidden, own_usable, prenorm] + gains,
        moved=3 * MIB,
        far=(0,),
    )

    df, dhn = local_call(
        down_back_kernel,
        "down_back",
        [shape((tokens, width), BF16), shape((tokens, units))],
        [ids] + df_parts + [after(w_down, bb_own)],
        flops=2 * tokens * width * units,
        moved=10 * MIB,
        stay=range(1, 9),
        far=(0,),
    )
    bb_parts = eight_parts(bb_own, dhn)
    bb, h, slope, sums_h = local_call(
        up_kernel,
        "up",
        [shape((tokens, width), BF16), shape((tokens, units)), shape((tokens, units)), stat],
        [ids] + bb_parts + [w_up, dhn, gain_h, sums_o],
        flops=2 * tokens * width * units,
        moved=14 * MIB,
        stay=range(1, 9),
        far=(0,),
    )
    sums_h = each_to_all(sums_h, EIGHT)
    keep, send, hn, du, sub_h = local_call(
        inner_back_kernel,
        "inner_back",
        pieces + [shape((tokens, units), BF16)] * 2 + [shape((2, units))],
        [ids, h, slope, dhn, sums_h, gain_h, shift_h, w_up],
        [pltpu.VMEM((tokens, units), BF16)],
        flops=2 * tokens * width * units,
        moved=14 * MIB,
        far=(2, 3),
    )
    scattered, (g_mlp,) = finish_scatter(
        keep, send, lambda own: [mlp_grad(df, hn, bb, after(du, own))]
    )
    g_mlp = lax.psum_scatter(after(g_mlp, *scattered), ZX, scatter_dimension=0, tiled=True)
    dr1, dattn_own, pre_three = local_call(
        middle_back_kernel,
        "middle_back",
        [shape((share, width)), shape((share, width), BF16), shape((2, width))],
        scattered + [r1, own_cot, own_usable, prenorm],
        moved=4 * MIB,
        far=(0,),
    )
    keep, send = local_call(
        down_kernel,
        "down",
        pieces,
        [ids, hn, w_down],
        [pltpu.VMEM((tokens, units), BF16)],
        flops=2 * tokens * width * units,
        moved=8 * MIB,
    )
    dattn_parts = eight_parts(dattn_own, keep)

    (c,) = local_call(
        lambda *refs: normed_heads_kernel(*refs, width=width),
        "normed_heads",
        [shape((tokens, half), BF16)],
        [o, sums_h, gain_o, shift_o],
        far=(0,),
    )
    dattn, dc, back_o, sub_o = local_call(
        out_back_kernel,
        "out_back",
        [shape((tokens, width), BF16), shape((half, tokens)), stat, shape((2, half))],
        [ids] + dattn_parts + [w_out, o, sums_h, gain_o],
        [pltpu.VMEM((tokens, half), F32)],
        flops=2 * tokens * width * half,
        moved=6 * MIB,
        stay=range(1, 9),
        far=(0,),
    )
    g_out = out_grad(dattn, c)
    back_o = after(each_to_all(back_o, EIGHT), g_out)
    (do,) = local_call(
        lambda *refs: head_grad_kernel(*refs, width=width),
        "head_grad",
        [shape((rows * heads, HDIM, group_slots), BF16)],
        [dc, o, sums_h, back_o, gain_o],
        moved=MIB,
    )
    f_parts = core_scatter(keep, after(send, *dattn_parts))
    do = after(each_to_all(do, ZX), x_turned, f_parts[0])
    scattered = line_scatter(*f_parts)
    dqkv = attend_back(qkv, do, o_head, top, start, tables)
    dqkv = each_to_all(after(dqkv, *scattered), ZX)

    both = 4 * half
    line = [shape((4 * seq_slots + 16, both), BF16)] * 4 + [shape((4 * seq_slots, both), BF16)] * 4
    *lines, dproj = local_call(
        in_grad_kernel,
        "in_grad",
        line + [shape((tokens, 3 * half), BF16)],
        [ids, dqkv, x_turned, w_att, prenorm, g_out, pre_three, sub_o, sub_h],
        [pltpu.VMEM((3 * half, tokens), BF16), pltpu.VMEM((2, width), F32)],
        flops=2 * tokens * width * 3 * half,
        moved=13 * MIB,
        far=range(8),
    )
    first, second = crossing(lines, X, Z)
    mlp_keep, mlp_give, squares_mlp = local_call(
        rest_kernel,
        "rest",
        [shape((seq_slots, 2 * units), BF16)] * 2 + [shape((8, 128))],
        [ids, after(g_mlp, dproj)],
        stay=(1,),
        far=(0,),
    )
    mlp_take = lax.ppermute(mlp_give, YH, SWAP)
    keep, send = local_call(
        in_back_kernel,
        "in_back",
        pieces,
        [ids, dproj, w_att],
        [pltpu.VMEM((tokens, 3 * half), BF16)],
        flops=2 * tokens * width * 3 * half,
        moved=7 * MIB,
    )
    da_parts = finish_scatter(keep, after(send, *first[1:], *second[1:], squares_mlp))
    piece = [shape((seq_slots + 16, both))] + [shape((seq_slots + 16, both), BF16)] * 3
    piece += [shape((seq_slots, both))] + [shape((seq_slots, both), BF16)] * 3
    lines = [*local_call(
        line_sum_kernel,
        "line_sum",
        piece,
        first + second,
        moved=6 * MIB,
    )]
    first, second = crossing(lines, Z, X)
    da_parts = da_parts[:1] + [after(part, *first[1:], *second[1:]) for part in da_parts[1:]]
    (own_grad,) = local_call(
        input_back_kernel,
        "input_back",
        [shape((share, width), BF16)],
        da_parts[:1] + [after(part, mlp_take) for part in da_parts[1:]] + [own_hidden, dr1, prenorm],
        moved=3 * MIB,
    )
    own_grad = own_grad.reshape(rows, quarter, width)
    line_grad = lax.ppermute(own_grad, YL, SWAP)
    grads = [own_grad, lax.ppermute(own_grad, C, SWAP), line_grad, lax.ppermute(line_grad, C, SWAP)]
    first_line = lax.axis_index(YL) == 0
    pairs = [
        jnp.concatenate([jnp.where(first_core, a, b), jnp.where(first_core, b, a)], axis=1)
        for a, b in (grads[:2], grads[2:])
    ]
    input_grad = jnp.concatenate(
        [jnp.where(first_line, *pairs), jnp.where(first_line, *pairs[::-1])], axis=1
    )

    grad_piece = shape((seq_slots + 16, 4 * half), BF16)
    att_keep, att_give, small = local_call(
        last_sum_kernel,
        "last_sum",
        [grad_piece, grad_piece, shape((8, 8, width), BF16)],
        [ids, *first, *second, squares_mlp],
        moved=MIB,
        far=(0,),
    )
    att_take = lax.ppermute(att_give, YH, SWAP)
    mlp_take = lax.ppermute(mlp_give, YH, SWAP)
    small = each_to_all(small, EIGHT)
    small_total, squares = local_call(
        group_total_kernel,
        "group_total",
        [shape((8, width)), shape((16, 8, 128))],
        [small],
        far=(0,),
    )
    squares = each_to_all(squares, ZX)
    hidden_out = local_call(
        result_kernel,
        "result",
        [shape((share, width), BF16)],
        scattered + [after(r1, small_total), own_usable],
        moved=3 * MIB,
        stay=range(5),
    )[0].reshape(rows, quarter, width)
    turns = ((1, 0, 2), (1, 0), (0, 1, 2), (0, 2, 1), (0, 1), (1, 0, 2))
    states = [
        (inward, inward_moment, inward_squares),
        (outward, outward_moment, outward_squares),
        (upward, upward_moment, upward_squares),
        (downward, downward_moment, downward_squares),
        (prenorm, prenorm_moment, prenorm_squares),
        (subnorm, subnorm_moment, subnorm_squares),
    ]
    *updated, norm = adam(
        ids,
        small_total,
        squares,
        [att_keep, att_take, mlp_keep, mlp_take],
        [tuple(jnp.transpose(a, turn) for a in state) for state, turn in zip(states, turns)],
    )
    updated = [jnp.transpose(a, turns[n // 3]) for n, a in enumerate(updated)]
    return (hidden_out, input_grad, *updated, norm[0, 0])


def solution(mesh):
    finer = Mesh(mesh.devices.reshape(4, 4, 2, 2, 2), SEQ_FFN)
    matrices = (P(SEQ, None, FFN),) * 3 + (P(FFN, SEQ),) * 3
    matrices += (P(SEQ, None, FFN),) * 3 + (P(None, FFN, SEQ),) * 3
    norms = (P(),) * 3 + (P(None, None, FFN),) * 3
    return jax.shard_map(
        shards,
        mesh=finer,
        in_specs=(P(None, SEQ, None), P(None, SEQ_FFN, None), P(), *matrices, *norms),
        out_specs=(P(None, SEQ_FFN, None), P(None, SEQ, None), *matrices, *norms, P()),
        check_vma=False,
    )
```

profile of v0, /device:TPU:1, one launch (start us, length us, event | category | flops | bytes accessed | tf_op | source)
XLA Modules:
  0.0 421.4 jit_solution(483674043624433868)
XLA Ops:
  9.4 3.8 collective-permute-start.9
  13.2 2.9 collective-permute-done.9
  17.4 3.0 collective-permute-start.20
  20.5 4.8 %collective-permute-done.20 = bf16[64,2048]{1,0:T(8,128)(2,1)S(1)} collective-permute-done((bf16[64,2048]{1,0:T(8,128)(2,1)S(1)}, bf16[64,2048]{1,0:T(8,128)(2,1)S(1)}, u32[]{:S(2)}, u32[]{:S(2)}) %collective-permute-start.20) | collective-permute-done | bytes 262176 | tf_op jit(solution)/shard_map/ppermute | solution.py:1010
  26.2 2.8 collective-permute-start
  29.7 8.9 %collective-permute-done.near_ref = bf16[4,32,2048]{2,1,0:T(8,128)(2,1)S(1)} collective-permute-done((bf16[4,32,2048]{2,1,0:T(8,128)(2,1)S(1)}, bf16[4,32,2048]{2,1,0:T(8,128)(2,1)S(1)}, u32[]{:S(2)}, u32[]{:S(2)}) %collective-permute-start) | collective-permute-done | bytes 524320 | tf_op jit(solution)/shard_map/ppermute | solution.py:1041
  38.7 3.7 collective-permute-start.5
  42.5 4.2 collective-permute-start.1
  46.6 3.5 collective-permute-start.4
  50.7 4.7 %collective-permute-start.6 = (bf16[64,2048]{1,0:T(8,128)(2,1)S(1)}, bf16[64,2048]{1,0:T(8,128)(2,1)}, u32[]{:S(2)}, u32[]{:S(2)}) collective-permute-start(bf16[64,2048]{1,0:T(8,128)(2,1)S(1)} %collective-permute-done.5.refs_4_), channel_id=1, source_target_pairs={{0,1},{1,0},{2,3},{3,2},{4,5},{5,4},{6,7},{7,6},{8,9},{9,8},{10,11... | collective-permute-start | bytes 786440 | tf_op jit(solution)/shard_map/ppermute | solution.py:925
  59.2 12.8 %all-gather.3.cloned.1.call-done.w_ref = bf16[2048,1024]{1,0:T(8,128)(2,1)} async-done(((bf16[128,1024]{1,0:T(8,128)(2,1)}), bf16[2048,1024]{1,0:T(8,128)(2,1)}) %all-gather.3.cloned.1.call-update) | async-done | bytes 4194320 | tf_op jit(solution)/shard_map/all_gather | solution.py:1022
  74.2 4.6 %project.1 = (bf16[16,3,64,128]{3,2,1,0:T(8,128)(2,1)}, bf16[512,2048]{1,0:T(8,128)(2,1)}) custom-call(s32[4]{0:T(128)S(1)} %pad_add_fusion.ids, bf16[4,64,2048]{2,1,0:T(8,128)(2,1)S(1)} %copy-done.6, bf16[4,32,2048]{2,1,0:T(8,128)(2,1)S(1)} %collective-permute-done.near_ref, bf16[4,32,2048]{2,1,0:T(8,128)(2,1)S(1)} %collective-permute-done.1.far_ref, ...), custom_call_target="tpu_custom_call" | custom-call | flops 1610612736 | bytes 8388608 | tf_op jit(solution)/shard_map/project/pallas_call | solution.py:68
  78.8 5.0 %all-to-all-start = ((bf16[16,3,64,128]{3,2,1,0:T(8,128)(2,1)}), bf16[16,3,64,128]{3,2,1,0:T(8,128)(2,1)S(1)}, u32[]{:S(2)}, u32[]{:S(2)}) async-start(bf16[16,3,64,128]{3,2,1,0:T(8,128)(2,1)} %get-tuple-element.144), calls=%async_computation | async-start | bytes 1572864 | tf_op jit(solution)/shard_map/all_to_all | solution.py:963
  87.6 2.8 collective-permute-start.11
  95.9 6.5 %all-to-all-done.qkv_ref = bf16[16,3,64,128]{3,2,1,0:T(8,128)(2,1)S(1)} async-done(((bf16[16,3,64,128]{3,2,1,0:T(8,128)(2,1)}), bf16[16,3,64,128]{3,2,1,0:T(8,128)(2,1)S(1)}, u32[]{:S(2)}, u32[]{:S(2)}) %all-to-all-start) | async-done | bytes 786464 | tf_op jit(solution)/shard_map/all_to_all | solution.py:963
  102.4 5.8 %attend.1 = (f32[16,64,128]{2,1,0:T(8,128)}, bf16[16,64,128]{2,1,0:T(8,128)(2,1)}, f32[1,2048]{1,0:T(1,128)S(1)}) custom-call(bf16[16,3,64,128]{3,2,1,0:T(8,128)(2,1)S(1)} %all-to-all-done.qkv_ref, s32[1,2048]{1,0:T(1,128)S(1)} %bitcast.78), custom_call_target="tpu_custom_call" | custom-call | flops 2000000000 | bytes 4000000 | tf_op jit(solution)/shard_map/attend/pallas_call | solution.py:200
  108.1 3.5 all-to-all-start.1
  111.9 7.3 %all-to-all-done.1.o_ref.refs_9_.refs_0_.refs_1_ = bf16[16,64,128]{2,1,0:T(8,128)(2,1)S(1)} async-done(((bf16[16,64,128]{2,1,0:T(8,128)(2,1)}), bf16[16,64,128]{2,1,0:T(8,128)(2,1)S(1)}, u32[]{:S(2)}, u32[]{:S(2)}) %all-to-all-start.1) | async-done | bytes 262176 | tf_op jit(solution)/shard_map/all_to_all | solution.py:963
  119.2 3.2 out.1
  122.4 7.6 %collective-permute-start.14 = (bf16[256,2176]{1,0:T(8,128)(2,1)S(1)}, bf16[256,2176]{1,0:T(8,128)(2,1)S(1)}, u32[]{:S(2)}, u32[]{:S(2)}) collective-permute-start(bf16[256,2176]{1,0:T(8,128)(2,1)S(1)} %get-tuple-element.150), channel_id=1, source_target_pairs={{0,1},{1,0},{2,3},{3,2},{4,5},{5,4},{6,7},{7,6},{8,9},{9,8},{10,11... | collective-permute-start | bytes 3342344 | tf_op jit(solution)/shard_map/ppermute | solution.py:931
  138.6 4.2 collective-permute-done.15.one
  142.8 8.2 %collective-permute-done.16.two = bf16[64,2176]{1,0:T(8,128)(2,1)} collective-permute-done((bf16[64,2176]{1,0:T(8,128)(2,1)}, bf16[64,2176]{1,0:T(8,128)(2,1)}, u32[]{:S(2)}, u32[]{:S(2)}) %collective-permute-start.16) | collective-permute-done | bytes 278560 | tf_op jit(solution)/shard_map/ppermute | solution.py:942
  156.7 3.0 collective-permute-start.19
  162.5 3.9 fusion.5
  166.4 6.8 %down_back.1 = (bf16[512,2048]{1,0:T(8,128)(2,1)}, f32[512,1024]{1,0:T(8,128)S(1)}) custom-call(s32[4]{0:T(128)S(1)} %pad_add_fusion.ids, bf16[64,2048]{1,0:T(8,128)(2,1)} %copy-done.52, bf16[64,2048]{1,0:T(8,128)(2,1)} %collective-permute-done.2.refs_1_, bf16[64,2048]{1,0:T(8,128)(2,1)} %copy-done.65, bf16[64,2048]{1,0:T(8,128)(2,1)} %collective-permute-done.4.refs_3_, ...), custom_call_target="tpu_custom_call" | custom-call | flops 2147483648 | bytes 10485760 | tf_op jit(solution)/shard_map/down_back/pallas_call | solution.py:68
  176.3 6.4 %up.1 = (bf16[512,2048]{1,0:T(8,128)(2,1)}, f32[512,1024]{1,0:T(8,128)S(1)}, f32[512,1024]{1,0:T(8,128)S(1)}, f32[8,8,512]{2,1,0:T(8,128)S(1)}) custom-call(s32[4]{0:T(128)S(1)} %pad_add_fusion.ids, bf16[64,2048]{1,0:T(8,128)(2,1)} %copy-done.28, bf16[64,2048]{1,0:T(8,128)(2,1)} %copy-done.48, bf16[64,2048]{1,0:T(8,128)(2,1)} %copy-done.47, ...), custom_call_target="tpu_custom_call" | custom-call | flops 2147483648 | bytes 14680064 | tf_op jit(solution)/shard_map/up/pallas_call | solution.py:68
  182.6 7.8 %all_to_all.40.sums_ref.refs_10_.refs_1_.refs_2_ = f32[8,8,512]{2,1,0:T(8,128)S(1)} all-to-all(f32[8,8,512]{2,1,0:T(8,128)S(1)} %get-tuple-element.164), channel_id=1, replica_groups=mesh['seq_0'=4,'seq_1'=4,'seq_2'=2,'ffn_0'=2,'ffn_1'=2] {'seq_2','ffn_0'..., dimensions={0} | all-to-all | bytes 262144 | tf_op jit(solution)/shard_map/all_to_all | solution.py:963
  190.4 7.5 %inner_back.1 = (f32[256,2048]{1,0:T(8,128)S(1)}, bf16[256,2048]{1,0:T(8,128)(2,1)S(1)}, bf16[512,1024]{1,0:T(8,128)(2,1)}, bf16[512,1024]{1,0:T(8,128)(2,1)}, f32[2,1024]{1,0:T(2,128)S(1)}) custom-call(s32[4]{0:T(128)S(1)} %pad_add_fusion.ids, f32[512,1024]{1,0:T(8,128)S(1)} %get-tuple-element.162.h_ref, f32[512,1024]{1,0:T(8,128)S(1)} %get-tuple-element.163.slope_ref, ...), custom_call_target="tpu_custom_call" | custom-call | flops 2147483648 | bytes 14680064 | tf_op jit(solution)/shard_map/inner_back/pallas_call | solution.py:68
  206.5 8.1 %mlp_grad.1 = bf16[2048,2048]{1,0:T(8,128)(2,1)} custom-call(bf16[512,2048]{1,0:T(8,128)(2,1)S(1)} %copy-done.38, bf16[512,1024]{1,0:T(8,128)(2,1)S(1)} %copy-done.33, bf16[512,2048]{1,0:T(8,128)(2,1)S(1)} %copy-done.32, bf16[512,1024]{1,0:T(8,128)(2,1)S(1)} %copy-done.36), custom_call_target="tpu_custom_call" | custom-call | flops 4294967296 | bytes 14680064 | tf_op jit(solution)/shard_map/mlp_grad/pallas_call | solution.py:552
  225.2 5.4 %down.1 = (f32[256,2048]{1,0:T(8,128)S(1)}, bf16[256,2048]{1,0:T(8,128)(2,1)}) custom-call(s32[4]{0:T(128)S(1)} %pad_add_fusion.ids, bf16[512,1024]{1,0:T(8,128)(2,1)S(1)} %copy-done.34, bf16[2048,1024]{1,0:T(8,128)(2,1)S(1)} %copy-done.4), custom_call_target="tpu_custom_call" | custom-call | flops 2147483648 | bytes 8388608 | tf_op jit(solution)/shard_map/down/pallas_call | solution.py:68
  237.9 4.1 out_back.1
  242.1 3.8 all-to-all-start.3
  253.4 3.5 all-to-all-start.4
  264.3 3.6 all-to-all-done.4.do_ref
  273.0 11.6 %attend_back.1 = bf16[16,3,64,128]{3,2,1,0:T(8,128)(2,1)} custom-call(bf16[16,3,64,128]{3,2,1,0:T(8,128)(2,1)S(1)} %copy-done.17, bf16[16,64,128]{2,1,0:T(8,128)(2,1)S(1)} %all-to-all-done.4.do_ref, f32[16,64,128]{2,1,0:T(8,128)S(1)} %copy-done.39, f32[1,2048]{1,0:T(1,128)S(1)} %get-tuple-element.197.top_ref, s32[1,2048]{1,0:T(1,128)S(1)} %bitcast.79, ...), custom_call_target="tpu_custom_call" | custom-call | flops 6000000000 | bytes 6000000 | tf_op jit(solution)/shard_map/attend_back/pallas_call | solution.py:226
  285.0 22.2 %all_to_all.41.dqkv_ref = bf16[16,3,64,128]{3,2,1,0:T(8,128)(2,1)S(1)} all-to-all(bf16[16,3,64,128]{3,2,1,0:T(8,128)(2,1)} %attend_back.1), channel_id=1, replica_groups=mesh['seq_0'=4,'seq_1'=4,'seq_2'=2,'ffn_0'=2,'ffn_1'=2] {'seq_0','seq_1'}, dimensions={0} | all-to-all | bytes 1572864 | tf_op jit(solution)/shard_map/all_to_all | solution.py:963
  307.2 6.4 %in_grad.1 = (bf16[272,1024]{1,0:T(8,128)(2,1)}, bf16[272,1024]{1,0:T(8,128)(2,1)}, bf16[272,1024]{1,0:T(8,128)(2,1)}, bf16[272,1024]{1,0:T(8,128)(2,1)}, bf16[2...) custom-call(s32[4]{0:T(128)S(1)} %pad_add_fusion.ids, ...), custom_call_target="tpu_custom_call" | custom-call | flops 1610612736 | bytes 13631488 | tf_op jit(solution)/shard_map/in_grad/pallas_call | solution.py:68
  319.5 6.6 %collective-permute-done.44.refs_5_ = bf16[256,1024]{1,0:T(8,128)(2,1)S(1)} collective-permute-done((bf16[256,1024]{1,0:T(8,128)(2,1)}, bf16[256,1024]{1,0:T(8,128)(2,1)S(1)}, u32[]{:S(2)}, u32[]{:S(2)}) %collective-permute-start.44) | collective-permute-done | bytes 524320 | tf_op jit(solution)/shard_map/ppermute | solution.py:958
  327.6 3.9 in_back.1
  334.4 3.3 collective-permute-done.45.refs_6_
  337.8 13.0 %collective-permute-done.46.refs_7_ = bf16[256,1024]{1,0:T(8,128)(2,1)} collective-permute-done((bf16[256,1024]{1,0:T(8,128)(2,1)}, bf16[256,1024]{1,0:T(8,128)(2,1)}, u32[]{:S(2)}, u32[]{:S(2)}) %collective-permute-start.46) | collective-permute-done | bytes 524320 | tf_op jit(solution)/shard_map/ppermute | solution.py:958
  359.7 2.8 collective-permute-start.48
  370.6 4.3 %collective-permute-done.49.refs_3_ = bf16[80,1024]{1,0:T(8,128)(2,1)S(1)} collective-permute-done((bf16[80,1024]{1,0:T(8,128)(2,1)S(1)}, bf16[80,1024]{1,0:T(8,128)(2,1)S(1)}, u32[]{:S(2)}, u32[]{:S(2)}) %collective-permute-start.49) | collective-permute-done | bytes 163872 | tf_op jit(solution)/shard_map/ppermute | solution.py:957
  376.5 6.1 %all-to-all-start.6 = ((bf16[8,8,2048]{2,1,0:T(8,128)(2,1)}), bf16[8,8,2048]{2,1,0:T(8,128)(2,1)S(1)}, u32[]{:S(2)}, u32[]{:S(2)}) async-start(bf16[8,8,2048]{2,1,0:T(8,128)(2,1)} %get-tuple-element.222), calls=%async_computation.7 | async-start | bytes 524288 | tf_op jit(solution)/shard_map/all_to_all | solution.py:963
  387.8 3.0 collective-permute-start.61
  391.5 4.2 %all-to-all-start.7 = ((f32[16,8,128]{2,1,0:T(8,128)}), f32[16,8,128]{2,1,0:T(8,128)S(1)}, u32[]{:S(2)}, u32[]{:S(2)}) async-start(f32[16,8,128]{2,1,0:T(8,128)} %get-tuple-element.240), calls=%async_computation.8 | async-start | bytes 131072 | tf_op jit(solution)/shard_map/all_to_all | solution.py:963
  398.2 4.1 all-to-all-done.7.norm_part
  402.9 6.4 %adam.1 = (f32[3,64,512]{2,1,0:T(8,128)}, f32[3,64,512]{2,1,0:T(8,128)}, f32[3,64,512]{2,1,0:T(8,128)}, f32[64,512]{1,0:T(8,128)}, f32[64,512]{1,0:T(8,128)}, /*...) custom-call(s32[4]{0:T(128)} %copy-done.30, ...), custom_call_target="tpu_custom_call" | custom-call | bytes 12582912 | tf_op jit(solution)/shard_map/adam/pallas_call | solution.py:899
  (312 shorter events, 131.0 us)
Async XLA Ops:
  7.2 64.8 %all-gather.3.cloned.1.call-start = ((), (), s32[]{:S(2)}) async-start(), calls=%async_computation.9 | async-start | bytes 4456448 | tf_op jit(solution)/shard_map/all_gather | solution.py:1022
  17.0 145.5 %all-gather.5.cloned.1.call-start = ((), (), s32[]{:S(2)}) async-start(), calls=%async_computation.10 | async-start | bytes 8912896 | tf_op jit(solution)/shard_map/all_gather | solution.py:1025
  26.2 12.3 %collective-permute-start = (bf16[4,32,2048]{2,1,0:T(8,128)(2,1)S(1)}, bf16[4,32,2048]{2,1,0:T(8,128)(2,1)S(1)}, u32[]{:S(2)}, u32[]{:S(2)}) collective-permute-start(bf16[4,32,2048]{2,1,0:T(8,128)(2,1)S(1)} %constant_dynamic-slice_fusion.8), channel_id=1, source_target_pairs={{0,6},{2,4},{4,2},{6,0},{1,7},{3,5},{5,3},{7,1},{8,14},{10,12},{12... | collective-permute-start | bytes 1572872 | tf_op jit(solution)/shard_map/ppermute | solution.py:1041
  38.7 12.1 %collective-permute-start.5 = (bf16[64,2048]{1,0:T(8,128)(2,1)S(1)}, bf16[64,2048]{1,0:T(8,128)(2,1)S(1)}, u32[]{:S(2)}, u32[]{:S(2)}) collective-permute-start(bf16[64,2048]{1,0:T(8,128)(2,1)S(1)} %multiply_convert_fusion.refs_0_), channel_id=1, source_target_pairs={{0,4},{2,6},{4,0},{6,2},{1,5},{3,7},{5,1},{7,3},{8,12},{10,14},{12... | collective-permute-start | bytes 786440 | tf_op jit(solution)/shard_map/ppermute | solution.py:919
  42.4 13.4 %collective-permute-start.7 = (bf16[64,2048]{1,0:T(8,128)(2,1)S(1)}, bf16[64,2048]{1,0:T(8,128)(2,1)S(1)}, u32[]{:S(2)}, u32[]{:S(2)}) collective-permute-start(bf16[64,2048]{1,0:T(8,128)(2,1)S(1)} %multiply_convert_fusion.refs_0_), channel_id=1, source_target_pairs={{0,6},{2,4},{4,2},{6,0},{1,7},{3,5},{5,3},{7,1},{8,14},{10,12},{12... | collective-permute-start | bytes 786440 | tf_op jit(solution)/shard_map/ppermute | solution.py:919
  42.5 16.8 %collective-permute-start.1 = (bf16[4,32,2048]{2,1,0:T(8,128)(2,1)S(1)}, bf16[4,32,2048]{2,1,0:T(8,128)(2,1)S(1)}, u32[]{:S(2)}, u32[]{:S(2)}) collective-permute-start(bf16[4,32,2048]{2,1,0:T(8,128)(2,1)S(1)} %collective-permute-done.near_ref), channel_id=1, source_target_pairs={{0,1},{1,0},{2,3},{3,2},{4,5},{5,4},{6,7},{7,6},{8,9},{9,8},{10,11... | collective-permute-start | bytes 1572872 | tf_op jit(solution)/shard_map/ppermute | solution.py:1042
  46.6 12.3 %collective-permute-start.2 = (bf16[64,2048]{1,0:T(8,128)(2,1)S(1)}, bf16[64,2048]{1,0:T(8,128)(2,1)}, u32[]{:S(2)}, u32[]{:S(2)}) collective-permute-start(bf16[64,2048]{1,0:T(8,128)(2,1)S(1)} %multiply_convert_fusion.refs_0_), channel_id=1, source_target_pairs={{0,1},{1,0},{2,3},{3,2},{4,5},{5,4},{6,7},{7,6},{8,9},{9,8},{10,11... | collective-permute-start | bytes 786440 | tf_op jit(solution)/shard_map/ppermute | solution.py:925
  46.6 12.3 %collective-permute-start.4 = (bf16[64,2048]{1,0:T(8,128)(2,1)S(1)}, bf16[64,2048]{1,0:T(8,128)(2,1)}, u32[]{:S(2)}, u32[]{:S(2)}) collective-permute-start(bf16[64,2048]{1,0:T(8,128)(2,1)S(1)} %collective-permute-done.3.refs_2_), channel_id=1, source_target_pairs={{0,1},{1,0},{2,3},{3,2},{4,5},{5,4},{6,7},{7,6},{8,9},{9,8},{10,11... | collective-permute-start | bytes 786440 | tf_op jit(solution)/shard_map/ppermute | solution.py:925
  78.8 23.5 %all-to-all-start = ((bf16[16,3,64,128]{3,2,1,0:T(8,128)(2,1)}), bf16[16,3,64,128]{3,2,1,0:T(8,128)(2,1)S(1)}, u32[]{:S(2)}, u32[]{:S(2)}) async-start(bf16[16,3,64,128]{3,2,1,0:T(8,128)(2,1)} %get-tuple-element.144), calls=%async_computation | async-start | bytes 1572864 | tf_op jit(solution)/shard_map/all_to_all | solution.py:963
  108.1 11.1 %all-to-all-start.1 = ((bf16[16,64,128]{2,1,0:T(8,128)(2,1)}), bf16[16,64,128]{2,1,0:T(8,128)(2,1)S(1)}, u32[]{:S(2)}, u32[]{:S(2)}) async-start(bf16[16,64,128]{2,1,0:T(8,128)(2,1)} %get-tuple-element.148), calls=%async_computation.1 | async-start | bytes 524288 | tf_op jit(solution)/shard_map/all_to_all | solution.py:963
  111.7 220.7 %reduce-scatter.2.cloned.1.call-start = ((), (), s32[]{:S(2)}) async-start(), calls=%async_computation.11 | async-start | bytes 8912896 | tf_op jit(solution)/shard_map/reduce_scatter | solution.py:1148
  122.4 10.0 %collective-permute-start.14 = (bf16[256,2176]{1,0:T(8,128)(2,1)S(1)}, bf16[256,2176]{1,0:T(8,128)(2,1)S(1)}, u32[]{:S(2)}, u32[]{:S(2)}) collective-permute-start(bf16[256,2176]{1,0:T(8,128)(2,1)S(1)} %get-tuple-element.150), channel_id=1, source_target_pairs={{0,1},{1,0},{2,3},{3,2},{4,5},{5,4},{6,7},{7,6},{8,9},{9,8},{10,11... | collective-permute-start | bytes 3342344 | tf_op jit(solution)/shard_map/ppermute | solution.py:931
  135.8 15.2 %collective-permute-start.16 = (bf16[64,2176]{1,0:T(8,128)(2,1)}, bf16[64,2176]{1,0:T(8,128)(2,1)}, u32[]{:S(2)}, u32[]{:S(2)}) collective-permute-start(bf16[64,2176]{1,0:T(8,128)(2,1)} %get-tuple-element.153), channel_id=1, source_target_pairs={{0,4},{2,6},{4,0},{6,2},{1,5},{3,7},{5,1},{7,3},{8,12},{10,14},{12... | collective-permute-start | bytes 835592 | tf_op jit(solution)/shard_map/ppermute | solution.py:942
  138.2 14.7 %collective-permute-start.17 = (bf16[64,2176]{1,0:T(8,128)(2,1)}, bf16[64,2176]{1,0:T(8,128)(2,1)}, u32[]{:S(2)}, u32[]{:S(2)}) collective-permute-start(bf16[64,2176]{1,0:T(8,128)(2,1)} %get-tuple-element.154), channel_id=1, source_target_pairs={{0,6},{2,4},{4,2},{6,0},{1,7},{3,5},{5,3},{7,1},{8,14},{10,12},{12... | collective-permute-start | bytes 835592 | tf_op jit(solution)/shard_map/ppermute | solution.py:942
  156.5 16.7 %collective-permute-start.24 = (bf16[64,2048]{1,0:T(8,128)(2,1)S(1)}, bf16[64,2048]{1,0:T(8,128)(2,1)S(1)}, u32[]{:S(2)}, u32[]{:S(2)}) collective-permute-start(bf16[64,2048]{1,0:T(8,128)(2,1)S(1)} %get-tuple-element.155.refs_0_), channel_id=1, source_target_pairs={{0,6},{2,4},{4,2},{6,0},{1,7},{3,5},{5,3},{7,1},{8,14},{10,12},{12... | collective-permute-start | bytes 786440 | tf_op jit(solution)/shard_map/ppermute | solution.py:919
  156.7 16.6 %collective-permute-start.22 = (bf16[64,2048]{1,0:T(8,128)(2,1)S(1)}, bf16[64,2048]{1,0:T(8,128)(2,1)S(1)}, u32[]{:S(2)}, u32[]{:S(2)}) collective-permute-start(bf16[64,2048]{1,0:T(8,128)(2,1)S(1)} %get-tuple-element.155.refs_0_), channel_id=1, source_target_pairs={{0,4},{2,6},{4,0},{6,2},{1,5},{3,7},{5,1},{7,3},{8,12},{10,14},{12... | collective-permute-start | bytes 786440 | tf_op jit(solution)/shard_map/ppermute | solution.py:919
  156.7 17.1 %collective-permute-start.19 = (bf16[64,2048]{1,0:T(8,128)(2,1)S(1)}, bf16[64,2048]{1,0:T(8,128)(2,1)S(1)}, u32[]{:S(2)}, u32[]{:S(2)}) collective-permute-start(bf16[64,2048]{1,0:T(8,128)(2,1)S(1)} %get-tuple-element.155.refs_0_), channel_id=1, source_target_pairs={{0,2},{2,0},{4,6},{6,4},{1,3},{3,1},{5,7},{7,5},{8,10},{10,8},{12,... | collective-permute-start | bytes 786440 | tf_op jit(solution)/shard_map/ppermute | solution.py:919
  159.8 14.4 %collective-permute-start.18 = (bf16[64,2048]{1,0:T(8,128)(2,1)S(1)}, bf16[64,2048]{1,0:T(8,128)(2,1)S(1)}, u32[]{:S(2)}, u32[]{:S(2)}) collective-permute-start(bf16[64,2048]{1,0:T(8,128)(2,1)S(1)} %get-tuple-element.155.refs_0_), channel_id=1, source_target_pairs={{0,1},{1,0},{2,3},{3,2},{4,5},{5,4},{6,7},{7,6},{8,9},{9,8},{10,11... | collective-permute-start | bytes 786440 | tf_op jit(solution)/shard_map/ppermute | solution.py:925
  202.0 14.7 %collective-permute-start.29 = (bf16[64,2048]{1,0:T(8,128)(2,1)}, bf16[64,2048]{1,0:T(8,128)(2,1)}, u32[]{:S(2)}, u32[]{:S(2)}) collective-permute-start(bf16[64,2048]{1,0:T(8,128)(2,1)} %get-tuple-element.179), channel_id=1, source_target_pairs={{0,6},{2,4},{4,2},{6,0},{1,7},{3,5},{5,3},{7,1},{8,14},{10,12},{12... | collective-permute-start | bytes 786440 | tf_op jit(solution)/shard_map/ppermute | solution.py:942
  202.9 13.8 %collective-permute-start.28 = (bf16[64,2048]{1,0:T(8,128)(2,1)}, bf16[64,2048]{1,0:T(8,128)(2,1)}, u32[]{:S(2)}, u32[]{:S(2)}) collective-permute-start(bf16[64,2048]{1,0:T(8,128)(2,1)} %get-tuple-element.177), channel_id=1, source_target_pairs={{0,4},{2,6},{4,0},{6,2},{1,5},{3,7},{5,1},{7,3},{8,12},{10,14},{12... | collective-permute-start | bytes 786440 | tf_op jit(solution)/shard_map/ppermute | solution.py:942
  204.1 12.9 %collective-permute-start.27 = (bf16[64,2048]{1,0:T(8,128)(2,1)}, bf16[64,2048]{1,0:T(8,128)(2,1)}, u32[]{:S(2)}, u32[]{:S(2)}) collective-permute-start(bf16[64,2048]{1,0:T(8,128)(2,1)} %get-tuple-element.171), channel_id=1, source_target_pairs={{0,2},{2,0},{4,6},{6,4},{1,3},{3,1},{5,7},{7,5},{8,10},{10,8},{12,... | collective-permute-start | bytes 786440 | tf_op jit(solution)/shard_map/ppermute | solution.py:942
  219.8 13.9 %collective-permute-start.35 = (bf16[64,2048]{1,0:T(8,128)(2,1)S(1)}, bf16[64,2048]{1,0:T(8,128)(2,1)S(1)}, u32[]{:S(2)}, u32[]{:S(2)}) collective-permute-start(bf16[64,2048]{1,0:T(8,128)(2,1)S(1)} %get-tuple-element.182.refs_0_), channel_id=1, source_target_pairs={{0,6},{2,4},{4,2},{6,0},{1,7},{3,5},{5,3},{7,1},{8,14},{10,12},{12... | collective-permute-start | bytes 786440 | tf_op jit(solution)/shard_map/ppermute | solution.py:919
  220.7 14.6 %collective-permute-start.33 = (bf16[64,2048]{1,0:T(8,128)(2,1)S(1)}, bf16[64,2048]{1,0:T(8,128)(2,1)S(1)}, u32[]{:S(2)}, u32[]{:S(2)}) collective-permute-start(bf16[64,2048]{1,0:T(8,128)(2,1)S(1)} %get-tuple-element.182.refs_0_), channel_id=1, source_target_pairs={{0,4},{2,6},{4,0},{6,2},{1,5},{3,7},{5,1},{7,3},{8,12},{10,14},{12... | collective-permute-start | bytes 786440 | tf_op jit(solution)/shard_map/ppermute | solution.py:919
  221.8 13.6 %collective-permute-start.31 = (bf16[64,2048]{1,0:T(8,128)(2,1)S(1)}, bf16[64,2048]{1,0:T(8,128)(2,1)S(1)}, u32[]{:S(2)}, u32[]{:S(2)}) collective-permute-start(bf16[64,2048]{1,0:T(8,128)(2,1)S(1)} %get-tuple-element.182.refs_0_), channel_id=1, source_target_pairs={{0,2},{2,0},{4,6},{6,4},{1,3},{3,1},{5,7},{7,5},{8,10},{10,8},{12,... | collective-permute-start | bytes 786440 | tf_op jit(solution)/shard_map/ppermute | solution.py:919
  237.2 24.0 %collective-permute-start.37 = (bf16[256,2048]{1,0:T(8,128)(2,1)}, bf16[256,2048]{1,0:T(8,128)(2,1)}, u32[]{:S(2)}, u32[]{:S(2)}) collective-permute-start(bf16[256,2048]{1,0:T(8,128)(2,1)} %get-tuple-element.186), channel_id=1, source_target_pairs={{0,1},{1,0},{2,3},{3,2},{4,5},{5,4},{6,7},{7,6},{8,9},{9,8},{10,11... | collective-permute-start | bytes 3145736 | tf_op jit(solution)/shard_map/ppermute | solution.py:931
  242.1 10.4 %all-to-all-start.3 = ((f32[8,8,512]{2,1,0:T(8,128)}), f32[8,8,512]{2,1,0:T(8,128)S(1)}, u32[]{:S(2)}, u32[]{:S(2)}) async-start(f32[8,8,512]{2,1,0:T(8,128)} %get-tuple-element.192), calls=%async_computation.3 | async-start | bytes 262144 | tf_op jit(solution)/shard_map/all_to_all | solution.py:963
  253.4 14.5 %all-to-all-start.4 = ((bf16[16,64,128]{2,1,0:T(8,128)(2,1)}), bf16[16,64,128]{2,1,0:T(8,128)(2,1)S(1)}, u32[]{:S(2)}, u32[]{:S(2)}) async-start(bf16[16,64,128]{2,1,0:T(8,128)(2,1)} %head_grad.1), calls=%async_computation.4 | async-start | bytes 524288 | tf_op jit(solution)/shard_map/all_to_all | solution.py:963
  267.9 16.8 %collective-permute-start.38 = (bf16[64,2048]{1,0:T(8,128)(2,1)}, bf16[64,2048]{1,0:T(8,128)(2,1)S(1)}, u32[]{:S(2)}, u32[]{:S(2)}) collective-permute-start(bf16[64,2048]{1,0:T(8,128)(2,1)} %copy-done.37), channel_id=1, source_target_pairs={{0,2},{2,0},{4,6},{6,4},{1,3},{3,1},{5,7},{7,5},{8,10},{10,8},{12,... | collective-permute-start | bytes 786440 | tf_op jit(solution)/shard_map/ppermute | solution.py:942
  269.4 15.2 %collective-permute-start.39 = (bf16[64,2048]{1,0:T(8,128)(2,1)S(1)}, bf16[64,2048]{1,0:T(8,128)(2,1)S(1)}, u32[]{:S(2)}, u32[]{:S(2)}) collective-permute-start(bf16[64,2048]{1,0:T(8,128)(2,1)S(1)} %get-tuple-element.189), channel_id=1, source_target_pairs={{0,4},{2,6},{4,0},{6,2},{1,5},{3,7},{5,1},{7,3},{8,12},{10,14},{12... | collective-permute-start | bytes 786440 | tf_op jit(solution)/shard_map/ppermute | solution.py:942
  271.5 13.6 %collective-permute-start.40 = (bf16[64,2048]{1,0:T(8,128)(2,1)S(1)}, bf16[64,2048]{1,0:T(8,128)(2,1)S(1)}, u32[]{:S(2)}, u32[]{:S(2)}) collective-permute-start(bf16[64,2048]{1,0:T(8,128)(2,1)S(1)} %get-tuple-element.190), channel_id=1, source_target_pairs={{0,6},{2,4},{4,2},{6,0},{1,7},{3,5},{5,3},{7,1},{8,14},{10,12},{12... | collective-permute-start | bytes 786440 | tf_op jit(solution)/shard_map/ppermute | solution.py:942
  313.7 12.4 %collective-permute-start.44 = (bf16[256,1024]{1,0:T(8,128)(2,1)}, bf16[256,1024]{1,0:T(8,128)(2,1)S(1)}, u32[]{:S(2)}, u32[]{:S(2)}) collective-permute-start(bf16[256,1024]{1,0:T(8,128)(2,1)} %get-tuple-element.207), channel_id=1, source_target_pairs={{0,32},{32,0},{64,96},{96,64},{1,33},{33,1},{65,97},{97,65},{2,34}... | collective-permute-start | bytes 1572872 | tf_op jit(solution)/shard_map/ppermute | solution.py:958
  313.8 37.0 %collective-permute-start.41 = (bf16[272,1024]{1,0:T(8,128)(2,1)}, bf16[272,1024]{1,0:T(8,128)(2,1)}, u32[]{:S(2)}, u32[]{:S(2)}) collective-permute-start(bf16[272,1024]{1,0:T(8,128)(2,1)} %get-tuple-element.203), channel_id=1, source_target_pairs={{0,8},{8,0},{16,24},{24,16},{1,9},{9,1},{17,25},{25,17},{2,10},{10... | collective-permute-start | bytes 1671176 | tf_op jit(solution)/shard_map/ppermute | solution.py:957
  313.9 36.9 %collective-permute-start.42 = (bf16[272,1024]{1,0:T(8,128)(2,1)}, bf16[272,1024]{1,0:T(8,128)(2,1)}, u32[]{:S(2)}, u32[]{:S(2)}) collective-permute-start(bf16[272,1024]{1,0:T(8,128)(2,1)} %get-tuple-element.204), channel_id=1, source_target_pairs={{0,16},{8,24},{16,0},{24,8},{1,17},{9,25},{17,1},{25,9},{2,18},{10... | collective-permute-start | bytes 1671176 | tf_op jit(solution)/shard_map/ppermute | solution.py:957
  315.1 35.7 %collective-permute-start.43 = (bf16[272,1024]{1,0:T(8,128)(2,1)}, bf16[272,1024]{1,0:T(8,128)(2,1)}, u32[]{:S(2)}, u32[]{:S(2)}) collective-permute-start(bf16[272,1024]{1,0:T(8,128)(2,1)} %get-tuple-element.205), channel_id=1, source_target_pairs={{0,24},{8,16},{16,8},{24,0},{1,25},{9,17},{17,9},{25,1},{2,26},{10... | collective-permute-start | bytes 1671176 | tf_op jit(solution)/shard_map/ppermute | solution.py:957
  317.7 20.0 %collective-permute-start.45 = (bf16[256,1024]{1,0:T(8,128)(2,1)}, bf16[256,1024]{1,0:T(8,128)(2,1)}, u32[]{:S(2)}, u32[]{:S(2)}) collective-permute-start(bf16[256,1024]{1,0:T(8,128)(2,1)} %get-tuple-element.208), channel_id=1, source_target_pairs={{0,64},{32,96},{64,0},{96,32},{1,65},{33,97},{65,1},{97,33},{2,66}... | collective-permute-start | bytes 1572872 | tf_op jit(solution)/shard_map/ppermute | solution.py:958
  326.9 23.9 %collective-permute-start.46 = (bf16[256,1024]{1,0:T(8,128)(2,1)}, bf16[256,1024]{1,0:T(8,128)(2,1)}, u32[]{:S(2)}, u32[]{:S(2)}) collective-permute-start(bf16[256,1024]{1,0:T(8,128)(2,1)} %get-tuple-element.209), channel_id=1, source_target_pairs={{0,96},{32,64},{64,32},{96,0},{1,97},{33,65},{65,33},{97,1},{2,98}... | collective-permute-start | bytes 1572872 | tf_op jit(solution)/shard_map/ppermute | solution.py:958
  355.7 13.0 %collective-permute-start.47 = (bf16[80,1024]{1,0:T(8,128)(2,1)S(1)}, bf16[80,1024]{1,0:T(8,128)(2,1)S(1)}, u32[]{:S(2)}, u32[]{:S(2)}) collective-permute-start(bf16[80,1024]{1,0:T(8,128)(2,1)S(1)} %get-tuple-element.211), channel_id=1, source_target_pairs={{0,32},{32,0},{64,96},{96,64},{1,33},{33,1},{65,97},{97,65},{2,34}... | collective-permute-start | bytes 491528 | tf_op jit(solution)/shard_map/ppermute | solution.py:957
  356.1 9.6 %collective-permute-start.51 = (bf16[64,1024]{1,0:T(8,128)(2,1)S(1)}, bf16[64,1024]{1,0:T(8,128)(2,1)S(1)}, u32[]{:S(2)}, u32[]{:S(2)}) collective-permute-start(bf16[64,1024]{1,0:T(8,128)(2,1)S(1)} %get-tuple-element.216), channel_id=1, source_target_pairs={{0,16},{8,24},{16,0},{24,8},{1,17},{9,25},{17,1},{25,9},{2,18},{10... | collective-permute-start | bytes 393224 | tf_op jit(solution)/shard_map/ppermute | solution.py:958
  359.7 9.6 %collective-permute-start.48 = (bf16[80,1024]{1,0:T(8,128)(2,1)S(1)}, bf16[80,1024]{1,0:T(8,128)(2,1)S(1)}, u32[]{:S(2)}, u32[]{:S(2)}) collective-permute-start(bf16[80,1024]{1,0:T(8,128)(2,1)S(1)} %get-tuple-element.212), channel_id=1, source_target_pairs={{0,64},{32,96},{64,0},{96,32},{1,65},{33,97},{65,1},{97,33},{2,66}... | collective-permute-start | bytes 491528 | tf_op jit(solution)/shard_map/ppermute | solution.py:957
  363.5 19.1 %collective-permute-start.57 = (bf16[64,2048]{1,0:T(8,128)(2,1)}, bf16[64,2048]{1,0:T(8,128)(2,1)S(1)}, u32[]{:S(2)}, u32[]{:S(2)}) collective-permute-start(bf16[64,2048]{1,0:T(8,128)(2,1)} %get-tuple-element.236), channel_id=1, source_target_pairs={{0,6},{2,4},{4,2},{6,0},{1,7},{3,5},{5,3},{7,1},{8,14},{10,12},{12... | collective-permute-start | bytes 786440 | tf_op jit(solution)/shard_map/ppermute | solution.py:942
  365.7 16.9 %collective-permute-start.55 = (bf16[64,2048]{1,0:T(8,128)(2,1)}, bf16[64,2048]{1,0:T(8,128)(2,1)S(1)}, u32[]{:S(2)}, u32[]{:S(2)}) collective-permute-start(bf16[64,2048]{1,0:T(8,128)(2,1)} %get-tuple-element.231), channel_id=1, source_target_pairs={{0,4},{4,0},{1,5},{5,1},{2,6},{6,2},{3,7},{7,3},{8,12},{12,8},{9,1... | collective-permute-start | bytes 786440 | tf_op jit(solution)/shard_map/ppermute | solution.py:1222
  366.5 16.2 %collective-permute-start.56 = (bf16[64,2048]{1,0:T(8,128)(2,1)}, bf16[64,2048]{1,0:T(8,128)(2,1)S(1)}, u32[]{:S(2)}, u32[]{:S(2)}) collective-permute-start(bf16[64,2048]{1,0:T(8,128)(2,1)} %get-tuple-element.233), channel_id=1, source_target_pairs={{0,4},{2,6},{4,0},{6,2},{1,5},{3,7},{5,1},{7,3},{8,12},{10,14},{12... | collective-permute-start | bytes 786440 | tf_op jit(solution)/shard_map/ppermute | solution.py:942
  368.7 14.3 %collective-permute-start.54 = (bf16[64,2048]{1,0:T(8,128)(2,1)}, bf16[64,2048]{1,0:T(8,128)(2,1)S(1)}, u32[]{:S(2)}, u32[]{:S(2)}) collective-permute-start(bf16[64,2048]{1,0:T(8,128)(2,1)} %get-tuple-element.229), channel_id=1, source_target_pairs={{0,2},{2,0},{4,6},{6,4},{1,3},{3,1},{5,7},{7,5},{8,10},{10,8},{12,... | collective-permute-start | bytes 786440 | tf_op jit(solution)/shard_map/ppermute | solution.py:942
  376.5 14.3 %all-to-all-start.6 = ((bf16[8,8,2048]{2,1,0:T(8,128)(2,1)}), bf16[8,8,2048]{2,1,0:T(8,128)(2,1)S(1)}, u32[]{:S(2)}, u32[]{:S(2)}) async-start(bf16[8,8,2048]{2,1,0:T(8,128)(2,1)} %get-tuple-element.222), calls=%async_computation.7 | async-start | bytes 524288 | tf_op jit(solution)/shard_map/all_to_all | solution.py:963
  384.6 25.9 %collective-permute-start.59 = (bf16[4,16,2048]{2,1,0:T(8,128)(2,1)S(1)}, bf16[4,16,2048]{2,1,0:T(8,128)(2,1)S(1)}, u32[]{:S(2)}, u32[]{:S(2)}) collective-permute-start(bf16[4,16,2048]{2,1,0:T(8,128)(2,1)S(1)} %bitcast.72), channel_id=1, source_target_pairs={{0,2},{2,0},{1,3},{3,1},{4,6},{6,4},{5,7},{7,5},{8,10},{10,8},{9,1... | collective-permute-start | bytes 786440 | tf_op jit(solution)/shard_map/ppermute | solution.py:1252
  385.7 26.4 %collective-permute-start.58 = (bf16[4,16,2048]{2,1,0:T(8,128)(2,1)S(1)}, bf16[4,16,2048]{2,1,0:T(8,128)(2,1)S(1)}, u32[]{:S(2)}, u32[]{:S(2)}) collective-permute-start(bf16[4,16,2048]{2,1,0:T(8,128)(2,1)S(1)} %bitcast.73), channel_id=1, source_target_pairs={{0,1},{1,0},{2,3},{3,2},{4,5},{5,4},{6,7},{7,6},{8,9},{9,8},{10,11... | collective-permute-start | bytes 786440 | tf_op jit(solution)/shard_map/ppermute | solution.py:1253
  387.8 10.3 %collective-permute-start.61 = (bf16[80,1024]{1,0:T(8,128)(2,1)S(1)}, bf16[80,1024]{1,0:T(8,128)(2,1)S(1)}, u32[]{:S(2)}, u32[]{:S(2)}) collective-permute-start(bf16[80,1024]{1,0:T(8,128)(2,1)S(1)} %get-tuple-element.242), channel_id=1, source_target_pairs={{0,4},{4,0},{1,5},{5,1},{2,6},{6,2},{3,7},{7,3},{8,12},{12,8},{9,1... | collective-permute-start | bytes 491528 | tf_op jit(solution)/shard_map/ppermute | solution.py:1272
  391.5 10.8 %all-to-all-start.7 = ((f32[16,8,128]{2,1,0:T(8,128)}), f32[16,8,128]{2,1,0:T(8,128)S(1)}, u32[]{:S(2)}, u32[]{:S(2)}) async-start(f32[16,8,128]{2,1,0:T(8,128)} %get-tuple-element.240), calls=%async_computation.8 | async-start | bytes 131072 | tf_op jit(solution)/shard_map/all_to_all | solution.py:963
  (91 other events, 1083.6 us)
Sparse Core Ops, SparseCore 0:
  17.1 54.9 all-gather.2
  74.8 79.1 all-gather.4
  217.2 89.6 reduce-scatter.1
where the time goes:
time: 430 us; the launch traced here: 421 us
  starting transfers between devices  122 us (28%)
  waiting for transfers between devices  112 us (26%)
  Pallas kernels  107 us (25%)
  blocking collectives  30 us (7%)
  local copies, waits for them, and re-layouts  29.5 us (7%)
  between operations  14.7 us (3%)
  other arithmetic  5.78 us (1%)
    pallas_call x25, Pallas kernels, local_call(): pl.pallas_call(kernel, out_shape=tuple((in_hbm(o) if n in far else o for...  72.7 us
    all_to_all x2, blocking collectives, each_to_all(): return lax.all_to_all(copies, axis, split_axis=0, concat_axis=0, tiled=True)  30 us
    all_to_all x6, starting transfers between devices, each_to_all(): return lax.all_to_all(copies, axis, split_axis=0, concat_axis=0, tiled=True)  26.2 us
    ppermute x6, waiting for transfers between devices, crossing(): second[k] = lax.ppermute(second[k], second_axis, xor_pairs(4, k))  23.7 us
    all_to_all x6, waiting for transfers between devices, each_to_all(): return lax.all_to_all(copies, axis, split_axis=0, concat_axis=0, tiled=True)  21.5 us
    unnamed x141, local copies, waits for them, and re-layouts  21.1 us
    ppermute x12, starting transfers between devices, eight_parts(): parts += [line, lax.ppermute(line, C, SWAP)]  18.4 us
    ppermute x12, waiting for transfers between devices, line_scatter(): lax.ppermute(s, YY, xor_pairs(4, k))  17.5 us
  transfers between devices with their start and end apart: 71, of which 37 were waited for; matrix products, arithmetic and copies ran while one was open for 2% of the time, Pallas kernels for 22%

commit v1 on v0

--- a/solution.py
+++ b/solution.py
@@ -662,9 +662,13 @@
     )(dattn, c)
 
 
+def ring_block(group, i, j):
+    return (((group >> 2) + i) & 3) * 4 + ((group + j) & 3)
+
+
 def turn_kernel(ids, a_ref, out_ref):
     for r in range(16):
-        at = pl.ds(pl.multiple_of((ids[3] ^ r) * 128, 128), 128)
+        at = pl.ds(pl.multiple_of(ring_block(ids[3], r // 4, r % 4) * 128, 128), 128)
         to = (r % 4) * 4 + r // 4
         out_ref[to * 128 : (to + 1) * 128, :] = jnp.transpose(a_ref[:, at])
 
@@ -680,7 +684,16 @@
 def in_grad_kernel(
     ids, dqkv_ref, xt_ref, w_ref, pre_ref, out_ref, three_ref, o_ref, h_ref, *refs
 ):
-    lines, (tokens_ref, d_s, one_s) = refs[:8], refs[8:]
+    lines, (tokens_ref, d_s, one_s) = refs[:10], refs[10:]
+
+    def put(side, place, other, columns, value):
+        refs = lines[5 * side : 5 * side + 5]
+        if place == 2:
+            ref, row = refs[2 + other // 2], (other % 2) * 64
+        else:
+            ref, row = refs[(0, 1, None, 4)[place]], other * 64
+        ref[row : row + 64, columns] = value
+
     count = dqkv_ref.shape[0]
     heads = count // 4
     units = d_s.shape[0]
@@ -705,15 +718,14 @@
     for j in range(4):
         products = dot(xt_ref[j * 512 : (j + 1) * 512, :], d_s[...], 1, 1)
         for i in range(4):
-            at = pl.ds(pl.multiple_of((ids[3] ^ (4 * i + j)) * 128, 128), 128)
+            at = pl.ds(pl.multiple_of(ring_block(ids[3], i, j) * 128, 128), 128)
             product = products[i * 128 : (i + 1) * 128]
             gradient = product * column(pre_ref[0:1, at]) + column(pre_ref[1:2, at]) * sums
             gradient = gradient.astype(BF16)
-            lines[j][i * 64 : (i + 1) * 64, :units] = gradient[:64]
-            lines[4 + i][j * 64 : (j + 1) * 64, :units] = gradient[64:]
             outward = out_ref[at, :]
-            lines[j][i * 64 : (i + 1) * 64, units:] = outward[:64]
-            lines[4 + i][j * 64 : (j + 1) * 64, units:] = outward[64:]
+            for columns, value in ((slice(units), gradient), (slice(units, None), outward)):
+                put(0, j, i, columns, value[:64])
+                put(1, i, j, columns, value[64:])
             w = w_ref[at, :units].astype(F32)
             one_s[0:1, at] = row_of(jnp.sum(w * product, axis=1, keepdims=True))
             one_s[1:2, at] = row_of(jnp.sum(w * sums, axis=1, keepdims=True))
@@ -729,8 +741,8 @@
         small += [jnp.concatenate(first, axis=1), jnp.concatenate(last, axis=1)]
     small.append(jnp.zeros((16 - len(small), width), F32))
     small = jnp.concatenate(small, axis=0).astype(BF16)
-    for j in range(4):
-        lines[j][256:272, :] = small
+    for ref in (lines[0], lines[1], lines[2], lines[4]):
+        ref[ref.shape[0] - 16 :, :] = small
 
 
 def in_back_kernel(ids, d_ref, w_ref, keep_ref, send_ref, l_s):
@@ -745,8 +757,25 @@
     return total
 
 
+def ring_sum_kernel(*refs):
+    ins, outs = refs[:8], refs[8:]
+    for side in range(2):
+        on, back, got_on, got_back = ins[4 * side : 4 * side + 4]
+        out_on, out_back = outs[2 * side : 2 * side + 2]
+        rows = got_back.shape[0]
+        out_on[:rows, :] = (on[:rows].astype(F32) + got_on[:rows].astype(F32)).astype(BF16)
+        out_on[rows : 2 * rows, :] = on[rows : 2 * rows]
+        out_back[:rows, :] = back[:rows]
+        both = back[rows : 2 * rows].astype(F32) + got_back[...].astype(F32)
+        out_back[rows : 2 * rows, :] = both.astype(BF16)
+        if got_on.shape[0] > rows:
+            small = on[2 * rows :].astype(F32) + got_on[rows:].astype(F32)
+            out_on[2 * rows :, :] = small.astype(BF16)
+            out_back[2 * rows :, :] = back[2 * rows :]
+
+
 def line_sum_kernel(*refs):
-    first, second, outs = refs[:4], refs[4:8], refs[8:]
+    first, second, outs = refs[:3], refs[3:6], refs[6:]
     total = summed_low(first)
     small = total[256:272]
     outs[0][0:64, :] = total[0:64]
@@ -895,7 +924,7 @@
     specs = [blocks(n // 3, a) for n, a in enumerate(flat)]
     rows = [pl.BlockSpec((step, g.shape[1]), lambda i: (i, 0)) for g in gradients]
     a_rows = gradients[2].shape[0] // 16
-    norm = shape((8, 128))
+    norm = shape((1, 1))
     return pl.pallas_call(
         adam_kernel,
         grid=(gradients[2].shape[0] // step,),
@@ -951,12 +980,30 @@
     return lines[:1] + [after(line, *done) for line in lines[1:]], done
 
 
+def ring_pairs(k):
+    return [(i, (i + k) % 4) for i in range(4)]
+
+
 def crossing(lines, first_axis, second_axis):
     first, second = list(lines[:4]), list(lines[4:])
     for k in (2, 1, 3):
-        first[k] = lax.ppermute(first[k], first_axis, xor_pairs(4, k))
-        second[k] = lax.ppermute(second[k], second_axis, xor_pairs(4, k))
+        first[k] = lax.ppermute(first[k], first_axis, ring_pairs(k))
+        second[k] = lax.ppermute(second[k], second_axis, ring_pairs(k))
     return first, second
+
+
+def ring_crossing(lines):
+    sides = [(lines[:5], X), (lines[5:], Z)]
+    ins = []
+    for (_, on, two_on, two_back, back), axis in sides:
+        ins += [on, back]
+        ins += [lax.ppermute(two_on, axis, ring_pairs(1)), lax.ppermute(two_back, axis, ring_pairs(3))]
+    outs = [shape(ins[n].shape, BF16) for n in (0, 1, 4, 5)]
+    sums = local_call(ring_sum_kernel, "ring_sum", outs, ins, moved=5 * MIB)
+    return [
+        [side[0], lax.ppermute(on, axis, ring_pairs(1)), lax.ppermute(back, axis, ring_pairs(3))]
+        for (side, axis), on, back in zip(sides, sums[::2], sums[1::2])
+    ]
 
 
 def each_to_all(copies, axis):
@@ -1199,7 +1246,8 @@
     dqkv = each_to_all(after(dqkv, *scattered), ZX)
 
     both = 4 * half
-    line = [shape((4 * seq_slots + 16, both), BF16)] * 4 + [shape((4 * seq_slots, both), BF16)] * 4
+    line = [shape((count, both), BF16) for count in (272, 272, 144, 128, 272)]
+    line += [shape((count, both), BF16) for count in (256, 256, 128, 128, 256)]
     *lines, dproj = local_call(
         in_grad_kernel,
         "in_grad",
@@ -1208,9 +1256,9 @@
         [pltpu.VMEM((3 * half, tokens), BF16), pltpu.VMEM((2, width), F32)],
         flops=2 * tokens * width * 3 * half,
         moved=13 * MIB,
-        far=range(8),
-    )
-    first, second = crossing(lines, X, Z)
+        far=range(10),
+    )
+    first, second = ring_crossing(lines)
     mlp_keep, mlp_give, squares_mlp = local_call(
         rest_kernel,
         "rest",
@@ -1305,7 +1353,7 @@
         [tuple(jnp.transpose(a, turn) for a in state) for state, turn in zip(states, turns)],
     )
     updated = [jnp.transpose(a, turns[n // 3]) for n, a in enumerate(updated)]
-    return (hidden_out, input_grad, *updated, norm[0, 0])
+    return (hidden_out, input_grad, *updated, norm.reshape(()))
 
 
 def solution(mesh):

time: 430 us -> 426 us (level)
  waiting for transfers between devices: 112 us -> 94.8 us
  starting transfers between devices: 122 us -> 134 us
    ppermute x12 -> x14, waiting for transfers between devices: 28.1 us -> 9.25 us  [the longest x2 3.15 us: ring_crossing(): lax.ppermute(two_on, axis, ring_pairs(1))]
    ppermute x12 -> x14, starting transfers between devices: 14.6 us -> 19.8 us  [the longest x3 6.33 us: crossing(): first[k] = lax.ppermute(first[k], first_axis, ring_pairs(k))]
    unnamed x141 -> x147, local copies, waits for them, and re-layouts: 21.1 us -> 23.9 us
    pallas_call x25 -> x26, Pallas kernels: 72.7 us -> 73.5 us  [local_call(): pl.pallas_call(kernel, out_shape=tuple((in_hbm(o) if n in far else o for...]
  transfers between devices with their start and end apart: 71 -> 73, of which waited for: 37 -> 38; matrix products, arithmetic and copies ran while one was open for 2% -> 2% of each run, Pallas kernels for 22% -> 22%
where the time goes in v1:
time: 426 us; the launch traced here: 417 us
  starting transfers between devices  134 us (31%)
  Pallas kernels  108 us (25%)
  waiting for transfers between devices  94.8 us (22%)
  local copies, waits for them, and re-layouts  31.1 us (7%)
  blocking collectives  28.6 us (7%)
  between operations  14.8 us (3%)
  other arithmetic  5.8 us (1%)
    pallas_call x26, Pallas kernels, local_call(): pl.pallas_call(kernel, out_shape=tuple((in_hbm(o) if n in far else o for...  73.5 us
    all_to_all x2, blocking collectives, each_to_all(): return lax.all_to_all(copies, axis, split_axis=0, concat_axis=0, tiled=True)  28.6 us
    all_to_all x6, starting transfers between devices, each_to_all(): return lax.all_to_all(copies, axis, split_axis=0, concat_axis=0, tiled=True)  27.4 us
    unnamed x147, local copies, waits for them, and re-layouts  23.9 us
    all_to_all x6, waiting for transfers between devices, each_to_all(): return lax.all_to_all(copies, axis, split_axis=0, concat_axis=0, tiled=True)  22.1 us
    ppermute x12, waiting for transfers between devices, line_scatter(): lax.ppermute(s, YY, xor_pairs(4, k))  18.5 us
    ppermute x12, starting transfers between devices, eight_parts(): parts += [line, lax.ppermute(line, C, SWAP)]  18.4 us
    ppermute x12, starting transfers between devices, line_scatter(): lax.ppermute(s, YY, xor_pairs(4, k))  17.3 us
  transfers between devices with their start and end apart: 73, of which 38 were waited for; matrix products, arithmetic and copies ran while one was open for 2% of the time, Pallas kernels for 22%

profile of v1, /device:TPU:1, one launch (start us, length us, event | category | flops | bytes accessed | tf_op | source)
XLA Modules:
  0.0 417.2 jit_solution(5303187214655008107)
XLA Ops:
  9.4 3.8 collective-permute-start.9
  13.2 2.9 collective-permute-done.9
  17.4 3.0 collective-permute-start.20
  20.5 4.8 %collective-permute-done.20 = bf16[64,2048]{1,0:T(8,128)(2,1)S(1)} collective-permute-done((bf16[64,2048]{1,0:T(8,128)(2,1)S(1)}, bf16[64,2048]{1,0:T(8,128)(2,1)S(1)}, u32[]{:S(2)}, u32[]{:S(2)}) %collective-permute-start.20) | collective-permute-done | bytes 262176 | tf_op jit(solution)/shard_map/ppermute | solution.py:1057
  29.7 8.9 %collective-permute-done.near_ref = bf16[4,32,2048]{2,1,0:T(8,128)(2,1)S(1)} collective-permute-done((bf16[4,32,2048]{2,1,0:T(8,128)(2,1)S(1)}, bf16[4,32,2048]{2,1,0:T(8,128)(2,1)S(1)}, u32[]{:S(2)}, u32[]{:S(2)}) %collective-permute-start) | collective-permute-done | bytes 524320 | tf_op jit(solution)/shard_map/ppermute | solution.py:1088
  38.7 3.7 collective-permute-start.5
  42.5 4.2 collective-permute-start.1
  46.6 3.5 collective-permute-start.4
  50.7 4.7 %collective-permute-start.6 = (bf16[64,2048]{1,0:T(8,128)(2,1)S(1)}, bf16[64,2048]{1,0:T(8,128)(2,1)}, u32[]{:S(2)}, u32[]{:S(2)}) collective-permute-start(bf16[64,2048]{1,0:T(8,128)(2,1)S(1)} %collective-permute-done.5.refs_4_), channel_id=1, source_target_pairs={{0,1},{1,0},{2,3},{3,2},{4,5},{5,4},{6,7},{7,6},{8,9},{9,8},{10,11... | collective-permute-start | bytes 786440 | tf_op jit(solution)/shard_map/ppermute | solution.py:954
  59.2 12.8 %all-gather.3.cloned.1.call-done.w_ref = bf16[2048,1024]{1,0:T(8,128)(2,1)} async-done(((bf16[128,1024]{1,0:T(8,128)(2,1)}), bf16[2048,1024]{1,0:T(8,128)(2,1)}) %all-gather.3.cloned.1.call-update) | async-done | bytes 4194320 | tf_op jit(solution)/shard_map/all_gather | solution.py:1069
  74.2 4.6 %project.1 = (bf16[16,3,64,128]{3,2,1,0:T(8,128)(2,1)}, bf16[512,2048]{1,0:T(8,128)(2,1)}) custom-call(s32[4]{0:T(128)S(1)} %pad_add_fusion.ids, bf16[4,64,2048]{2,1,0:T(8,128)(2,1)S(1)} %copy-done.6, bf16[4,32,2048]{2,1,0:T(8,128)(2,1)S(1)} %collective-permute-done.near_ref, bf16[4,32,2048]{2,1,0:T(8,128)(2,1)S(1)} %collective-permute-done.1.far_ref, ...), custom_call_target="tpu_custom_call" | custom-call | flops 1610612736 | bytes 8388608 | tf_op jit(solution)/shard_map/project/pallas_call | solution.py:68
  78.8 5.0 %all-to-all-start = ((bf16[16,3,64,128]{3,2,1,0:T(8,128)(2,1)}), bf16[16,3,64,128]{3,2,1,0:T(8,128)(2,1)S(1)}, u32[]{:S(2)}, u32[]{:S(2)}) async-start(bf16[16,3,64,128]{3,2,1,0:T(8,128)(2,1)} %get-tuple-element.150), calls=%async_computation | async-start | bytes 1572864 | tf_op jit(solution)/shard_map/all_to_all | solution.py:1010
  87.5 2.8 collective-permute-start.11
  95.6 6.8 %all-to-all-done.qkv_ref = bf16[16,3,64,128]{3,2,1,0:T(8,128)(2,1)S(1)} async-done(((bf16[16,3,64,128]{3,2,1,0:T(8,128)(2,1)}), bf16[16,3,64,128]{3,2,1,0:T(8,128)(2,1)S(1)}, u32[]{:S(2)}, u32[]{:S(2)}) %all-to-all-start) | async-done | bytes 786464 | tf_op jit(solution)/shard_map/all_to_all | solution.py:1010
  102.4 5.8 %attend.1 = (f32[16,64,128]{2,1,0:T(8,128)}, bf16[16,64,128]{2,1,0:T(8,128)(2,1)}, f32[1,2048]{1,0:T(1,128)S(1)}) custom-call(bf16[16,3,64,128]{3,2,1,0:T(8,128)(2,1)S(1)} %all-to-all-done.qkv_ref, s32[1,2048]{1,0:T(1,128)S(1)} %bitcast.78), custom_call_target="tpu_custom_call" | custom-call | flops 2000000000 | bytes 4000000 | tf_op jit(solution)/shard_map/attend/pallas_call | solution.py:200
  108.1 3.5 all-to-all-start.1
  111.9 7.3 %all-to-all-done.1.o_ref.refs_9_.refs_0_.refs_1_ = bf16[16,64,128]{2,1,0:T(8,128)(2,1)S(1)} async-done(((bf16[16,64,128]{2,1,0:T(8,128)(2,1)}), bf16[16,64,128]{2,1,0:T(8,128)(2,1)S(1)}, u32[]{:S(2)}, u32[]{:S(2)}) %all-to-all-start.1) | async-done | bytes 262176 | tf_op jit(solution)/shard_map/all_to_all | solution.py:1010
  119.2 3.2 out.1
  122.4 7.6 %collective-permute-start.14 = (bf16[256,2176]{1,0:T(8,128)(2,1)S(1)}, bf16[256,2176]{1,0:T(8,128)(2,1)S(1)}, u32[]{:S(2)}, u32[]{:S(2)}) collective-permute-start(bf16[256,2176]{1,0:T(8,128)(2,1)S(1)} %get-tuple-element.156), channel_id=1, source_target_pairs={{0,1},{1,0},{2,3},{3,2},{4,5},{5,4},{6,7},{7,6},{8,9},{9,8},{10,11... | collective-permute-start | bytes 3342344 | tf_op jit(solution)/shard_map/ppermute | solution.py:960
  138.6 4.2 %collective-permute-done.15.one = bf16[64,2176]{1,0:T(8,128)(2,1)S(1)} collective-permute-done((bf16[64,2176]{1,0:T(8,128)(2,1)}, bf16[64,2176]{1,0:T(8,128)(2,1)S(1)}, u32[]{:S(2)}, u32[]{:S(2)}) %collective-permute-start.15) | collective-permute-done | bytes 278560 | tf_op jit(solution)/shard_map/ppermute | solution.py:971
  142.8 8.2 %collective-permute-done.16.two = bf16[64,2176]{1,0:T(8,128)(2,1)} collective-permute-done((bf16[64,2176]{1,0:T(8,128)(2,1)}, bf16[64,2176]{1,0:T(8,128)(2,1)}, u32[]{:S(2)}, u32[]{:S(2)}) %collective-permute-start.16) | collective-permute-done | bytes 278560 | tf_op jit(solution)/shard_map/ppermute | solution.py:971
  156.7 3.1 collective-permute-start.19
  162.5 3.9 fusion.5
  166.4 6.7 %down_back.1 = (bf16[512,2048]{1,0:T(8,128)(2,1)}, f32[512,1024]{1,0:T(8,128)S(1)}) custom-call(s32[4]{0:T(128)S(1)} %pad_add_fusion.ids, bf16[64,2048]{1,0:T(8,128)(2,1)} %copy-done.55, bf16[64,2048]{1,0:T(8,128)(2,1)} %collective-permute-done.2.refs_1_, bf16[64,2048]{1,0:T(8,128)(2,1)} %copy-done.68, bf16[64,2048]{1,0:T(8,128)(2,1)} %collective-permute-done.4.refs_3_, ...), custom_call_target="tpu_custom_call" | custom-call | flops 2147483648 | bytes 10485760 | tf_op jit(solution)/shard_map/down_back/pallas_call | solution.py:68
  176.2 6.4 %up.1 = (bf16[512,2048]{1,0:T(8,128)(2,1)}, f32[512,1024]{1,0:T(8,128)S(1)}, f32[512,1024]{1,0:T(8,128)S(1)}, f32[8,8,512]{2,1,0:T(8,128)S(1)}) custom-call(s32[4]{0:T(128)S(1)} %pad_add_fusion.ids, bf16[64,2048]{1,0:T(8,128)(2,1)} %copy-done.30, bf16[64,2048]{1,0:T(8,128)(2,1)} %copy-done.51, bf16[64,2048]{1,0:T(8,128)(2,1)} %copy-done.50, ...), custom_call_target="tpu_custom_call" | custom-call | flops 2147483648 | bytes 14680064 | tf_op jit(solution)/shard_map/up/pallas_call | solution.py:68
  182.7 7.8 %all_to_all.40.sums_ref.refs_10_.refs_1_.refs_2_ = f32[8,8,512]{2,1,0:T(8,128)S(1)} all-to-all(f32[8,8,512]{2,1,0:T(8,128)S(1)} %get-tuple-element.170), channel_id=1, replica_groups=mesh['seq_0'=4,'seq_1'=4,'seq_2'=2,'ffn_0'=2,'ffn_1'=2] {'seq_2','ffn_0'..., dimensions={0} | all-to-all | bytes 262144 | tf_op jit(solution)/shard_map/all_to_all | solution.py:1010
  190.4 7.4 %inner_back.1 = (f32[256,2048]{1,0:T(8,128)S(1)}, bf16[256,2048]{1,0:T(8,128)(2,1)S(1)}, bf16[512,1024]{1,0:T(8,128)(2,1)}, bf16[512,1024]{1,0:T(8,128)(2,1)}, f32[2,1024]{1,0:T(2,128)S(1)}) custom-call(s32[4]{0:T(128)S(1)} %pad_add_fusion.ids, f32[512,1024]{1,0:T(8,128)S(1)} %get-tuple-element.168.h_ref, f32[512,1024]{1,0:T(8,128)S(1)} %get-tuple-element.169.slope_ref, ...), custom_call_target="tpu_custom_call" | custom-call | flops 2147483648 | bytes 14680064 | tf_op jit(solution)/shard_map/inner_back/pallas_call | solution.py:68
  206.5 8.1 %mlp_grad.1 = bf16[2048,2048]{1,0:T(8,128)(2,1)} custom-call(bf16[512,2048]{1,0:T(8,128)(2,1)S(1)} %copy-done.42, bf16[512,1024]{1,0:T(8,128)(2,1)S(1)} %copy-done.35, bf16[512,2048]{1,0:T(8,128)(2,1)S(1)} %copy-done.34, bf16[512,1024]{1,0:T(8,128)(2,1)S(1)} %copy-done.38), custom_call_target="tpu_custom_call" | custom-call | flops 4294967296 | bytes 14680064 | tf_op jit(solution)/shard_map/mlp_grad/pallas_call | solution.py:552
  225.3 5.4 %down.1 = (f32[256,2048]{1,0:T(8,128)S(1)}, bf16[256,2048]{1,0:T(8,128)(2,1)}) custom-call(s32[4]{0:T(128)S(1)} %pad_add_fusion.ids, bf16[512,1024]{1,0:T(8,128)(2,1)S(1)} %copy-done.36, bf16[2048,1024]{1,0:T(8,128)(2,1)S(1)} %copy-done.4), custom_call_target="tpu_custom_call" | custom-call | flops 2147483648 | bytes 8388608 | tf_op jit(solution)/shard_map/down/pallas_call | solution.py:68
  238.0 4.1 out_back.1
  242.1 3.8 all-to-all-start.3
  253.3 3.5 all-to-all-start.4
  264.1 3.9 all-to-all-done.4.do_ref
  273.5 11.6 %attend_back.1 = bf16[16,3,64,128]{3,2,1,0:T(8,128)(2,1)} custom-call(bf16[16,3,64,128]{3,2,1,0:T(8,128)(2,1)S(1)} %copy-done.17, bf16[16,64,128]{2,1,0:T(8,128)(2,1)S(1)} %all-to-all-done.4.do_ref, f32[16,64,128]{2,1,0:T(8,128)S(1)} %copy-done.43, f32[1,2048]{1,0:T(1,128)S(1)} %get-tuple-element.203.top_ref, s32[1,2048]{1,0:T(1,128)S(1)} %bitcast.79, ...), custom_call_target="tpu_custom_call" | custom-call | flops 6000000000 | bytes 6000000 | tf_op jit(solution)/shard_map/attend_back/pallas_call | solution.py:226
  285.9 20.9 %all_to_all.41.dqkv_ref = bf16[16,3,64,128]{3,2,1,0:T(8,128)(2,1)S(1)} all-to-all(bf16[16,3,64,128]{3,2,1,0:T(8,128)(2,1)} %attend_back.1), channel_id=1, replica_groups=mesh['seq_0'=4,'seq_1'=4,'seq_2'=2,'ffn_0'=2,'ffn_1'=2] {'seq_0','seq_1'}, dimensions={0} | all-to-all | bytes 1572864 | tf_op jit(solution)/shard_map/all_to_all | solution.py:1010
  306.8 6.3 %in_grad.1 = (bf16[272,1024]{1,0:T(8,128)(2,1)}, bf16[272,1024]{1,0:T(8,128)(2,1)}, bf16[144,1024]{1,0:T(8,128)(2,1)}, bf16[128,1024]{1,0:T(8,128)(2,1)}, bf16[2...) custom-call(s32[4]{0:T(128)S(1)} %pad_add_fusion.ids, ...), custom_call_target="tpu_custom_call" | custom-call | flops 1610612736 | bytes 13631488 | tf_op jit(solution)/shard_map/in_grad/pallas_call | solution.py:68
  319.6 3.1 collective-permute-done.43.refs_6_
  333.8 3.9 in_back.1
  342.2 4.8 %collective-permute-start.55 = (bf16[256,2048]{1,0:T(8,128)(2,1)}, bf16[256,2048]{1,0:T(8,128)(2,1)S(1)}, u32[]{:S(2)}, u32[]{:S(2)}) collective-permute-start(bf16[256,2048]{1,0:T(8,128)(2,1)} %copy-done.37), channel_id=1, source_target_pairs={{0,1},{1,0},{2,3},{3,2},{4,5},{5,4},{6,7},{7,6},{8,9},{9,8},{10,11... | collective-permute-start | bytes 3145736 | tf_op jit(solution)/shard_map/ppermute | solution.py:960
  353.2 3.3 collective-permute-start.50
  359.4 2.8 collective-permute-start.59
  362.2 3.0 collective-permute-start.58
  372.2 6.5 %all-to-all-start.6 = ((bf16[8,8,2048]{2,1,0:T(8,128)(2,1)}), bf16[8,8,2048]{2,1,0:T(8,128)(2,1)S(1)}, u32[]{:S(2)}, u32[]{:S(2)}) async-start(bf16[8,8,2048]{2,1,0:T(8,128)(2,1)} %get-tuple-element.234), calls=%async_computation.7 | async-start | bytes 524288 | tf_op jit(solution)/shard_map/all_to_all | solution.py:1010
  380.7 3.0 collective-permute-start.60
  383.7 3.0 collective-permute-start.63
  387.4 5.2 %all-to-all-start.7 = ((f32[16,8,128]{2,1,0:T(8,128)}), f32[16,8,128]{2,1,0:T(8,128)S(1)}, u32[]{:S(2)}, u32[]{:S(2)}) async-start(f32[16,8,128]{2,1,0:T(8,128)} %get-tuple-element.252), calls=%async_computation.8 | async-start | bytes 131072 | tf_op jit(solution)/shard_map/all_to_all | solution.py:1010
  395.0 4.1 all-to-all-done.7.norm_part
  399.7 6.4 %adam.1 = (f32[3,64,512]{2,1,0:T(8,128)}, f32[3,64,512]{2,1,0:T(8,128)}, f32[3,64,512]{2,1,0:T(8,128)}, f32[64,512]{1,0:T(8,128)}, f32[64,512]{1,0:T(8,128)}, /*...) custom-call(s32[4]{0:T(128)} %copy-done.32, ...), custom_call_target="tpu_custom_call" | custom-call | bytes 12582912 | tf_op jit(solution)/shard_map/adam/pallas_call | solution.py:928
  (322 shorter events, 139.2 us)
Async XLA Ops:
  7.2 64.8 %all-gather.3.cloned.1.call-start = ((), (), s32[]{:S(2)}) async-start(), calls=%async_computation.9 | async-start | bytes 4456448 | tf_op jit(solution)/shard_map/all_gather | solution.py:1069
  17.0 145.5 %all-gather.5.cloned.1.call-start = ((), (), s32[]{:S(2)}) async-start(), calls=%async_computation.10 | async-start | bytes 8912896 | tf_op jit(solution)/shard_map/all_gather | solution.py:1072
  26.2 12.3 %collective-permute-start = (bf16[4,32,2048]{2,1,0:T(8,128)(2,1)S(1)}, bf16[4,32,2048]{2,1,0:T(8,128)(2,1)S(1)}, u32[]{:S(2)}, u32[]{:S(2)}) collective-permute-start(bf16[4,32,2048]{2,1,0:T(8,128)(2,1)S(1)} %constant_dynamic-slice_fusion.8), channel_id=1, source_target_pairs={{0,6},{2,4},{4,2},{6,0},{1,7},{3,5},{5,3},{7,1},{8,14},{10,12},{12... | collective-permute-start | bytes 1572872 | tf_op jit(solution)/shard_map/ppermute | solution.py:1088
  38.7 12.1 %collective-permute-start.5 = (bf16[64,2048]{1,0:T(8,128)(2,1)S(1)}, bf16[64,2048]{1,0:T(8,128)(2,1)S(1)}, u32[]{:S(2)}, u32[]{:S(2)}) collective-permute-start(bf16[64,2048]{1,0:T(8,128)(2,1)S(1)} %multiply_convert_fusion.refs_0_), channel_id=1, source_target_pairs={{0,4},{2,6},{4,0},{6,2},{1,5},{3,7},{5,1},{7,3},{8,12},{10,14},{12... | collective-permute-start | bytes 786440 | tf_op jit(solution)/shard_map/ppermute | solution.py:948
  42.4 13.4 %collective-permute-start.7 = (bf16[64,2048]{1,0:T(8,128)(2,1)S(1)}, bf16[64,2048]{1,0:T(8,128)(2,1)S(1)}, u32[]{:S(2)}, u32[]{:S(2)}) collective-permute-start(bf16[64,2048]{1,0:T(8,128)(2,1)S(1)} %multiply_convert_fusion.refs_0_), channel_id=1, source_target_pairs={{0,6},{2,4},{4,2},{6,0},{1,7},{3,5},{5,3},{7,1},{8,14},{10,12},{12... | collective-permute-start | bytes 786440 | tf_op jit(solution)/shard_map/ppermute | solution.py:948
  42.5 16.8 %collective-permute-start.1 = (bf16[4,32,2048]{2,1,0:T(8,128)(2,1)S(1)}, bf16[4,32,2048]{2,1,0:T(8,128)(2,1)S(1)}, u32[]{:S(2)}, u32[]{:S(2)}) collective-permute-start(bf16[4,32,2048]{2,1,0:T(8,128)(2,1)S(1)} %collective-permute-done.near_ref), channel_id=1, source_target_pairs={{0,1},{1,0},{2,3},{3,2},{4,5},{5,4},{6,7},{7,6},{8,9},{9,8},{10,11... | collective-permute-start | bytes 1572872 | tf_op jit(solution)/shard_map/ppermute | solution.py:1089
  46.6 12.3 %collective-permute-start.2 = (bf16[64,2048]{1,0:T(8,128)(2,1)S(1)}, bf16[64,2048]{1,0:T(8,128)(2,1)}, u32[]{:S(2)}, u32[]{:S(2)}) collective-permute-start(bf16[64,2048]{1,0:T(8,128)(2,1)S(1)} %multiply_convert_fusion.refs_0_), channel_id=1, source_target_pairs={{0,1},{1,0},{2,3},{3,2},{4,5},{5,4},{6,7},{7,6},{8,9},{9,8},{10,11... | collective-permute-start | bytes 786440 | tf_op jit(solution)/shard_map/ppermute | solution.py:954
  46.6 12.3 %collective-permute-start.4 = (bf16[64,2048]{1,0:T(8,128)(2,1)S(1)}, bf16[64,2048]{1,0:T(8,128)(2,1)}, u32[]{:S(2)}, u32[]{:S(2)}) collective-permute-start(bf16[64,2048]{1,0:T(8,128)(2,1)S(1)} %collective-permute-done.3.refs_2_), channel_id=1, source_target_pairs={{0,1},{1,0},{2,3},{3,2},{4,5},{5,4},{6,7},{7,6},{8,9},{9,8},{10,11... | collective-permute-start | bytes 786440 | tf_op jit(solution)/shard_map/ppermute | solution.py:954
  78.8 23.5 %all-to-all-start = ((bf16[16,3,64,128]{3,2,1,0:T(8,128)(2,1)}), bf16[16,3,64,128]{3,2,1,0:T(8,128)(2,1)S(1)}, u32[]{:S(2)}, u32[]{:S(2)}) async-start(bf16[16,3,64,128]{3,2,1,0:T(8,128)(2,1)} %get-tuple-element.150), calls=%async_computation | async-start | bytes 1572864 | tf_op jit(solution)/shard_map/all_to_all | solution.py:1010
  108.1 11.1 %all-to-all-start.1 = ((bf16[16,64,128]{2,1,0:T(8,128)(2,1)}), bf16[16,64,128]{2,1,0:T(8,128)(2,1)S(1)}, u32[]{:S(2)}, u32[]{:S(2)}) async-start(bf16[16,64,128]{2,1,0:T(8,128)(2,1)} %get-tuple-element.154), calls=%async_computation.1 | async-start | bytes 524288 | tf_op jit(solution)/shard_map/all_to_all | solution.py:1010
  111.7 227.0 %reduce-scatter.2.cloned.1.call-start = ((), (), s32[]{:S(2)}) async-start(), calls=%async_computation.11 | async-start | bytes 8912896 | tf_op jit(solution)/shard_map/reduce_scatter | solution.py:1195
  122.4 10.0 %collective-permute-start.14 = (bf16[256,2176]{1,0:T(8,128)(2,1)S(1)}, bf16[256,2176]{1,0:T(8,128)(2,1)S(1)}, u32[]{:S(2)}, u32[]{:S(2)}) collective-permute-start(bf16[256,2176]{1,0:T(8,128)(2,1)S(1)} %get-tuple-element.156), channel_id=1, source_target_pairs={{0,1},{1,0},{2,3},{3,2},{4,5},{5,4},{6,7},{7,6},{8,9},{9,8},{10,11... | collective-permute-start | bytes 3342344 | tf_op jit(solution)/shard_map/ppermute | solution.py:960
  135.8 15.2 %collective-permute-start.16 = (bf16[64,2176]{1,0:T(8,128)(2,1)}, bf16[64,2176]{1,0:T(8,128)(2,1)}, u32[]{:S(2)}, u32[]{:S(2)}) collective-permute-start(bf16[64,2176]{1,0:T(8,128)(2,1)} %get-tuple-element.159), channel_id=1, source_target_pairs={{0,4},{2,6},{4,0},{6,2},{1,5},{3,7},{5,1},{7,3},{8,12},{10,14},{12... | collective-permute-start | bytes 835592 | tf_op jit(solution)/shard_map/ppermute | solution.py:971
  138.2 14.7 %collective-permute-start.17 = (bf16[64,2176]{1,0:T(8,128)(2,1)}, bf16[64,2176]{1,0:T(8,128)(2,1)}, u32[]{:S(2)}, u32[]{:S(2)}) collective-permute-start(bf16[64,2176]{1,0:T(8,128)(2,1)} %get-tuple-element.160), channel_id=1, source_target_pairs={{0,6},{2,4},{4,2},{6,0},{1,7},{3,5},{5,3},{7,1},{8,14},{10,12},{12... | collective-permute-start | bytes 835592 | tf_op jit(solution)/shard_map/ppermute | solution.py:971
  156.5 16.6 %collective-permute-start.24 = (bf16[64,2048]{1,0:T(8,128)(2,1)S(1)}, bf16[64,2048]{1,0:T(8,128)(2,1)S(1)}, u32[]{:S(2)}, u32[]{:S(2)}) collective-permute-start(bf16[64,2048]{1,0:T(8,128)(2,1)S(1)} %get-tuple-element.161.refs_0_), channel_id=1, source_target_pairs={{0,6},{2,4},{4,2},{6,0},{1,7},{3,5},{5,3},{7,1},{8,14},{10,12},{12... | collective-permute-start | bytes 786440 | tf_op jit(solution)/shard_map/ppermute | solution.py:948
  156.7 16.5 %collective-permute-start.22 = (bf16[64,2048]{1,0:T(8,128)(2,1)S(1)}, bf16[64,2048]{1,0:T(8,128)(2,1)S(1)}, u32[]{:S(2)}, u32[]{:S(2)}) collective-permute-start(bf16[64,2048]{1,0:T(8,128)(2,1)S(1)} %get-tuple-element.161.refs_0_), channel_id=1, source_target_pairs={{0,4},{2,6},{4,0},{6,2},{1,5},{3,7},{5,1},{7,3},{8,12},{10,14},{12... | collective-permute-start | bytes 786440 | tf_op jit(solution)/shard_map/ppermute | solution.py:948
  156.7 17.0 %collective-permute-start.19 = (bf16[64,2048]{1,0:T(8,128)(2,1)S(1)}, bf16[64,2048]{1,0:T(8,128)(2,1)S(1)}, u32[]{:S(2)}, u32[]{:S(2)}) collective-permute-start(bf16[64,2048]{1,0:T(8,128)(2,1)S(1)} %get-tuple-element.161.refs_0_), channel_id=1, source_target_pairs={{0,2},{2,0},{4,6},{6,4},{1,3},{3,1},{5,7},{7,5},{8,10},{10,8},{12,... | collective-permute-start | bytes 786440 | tf_op jit(solution)/shard_map/ppermute | solution.py:948
  159.8 14.4 %collective-permute-start.18 = (bf16[64,2048]{1,0:T(8,128)(2,1)S(1)}, bf16[64,2048]{1,0:T(8,128)(2,1)S(1)}, u32[]{:S(2)}, u32[]{:S(2)}) collective-permute-start(bf16[64,2048]{1,0:T(8,128)(2,1)S(1)} %get-tuple-element.161.refs_0_), channel_id=1, source_target_pairs={{0,1},{1,0},{2,3},{3,2},{4,5},{5,4},{6,7},{7,6},{8,9},{9,8},{10,11... | collective-permute-start | bytes 786440 | tf_op jit(solution)/shard_map/ppermute | solution.py:954
  202.0 14.7 %collective-permute-start.29 = (bf16[64,2048]{1,0:T(8,128)(2,1)}, bf16[64,2048]{1,0:T(8,128)(2,1)}, u32[]{:S(2)}, u32[]{:S(2)}) collective-permute-start(bf16[64,2048]{1,0:T(8,128)(2,1)} %get-tuple-element.185), channel_id=1, source_target_pairs={{0,6},{2,4},{4,2},{6,0},{1,7},{3,5},{5,3},{7,1},{8,14},{10,12},{12... | collective-permute-start | bytes 786440 | tf_op jit(solution)/shard_map/ppermute | solution.py:971
  202.9 13.8 %collective-permute-start.28 = (bf16[64,2048]{1,0:T(8,128)(2,1)}, bf16[64,2048]{1,0:T(8,128)(2,1)}, u32[]{:S(2)}, u32[]{:S(2)}) collective-permute-start(bf16[64,2048]{1,0:T(8,128)(2,1)} %get-tuple-element.183), channel_id=1, source_target_pairs={{0,4},{2,6},{4,0},{6,2},{1,5},{3,7},{5,1},{7,3},{8,12},{10,14},{12... | collective-permute-start | bytes 786440 | tf_op jit(solution)/shard_map/ppermute | solution.py:971
  204.1 12.9 %collective-permute-start.27 = (bf16[64,2048]{1,0:T(8,128)(2,1)}, bf16[64,2048]{1,0:T(8,128)(2,1)}, u32[]{:S(2)}, u32[]{:S(2)}) collective-permute-start(bf16[64,2048]{1,0:T(8,128)(2,1)} %get-tuple-element.177), channel_id=1, source_target_pairs={{0,2},{2,0},{4,6},{6,4},{1,3},{3,1},{5,7},{7,5},{8,10},{10,8},{12,... | collective-permute-start | bytes 786440 | tf_op jit(solution)/shard_map/ppermute | solution.py:971
  219.8 13.9 %collective-permute-start.35 = (bf16[64,2048]{1,0:T(8,128)(2,1)S(1)}, bf16[64,2048]{1,0:T(8,128)(2,1)S(1)}, u32[]{:S(2)}, u32[]{:S(2)}) collective-permute-start(bf16[64,2048]{1,0:T(8,128)(2,1)S(1)} %get-tuple-element.188.refs_0_), channel_id=1, source_target_pairs={{0,6},{2,4},{4,2},{6,0},{1,7},{3,5},{5,3},{7,1},{8,14},{10,12},{12... | collective-permute-start | bytes 786440 | tf_op jit(solution)/shard_map/ppermute | solution.py:948
  220.7 14.7 %collective-permute-start.33 = (bf16[64,2048]{1,0:T(8,128)(2,1)S(1)}, bf16[64,2048]{1,0:T(8,128)(2,1)S(1)}, u32[]{:S(2)}, u32[]{:S(2)}) collective-permute-start(bf16[64,2048]{1,0:T(8,128)(2,1)S(1)} %get-tuple-element.188.refs_0_), channel_id=1, source_target_pairs={{0,4},{2,6},{4,0},{6,2},{1,5},{3,7},{5,1},{7,3},{8,12},{10,14},{12... | collective-permute-start | bytes 786440 | tf_op jit(solution)/shard_map/ppermute | solution.py:948
  221.8 13.6 %collective-permute-start.31 = (bf16[64,2048]{1,0:T(8,128)(2,1)S(1)}, bf16[64,2048]{1,0:T(8,128)(2,1)S(1)}, u32[]{:S(2)}, u32[]{:S(2)}) collective-permute-start(bf16[64,2048]{1,0:T(8,128)(2,1)S(1)} %get-tuple-element.188.refs_0_), channel_id=1, source_target_pairs={{0,2},{2,0},{4,6},{6,4},{1,3},{3,1},{5,7},{7,5},{8,10},{10,8},{12,... | collective-permute-start | bytes 786440 | tf_op jit(solution)/shard_map/ppermute | solution.py:948
  237.2 23.8 %collective-permute-start.37 = (bf16[256,2048]{1,0:T(8,128)(2,1)}, bf16[256,2048]{1,0:T(8,128)(2,1)}, u32[]{:S(2)}, u32[]{:S(2)}) collective-permute-start(bf16[256,2048]{1,0:T(8,128)(2,1)} %get-tuple-element.192), channel_id=1, source_target_pairs={{0,1},{1,0},{2,3},{3,2},{4,5},{5,4},{6,7},{7,6},{8,9},{9,8},{10,11... | collective-permute-start | bytes 3145736 | tf_op jit(solution)/shard_map/ppermute | solution.py:960
  242.1 10.3 %all-to-all-start.3 = ((f32[8,8,512]{2,1,0:T(8,128)}), f32[8,8,512]{2,1,0:T(8,128)S(1)}, u32[]{:S(2)}, u32[]{:S(2)}) async-start(f32[8,8,512]{2,1,0:T(8,128)} %get-tuple-element.198), calls=%async_computation.3 | async-start | bytes 262144 | tf_op jit(solution)/shard_map/all_to_all | solution.py:1010
  253.3 14.7 %all-to-all-start.4 = ((bf16[16,64,128]{2,1,0:T(8,128)(2,1)}), bf16[16,64,128]{2,1,0:T(8,128)(2,1)S(1)}, u32[]{:S(2)}, u32[]{:S(2)}) async-start(bf16[16,64,128]{2,1,0:T(8,128)(2,1)} %head_grad.1), calls=%async_computation.4 | async-start | bytes 524288 | tf_op jit(solution)/shard_map/all_to_all | solution.py:1010
  268.0 17.1 %collective-permute-start.38 = (bf16[64,2048]{1,0:T(8,128)(2,1)}, bf16[64,2048]{1,0:T(8,128)(2,1)S(1)}, u32[]{:S(2)}, u32[]{:S(2)}) collective-permute-start(bf16[64,2048]{1,0:T(8,128)(2,1)} %copy-done.39), channel_id=1, source_target_pairs={{0,2},{2,0},{4,6},{6,4},{1,3},{3,1},{5,7},{7,5},{8,10},{10,8},{12,... | collective-permute-start | bytes 786440 | tf_op jit(solution)/shard_map/ppermute | solution.py:971
  269.4 15.7 %collective-permute-start.39 = (bf16[64,2048]{1,0:T(8,128)(2,1)S(1)}, bf16[64,2048]{1,0:T(8,128)(2,1)S(1)}, u32[]{:S(2)}, u32[]{:S(2)}) collective-permute-start(bf16[64,2048]{1,0:T(8,128)(2,1)S(1)} %get-tuple-element.195), channel_id=1, source_target_pairs={{0,4},{2,6},{4,0},{6,2},{1,5},{3,7},{5,1},{7,3},{8,12},{10,14},{12... | collective-permute-start | bytes 786440 | tf_op jit(solution)/shard_map/ppermute | solution.py:971
  272.0 13.8 %collective-permute-start.40 = (bf16[64,2048]{1,0:T(8,128)(2,1)S(1)}, bf16[64,2048]{1,0:T(8,128)(2,1)S(1)}, u32[]{:S(2)}, u32[]{:S(2)}) collective-permute-start(bf16[64,2048]{1,0:T(8,128)(2,1)S(1)} %get-tuple-element.196), channel_id=1, source_target_pairs={{0,6},{2,4},{4,2},{6,0},{1,7},{3,5},{5,3},{7,1},{8,14},{10,12},{12... | collective-permute-start | bytes 786440 | tf_op jit(solution)/shard_map/ppermute | solution.py:971
  328.4 13.8 %collective-permute-start.45 = (bf16[272,1024]{1,0:T(8,128)(2,1)}, bf16[272,1024]{1,0:T(8,128)(2,1)}, u32[]{:S(2)}, u32[]{:S(2)}) collective-permute-start(bf16[272,1024]{1,0:T(8,128)(2,1)} %get-tuple-element.217), channel_id=1, source_target_pairs={{0,8},{8,16},{16,24},{24,0},{1,9},{9,17},{17,25},{25,1},{2,10},{10... | collective-permute-start | bytes 1671176 | tf_op jit(solution)/shard_map/ppermute | solution.py:1004
  328.4 13.8 %collective-permute-start.46 = (bf16[272,1024]{1,0:T(8,128)(2,1)}, bf16[272,1024]{1,0:T(8,128)(2,1)}, u32[]{:S(2)}, u32[]{:S(2)}) collective-permute-start(bf16[272,1024]{1,0:T(8,128)(2,1)} %get-tuple-element.218), channel_id=1, source_target_pairs={{0,24},{8,0},{16,8},{24,16},{1,25},{9,1},{17,9},{25,17},{2,26},{10... | collective-permute-start | bytes 1671176 | tf_op jit(solution)/shard_map/ppermute | solution.py:1004
  331.1 11.1 %collective-permute-start.47 = (bf16[256,1024]{1,0:T(8,128)(2,1)}, bf16[256,1024]{1,0:T(8,128)(2,1)}, u32[]{:S(2)}, u32[]{:S(2)}) collective-permute-start(bf16[256,1024]{1,0:T(8,128)(2,1)} %get-tuple-element.220), channel_id=1, source_target_pairs={{0,32},{32,64},{64,96},{96,0},{1,33},{33,65},{65,97},{97,1},{2,34}... | collective-permute-start | bytes 1572872 | tf_op jit(solution)/shard_map/ppermute | solution.py:1004
  331.1 11.1 %collective-permute-start.48 = (bf16[256,1024]{1,0:T(8,128)(2,1)}, bf16[256,1024]{1,0:T(8,128)(2,1)}, u32[]{:S(2)}, u32[]{:S(2)}) collective-permute-start(bf16[256,1024]{1,0:T(8,128)(2,1)} %get-tuple-element.221), channel_id=1, source_target_pairs={{0,96},{32,0},{64,32},{96,64},{1,97},{33,1},{65,33},{97,65},{2,98}... | collective-permute-start | bytes 1572872 | tf_op jit(solution)/shard_map/ppermute | solution.py:1004
  342.2 11.0 %collective-permute-start.55 = (bf16[256,2048]{1,0:T(8,128)(2,1)}, bf16[256,2048]{1,0:T(8,128)(2,1)S(1)}, u32[]{:S(2)}, u32[]{:S(2)}) collective-permute-start(bf16[256,2048]{1,0:T(8,128)(2,1)} %copy-done.37), channel_id=1, source_target_pairs={{0,1},{1,0},{2,3},{3,2},{4,5},{5,4},{6,7},{7,6},{8,9},{9,8},{10,11... | collective-permute-start | bytes 3145736 | tf_op jit(solution)/shard_map/ppermute | solution.py:960
  350.0 15.2 %collective-permute-start.49 = (bf16[80,1024]{1,0:T(8,128)(2,1)S(1)}, bf16[80,1024]{1,0:T(8,128)(2,1)S(1)}, u32[]{:S(2)}, u32[]{:S(2)}) collective-permute-start(bf16[80,1024]{1,0:T(8,128)(2,1)S(1)} %get-tuple-element.223), channel_id=1, source_target_pairs={{0,32},{32,64},{64,96},{96,0},{1,33},{33,65},{65,97},{97,1},{2,34}... | collective-permute-start | bytes 491528 | tf_op jit(solution)/shard_map/ppermute | solution.py:990
  350.6 11.6 %collective-permute-start.53 = (bf16[64,1024]{1,0:T(8,128)(2,1)S(1)}, bf16[64,1024]{1,0:T(8,128)(2,1)S(1)}, u32[]{:S(2)}, u32[]{:S(2)}) collective-permute-start(bf16[64,1024]{1,0:T(8,128)(2,1)S(1)} %get-tuple-element.228), channel_id=1, source_target_pairs={{0,16},{8,24},{16,0},{24,8},{1,17},{9,25},{17,1},{25,9},{2,18},{10... | collective-permute-start | bytes 393224 | tf_op jit(solution)/shard_map/ppermute | solution.py:991
  352.0 10.2 %collective-permute-start.54 = (bf16[64,1024]{1,0:T(8,128)(2,1)S(1)}, bf16[64,1024]{1,0:T(8,128)(2,1)S(1)}, u32[]{:S(2)}, u32[]{:S(2)}) collective-permute-start(bf16[64,1024]{1,0:T(8,128)(2,1)S(1)} %get-tuple-element.229), channel_id=1, source_target_pairs={{0,24},{8,0},{16,8},{24,16},{1,25},{9,1},{17,9},{25,17},{2,26},{10... | collective-permute-start | bytes 393224 | tf_op jit(solution)/shard_map/ppermute | solution.py:991
  353.2 11.9 %collective-permute-start.50 = (bf16[80,1024]{1,0:T(8,128)(2,1)S(1)}, bf16[80,1024]{1,0:T(8,128)(2,1)S(1)}, u32[]{:S(2)}, u32[]{:S(2)}) collective-permute-start(bf16[80,1024]{1,0:T(8,128)(2,1)S(1)} %get-tuple-element.224), channel_id=1, source_target_pairs={{0,64},{32,96},{64,0},{96,32},{1,65},{33,97},{65,1},{97,33},{2,66}... | collective-permute-start | bytes 491528 | tf_op jit(solution)/shard_map/ppermute | solution.py:990
  359.4 19.9 %collective-permute-start.59 = (bf16[64,2048]{1,0:T(8,128)(2,1)}, bf16[64,2048]{1,0:T(8,128)(2,1)S(1)}, u32[]{:S(2)}, u32[]{:S(2)}) collective-permute-start(bf16[64,2048]{1,0:T(8,128)(2,1)} %get-tuple-element.248), channel_id=1, source_target_pairs={{0,6},{2,4},{4,2},{6,0},{1,7},{3,5},{5,3},{7,1},{8,14},{10,12},{12... | collective-permute-start | bytes 786440 | tf_op jit(solution)/shard_map/ppermute | solution.py:971
  362.2 17.1 %collective-permute-start.57 = (bf16[64,2048]{1,0:T(8,128)(2,1)}, bf16[64,2048]{1,0:T(8,128)(2,1)}, u32[]{:S(2)}, u32[]{:S(2)}) collective-permute-start(bf16[64,2048]{1,0:T(8,128)(2,1)} %get-tuple-element.243), channel_id=1, source_target_pairs={{0,4},{4,0},{1,5},{5,1},{2,6},{6,2},{3,7},{7,3},{8,12},{12,8},{9,1... | collective-permute-start | bytes 786440 | tf_op jit(solution)/shard_map/ppermute | solution.py:1270
  362.2 17.1 %collective-permute-start.58 = (bf16[64,2048]{1,0:T(8,128)(2,1)}, bf16[64,2048]{1,0:T(8,128)(2,1)S(1)}, u32[]{:S(2)}, u32[]{:S(2)}) collective-permute-start(bf16[64,2048]{1,0:T(8,128)(2,1)} %get-tuple-element.245), channel_id=1, source_target_pairs={{0,4},{2,6},{4,0},{6,2},{1,5},{3,7},{5,1},{7,3},{8,12},{10,14},{12... | collective-permute-start | bytes 786440 | tf_op jit(solution)/shard_map/ppermute | solution.py:971
  365.2 14.4 %collective-permute-start.56 = (bf16[64,2048]{1,0:T(8,128)(2,1)}, bf16[64,2048]{1,0:T(8,128)(2,1)S(1)}, u32[]{:S(2)}, u32[]{:S(2)}) collective-permute-start(bf16[64,2048]{1,0:T(8,128)(2,1)} %get-tuple-element.241), channel_id=1, source_target_pairs={{0,2},{2,0},{4,6},{6,4},{1,3},{3,1},{5,7},{7,5},{8,10},{10,8},{12,... | collective-permute-start | bytes 786440 | tf_op jit(solution)/shard_map/ppermute | solution.py:971
  372.2 14.6 %all-to-all-start.6 = ((bf16[8,8,2048]{2,1,0:T(8,128)(2,1)}), bf16[8,8,2048]{2,1,0:T(8,128)(2,1)S(1)}, u32[]{:S(2)}, u32[]{:S(2)}) async-start(bf16[8,8,2048]{2,1,0:T(8,128)(2,1)} %get-tuple-element.234), calls=%async_computation.7 | async-start | bytes 524288 | tf_op jit(solution)/shard_map/all_to_all | solution.py:1010
  380.1 26.0 %collective-permute-start.61 = (bf16[4,16,2048]{2,1,0:T(8,128)(2,1)S(1)}, bf16[4,16,2048]{2,1,0:T(8,128)(2,1)S(1)}, u32[]{:S(2)}, u32[]{:S(2)}) collective-permute-start(bf16[4,16,2048]{2,1,0:T(8,128)(2,1)S(1)} %bitcast.72), channel_id=1, source_target_pairs={{0,2},{2,0},{1,3},{3,1},{4,6},{6,4},{5,7},{7,5},{8,10},{10,8},{9,1... | collective-permute-start | bytes 786440 | tf_op jit(solution)/shard_map/ppermute | solution.py:1300
  380.7 27.2 %collective-permute-start.60 = (bf16[4,16,2048]{2,1,0:T(8,128)(2,1)S(1)}, bf16[4,16,2048]{2,1,0:T(8,128)(2,1)S(1)}, u32[]{:S(2)}, u32[]{:S(2)}) collective-permute-start(bf16[4,16,2048]{2,1,0:T(8,128)(2,1)S(1)} %bitcast.73), channel_id=1, source_target_pairs={{0,1},{1,0},{2,3},{3,2},{4,5},{5,4},{6,7},{7,6},{8,9},{9,8},{10,11... | collective-permute-start | bytes 786440 | tf_op jit(solution)/shard_map/ppermute | solution.py:1301
  383.7 11.2 %collective-permute-start.63 = (bf16[80,1024]{1,0:T(8,128)(2,1)S(1)}, bf16[80,1024]{1,0:T(8,128)(2,1)S(1)}, u32[]{:S(2)}, u32[]{:S(2)}) collective-permute-start(bf16[80,1024]{1,0:T(8,128)(2,1)S(1)} %copy-done.41), channel_id=1, source_target_pairs={{0,4},{4,0},{1,5},{5,1},{2,6},{6,2},{3,7},{7,3},{8,12},{12,8},{9,1... | collective-permute-start | bytes 491528 | tf_op jit(solution)/shard_map/ppermute | solution.py:1320
  387.4 11.7 %all-to-all-start.7 = ((f32[16,8,128]{2,1,0:T(8,128)}), f32[16,8,128]{2,1,0:T(8,128)S(1)}, u32[]{:S(2)}, u32[]{:S(2)}) async-start(f32[16,8,128]{2,1,0:T(8,128)} %get-tuple-element.252), calls=%async_computation.8 | async-start | bytes 131072 | tf_op jit(solution)/shard_map/all_to_all | solution.py:1010
  (96 other events, 1081.7 us)
Sparse Core Ops, SparseCore 0:
  17.1 54.9 all-gather.2
  74.8 79.0 all-gather.4
  217.2 89.4 reduce-scatter.1

commit v2 on v1

--- a/solution.py
+++ b/solution.py
@@ -472,7 +472,7 @@
 
 def up_kernel(ids, *refs):
     parts, refs = refs[:8], refs[8:]
-    w_ref, dhn_ref, gain_ref, o_ref, bb_ref, h_ref, slope_ref, sums_ref = refs
+    w_ref, dhn_ref, gain_ref, o_ref, bb_ref, h_ref, u_ref, sums_ref = refs
     place_parts(parts, bb_ref, ids[0])
     tokens, units = h_ref.shape
     step = 256
@@ -483,9 +483,7 @@
         cdf = 0.5 * (1.0 + lax.erf(u * (1.0 / math.sqrt(2.0))))
         h = u * cdf
         h_ref[:, at] = h
-        slope_ref[:, at] = cdf + u * (
-            jnp.exp(-0.5 * u * u) * (1.0 / math.sqrt(2.0 * math.pi))
-        )
+        u_ref[:, at] = u
         scaled = dhn_ref[:, at] * gain_ref[:, at]
         terms = (h, h * h, scaled, scaled * h)
         return tuple(c + jnp.sum(t, axis=1, keepdims=True) for c, t in zip(carry, terms))
@@ -502,34 +500,61 @@
         sums_ref[k] = line
 
 
-def inner_back_kernel(
-    ids, h_ref, slope_ref, dhn_ref, sums_ref, gain_ref, shift_ref, w_ref,
-    keep_ref, send_ref, hn_ref, du_ref, sub_ref, l_s,
-):
+def slope_kernel(h_ref, u_ref, dhn_ref, gain_ref, first_ref, slope_ref, last_ref):
+    def body(i, _):
+        at = pl.ds(pl.multiple_of(i * 256, 256), 256)
+        u = u_ref[:, at]
+        slope = 0.5 * (1.0 + lax.erf(u * (1.0 / math.sqrt(2.0)))) + u * (
+            jnp.exp(-0.5 * u * u) * (1.0 / math.sqrt(2.0 * math.pi))
+        )
+        first_ref[:, at] = dhn_ref[:, at] * gain_ref[:, at] * slope
+        slope_ref[:, at] = slope
+        last_ref[:, at] = h_ref[:, at] * slope
+        return 0
+
+    lax.fori_loop(0, u_ref.shape[1] // 256, body, 0)
+
+
+def inner_columns(sums_ref):
     sums, center, inverse = inner_moments(sums_ref, FF)
     mean_scaled = sums[2:3] / FF
     mean_both = inverse * (sums[3:4] / FF - center * mean_scaled)
-    rows = jnp.concatenate([center, inverse, mean_scaled, mean_both, sums[4:8]], axis=0)
+    by_slope = inverse * (inverse * mean_both * center - mean_scaled)
+    by_last = inverse * inverse * mean_both
+    rows = jnp.concatenate([center, inverse, by_slope, by_last, sums[4:8]], axis=0)
     columns = jnp.transpose(jnp.concatenate([rows] * 16, axis=0))
-    tokens = h_ref.shape[0]
-    center, inverse, mean_scaled, mean_both = (columns[:, n : n + 1] for n in range(4))
-    units = h_ref.shape[1]
+    return tuple(columns[:, n : n + 1] for n in range(4))
+
+
+def inner_back_kernel(
+    ids, first_ref, slope_ref, last_ref, sums_ref, w_ref, keep_ref, send_ref, du_ref, l_s
+):
+    _, inverse, by_slope, by_last = inner_columns(sums_ref)
+
+    def body(i, _):
+        at = pl.ds(pl.multiple_of(i * 256, 256), 256)
+        du = inverse * first_ref[:, at] + by_slope * slope_ref[:, at] - by_last * last_ref[:, at]
+        du_ref[:, at] = du.astype(BF16)
+        return 0
+
+    lax.fori_loop(0, du_ref.shape[1] // 256, body, 0)
+    take_for_scatter(du_ref, l_s, ids[0])
+    scatter_product(l_s, w_ref, keep_ref, send_ref)
+
+
+def inner_norm_kernel(h_ref, dhn_ref, sums_ref, gain_ref, shift_ref, hn_ref, sub_ref):
+    center, inverse, _, _ = inner_columns(sums_ref)
 
     def body(i, _):
         at = pl.ds(pl.multiple_of(i * 256, 256), 256)
         hat = (h_ref[:, at] - center) * inverse
         dhn = dhn_ref[:, at]
-        gain = gain_ref[:, at]
-        hn_ref[:, at] = (hat * gain + shift_ref[:, at]).astype(BF16)
-        du = inverse * (dhn * gain - mean_scaled - hat * mean_both) * slope_ref[:, at]
-        du_ref[:, at] = du.astype(BF16)
+        hn_ref[:, at] = (hat * gain_ref[:, at] + shift_ref[:, at]).astype(BF16)
         sub_ref[0:1, at] = jnp.sum(dhn * hat, axis=0, keepdims=True)
         sub_ref[1:2, at] = jnp.sum(dhn, axis=0, keepdims=True)
         return 0
 
-    lax.fori_loop(0, units // 256, body, 0)
-    take_for_scatter(du_ref, l_s, ids[0])
-    scatter_product(l_s, w_ref, keep_ref, send_ref)
+    lax.fori_loop(0, h_ref.shape[1] // 256, body, 0)
 
 
 def down_kernel(ids, hn_ref, w_ref, keep_ref, send_ref, l_s):
@@ -1168,7 +1193,7 @@
         far=(0,),
     )
     bb_parts = eight_parts(bb_own, dhn)
-    bb, h, slope, sums_h = local_call(
+    bb, h, u, sums_h = local_call(
         up_kernel,
         "up",
         [shape((tokens, width), BF16), shape((tokens, units)), shape((tokens, units)), stat],
@@ -1179,19 +1204,31 @@
         far=(0,),
     )
     sums_h = each_to_all(sums_h, EIGHT)
-    keep, send, hn, du, sub_h = local_call(
+    table = shape((tokens, units))
+    terms = local_call(slope_kernel, "slopes", [table] * 3, [h, u, dhn, gain_h], moved=12 * MIB)
+    keep, send, du = local_call(
         inner_back_kernel,
         "inner_back",
-        pieces + [shape((tokens, units), BF16)] * 2 + [shape((2, units))],
-        [ids, h, slope, dhn, sums_h, gain_h, shift_h, w_up],
+        pieces + [shape((tokens, units), BF16)],
+        [ids, *terms, sums_h, w_up],
         [pltpu.VMEM((tokens, units), BF16)],
         flops=2 * tokens * width * units,
         moved=14 * MIB,
-        far=(2, 3),
-    )
-    scattered, (g_mlp,) = finish_scatter(
-        keep, send, lambda own: [mlp_grad(df, hn, bb, after(du, own))]
-    )
+        far=(2,),
+    )
+
+    def feed_forward_grad(own):
+        hn, sub_h = local_call(
+            inner_norm_kernel,
+            "inner_norm",
+            [shape((tokens, units), BF16), shape((2, units))],
+            [after(h, own), dhn, sums_h, gain_h, shift_h],
+            moved=5 * MIB,
+            far=(0,),
+        )
+        return [mlp_grad(df, hn, bb, after(du, own)), hn, sub_h]
+
+    scattered, (g_mlp, hn, sub_h) = finish_scatter(keep, send, feed_forward_grad)
     g_mlp = lax.psum_scatter(after(g_mlp, *scattered), ZX, scatter_dimension=0, tiled=True)
     dr1, dattn_own, pre_three = local_call(
         middle_back_kernel,

time: 426 us -> 444 us (1.042)
  local copies, waits for them, and re-layouts: 31.1 us -> 56.5 us
  blocking collectives: 28.6 us -> 18.5 us
  Pallas kernels: 108 us -> 113 us
  waiting for transfers between devices: 94.8 us -> 90 us
    unnamed x147 -> x201, local copies, waits for them, and re-layouts: 23.9 us -> 47.2 us
    all_to_all x2 -> x1, blocking collectives: 28.6 us -> 18.5 us  [each_to_all(): return lax.all_to_all(copies, axis, split_axis=0, concat_axis=0, tiled=True)]
    all_to_all x6 -> x7, starting transfers between devices: 27.4 us -> 31.8 us  [each_to_all(): return lax.all_to_all(copies, axis, split_axis=0, concat_axis=0, tiled=True)]
    pallas_call x26 -> x28, Pallas kernels: 73.5 us -> 75.9 us  [local_call(): pl.pallas_call(kernel, out_shape=tuple((in_hbm(o) if n in far else o for...]
    all_to_all x6 -> x7, waiting for transfers between devices: 22.1 us -> 20 us  [each_to_all(): return lax.all_to_all(copies, axis, split_axis=0, concat_axis=0, tiled=True)]
  transfers between devices with their start and end apart: 73 -> 74, of which waited for: 38 -> 33; matrix products, arithmetic and copies ran while one was open for 2% -> 3% of each run, Pallas kernels for 22% -> 23%
where the time goes in v2:
time: 444 us; the launch traced here: 436 us
  starting transfers between devices  137 us (31%)
  Pallas kernels  113 us (25%)
  waiting for transfers between devices  90 us (20%)
  local copies, waits for them, and re-layouts  56.5 us (13%)
  blocking collectives  18.5 us (4%)
  between operations  15.1 us (3%)
  other arithmetic  5.79 us (1%)
    pallas_call x28, Pallas kernels, local_call(): pl.pallas_call(kernel, out_shape=tuple((in_hbm(o) if n in far else o for...  75.9 us
    unnamed x201, local copies, waits for them, and re-layouts  47.2 us
    all_to_all x7, starting transfers between devices, each_to_all(): return lax.all_to_all(copies, axis, split_axis=0, concat_axis=0, tiled=True)  31.8 us
    all_to_all x7, waiting for transfers between devices, each_to_all(): return lax.all_to_all(copies, axis, split_axis=0, concat_axis=0, tiled=True)  20 us
    all_to_all x1, blocking collectives, each_to_all(): return lax.all_to_all(copies, axis, split_axis=0, concat_axis=0, tiled=True)  18.5 us
    ppermute x12, starting transfers between devices, eight_parts(): parts += [line, lax.ppermute(line, C, SWAP)]  18.2 us
    ppermute x12, starting transfers between devices, line_scatter(): lax.ppermute(s, YY, xor_pairs(4, k))  15.9 us
    ppermute x12, waiting for transfers between devices, line_scatter(): lax.ppermute(s, YY, xor_pairs(4, k))  15.6 us
  transfers between devices with their start and end apart: 74, of which 33 were waited for; matrix products, arithmetic and copies ran while one was open for 3% of the time, Pallas kernels for 23%

profile of v2, /device:TPU:1, one launch (start us, length us, event | category | flops | bytes accessed | tf_op | source)
XLA Modules:
  0.0 435.8 jit_solution(5246486673530363349)
XLA Ops:
  9.4 3.8 collective-permute-start.9
  13.2 2.9 collective-permute-done.9
  17.4 3.0 collective-permute-start.20
  20.5 4.8 %collective-permute-done.20 = bf16[64,2048]{1,0:T(8,128)(2,1)S(1)} collective-permute-done((bf16[64,2048]{1,0:T(8,128)(2,1)S(1)}, bf16[64,2048]{1,0:T(8,128)(2,1)S(1)}, u32[]{:S(2)}, u32[]{:S(2)}) %collective-permute-start.20) | collective-permute-done | bytes 262176 | tf_op jit(solution)/shard_map/ppermute | solution.py:1082
  26.3 2.8 collective-permute-start
  29.7 8.9 %collective-permute-done.near_ref = bf16[4,32,2048]{2,1,0:T(8,128)(2,1)S(1)} collective-permute-done((bf16[4,32,2048]{2,1,0:T(8,128)(2,1)S(1)}, bf16[4,32,2048]{2,1,0:T(8,128)(2,1)S(1)}, u32[]{:S(2)}, u32[]{:S(2)}) %collective-permute-start) | collective-permute-done | bytes 524320 | tf_op jit(solution)/shard_map/ppermute | solution.py:1113
  38.7 3.7 collective-permute-start.5
  42.5 4.2 collective-permute-start.1
  46.6 3.5 collective-permute-start.4
  50.7 4.7 %collective-permute-start.6 = (bf16[64,2048]{1,0:T(8,128)(2,1)S(1)}, bf16[64,2048]{1,0:T(8,128)(2,1)}, u32[]{:S(2)}, u32[]{:S(2)}) collective-permute-start(bf16[64,2048]{1,0:T(8,128)(2,1)S(1)} %collective-permute-done.5.refs_4_), channel_id=1, source_target_pairs={{0,1},{1,0},{2,3},{3,2},{4,5},{5,4},{6,7},{7,6},{8,9},{9,8},{10,11... | collective-permute-start | bytes 786440 | tf_op jit(solution)/shard_map/ppermute | solution.py:979
  59.6 12.5 %all-gather.3.cloned.1.call-done.w_ref = bf16[2048,1024]{1,0:T(8,128)(2,1)} async-done(((bf16[128,1024]{1,0:T(8,128)(2,1)}), bf16[2048,1024]{1,0:T(8,128)(2,1)}) %all-gather.3.cloned.1.call-update) | async-done | bytes 4194320 | tf_op jit(solution)/shard_map/all_gather | solution.py:1094
  74.2 4.6 %project.1 = (bf16[16,3,64,128]{3,2,1,0:T(8,128)(2,1)}, bf16[512,2048]{1,0:T(8,128)(2,1)}) custom-call(s32[4]{0:T(128)S(1)} %pad_add_fusion.ids, bf16[4,64,2048]{2,1,0:T(8,128)(2,1)S(1)} %copy-done.11, bf16[4,32,2048]{2,1,0:T(8,128)(2,1)S(1)} %collective-permute-done.near_ref, bf16[4,32,2048]{2,1,0:T(8,128)(2,1)S(1)} %collective-permute-done.1.far_ref, ...), custom_call_target="tpu_custom_call" | custom-call | flops 1610612736 | bytes 8388608 | tf_op jit(solution)/shard_map/project/pallas_call | solution.py:68
  78.8 5.0 %all-to-all-start = ((bf16[16,3,64,128]{3,2,1,0:T(8,128)(2,1)}), bf16[16,3,64,128]{3,2,1,0:T(8,128)(2,1)}, u32[]{:S(2)}, u32[]{:S(2)}) async-start(bf16[16,3,64,128]{3,2,1,0:T(8,128)(2,1)} %get-tuple-element.154), calls=%async_computation | async-start | bytes 1572864 | tf_op jit(solution)/shard_map/all_to_all | solution.py:1035
  88.9 2.8 collective-permute-start.11
  96.9 5.6 %all-to-all-done.qkv_ref = bf16[16,3,64,128]{3,2,1,0:T(8,128)(2,1)} async-done(((bf16[16,3,64,128]{3,2,1,0:T(8,128)(2,1)}), bf16[16,3,64,128]{3,2,1,0:T(8,128)(2,1)}, u32[]{:S(2)}, u32[]{:S(2)}) %all-to-all-start) | async-done | bytes 786464 | tf_op jit(solution)/shard_map/all_to_all | solution.py:1035
  102.5 6.9 %attend.1 = (f32[16,64,128]{2,1,0:T(8,128)}, bf16[16,64,128]{2,1,0:T(8,128)(2,1)}, f32[1,2048]{1,0:T(1,128)S(1)}) custom-call(bf16[16,3,64,128]{3,2,1,0:T(8,128)(2,1)} %all-to-all-done.qkv_ref, s32[1,2048]{1,0:T(1,128)S(1)} %bitcast.79), custom_call_target="tpu_custom_call" | custom-call | flops 2000000000 | bytes 4000000 | tf_op jit(solution)/shard_map/attend/pallas_call | solution.py:200
  109.4 3.5 all-to-all-start.1
  113.1 8.1 %all-to-all-done.1.o_ref.refs_9_.refs_0_.refs_1_ = bf16[16,64,128]{2,1,0:T(8,128)(2,1)S(1)} async-done(((bf16[16,64,128]{2,1,0:T(8,128)(2,1)}), bf16[16,64,128]{2,1,0:T(8,128)(2,1)S(1)}, u32[]{:S(2)}, u32[]{:S(2)}) %all-to-all-start.1) | async-done | bytes 262176 | tf_op jit(solution)/shard_map/all_to_all | solution.py:1035
  121.2 3.2 out.1
  124.4 6.9 %collective-permute-start.14 = (bf16[256,2176]{1,0:T(8,128)(2,1)S(1)}, bf16[256,2176]{1,0:T(8,128)(2,1)S(1)}, u32[]{:S(2)}, u32[]{:S(2)}) collective-permute-start(bf16[256,2176]{1,0:T(8,128)(2,1)S(1)} %get-tuple-element.160), channel_id=1, source_target_pairs={{0,1},{1,0},{2,3},{3,2},{4,5},{5,4},{6,7},{7,6},{8,9},{9,8},{10,11... | collective-permute-start | bytes 3342344 | tf_op jit(solution)/shard_map/ppermute | solution.py:985
  139.1 4.2 collective-permute-done.15.one
  143.3 8.2 %collective-permute-done.16.two = bf16[64,2176]{1,0:T(8,128)(2,1)} collective-permute-done((bf16[64,2176]{1,0:T(8,128)(2,1)}, bf16[64,2176]{1,0:T(8,128)(2,1)}, u32[]{:S(2)}, u32[]{:S(2)}) %collective-permute-start.16) | collective-permute-done | bytes 278560 | tf_op jit(solution)/shard_map/ppermute | solution.py:996
  154.3 2.7 middle.1
  157.3 3.0 collective-permute-start.19
  160.3 2.7 collective-permute-start.18
  163.0 3.9 fusion.5
  167.0 6.8 %down_back.1 = (bf16[512,2048]{1,0:T(8,128)(2,1)}, f32[512,1024]{1,0:T(8,128)S(1)}) custom-call(s32[4]{0:T(128)S(1)} %pad_add_fusion.ids, bf16[64,2048]{1,0:T(8,128)(2,1)} %copy-done.83, bf16[64,2048]{1,0:T(8,128)(2,1)} %collective-permute-done.2.refs_1_, bf16[64,2048]{1,0:T(8,128)(2,1)} %copy-done.96, bf16[64,2048]{1,0:T(8,128)(2,1)} %collective-permute-done.4.refs_3_, ...), custom_call_target="tpu_custom_call" | custom-call | flops 2147483648 | bytes 10485760 | tf_op jit(solution)/shard_map/down_back/pallas_call | solution.py:68
  179.0 6.1 %up.1 = (bf16[512,2048]{1,0:T(8,128)(2,1)}, f32[512,1024]{1,0:T(8,128)S(1)}, f32[512,1024]{1,0:T(8,128)S(1)}, f32[8,8,512]{2,1,0:T(8,128)S(1)}) custom-call(s32[4]{0:T(128)S(1)} %pad_add_fusion.ids, bf16[64,2048]{1,0:T(8,128)(2,1)} %get-tuple-element.165.refs_0_, bf16[64,2048]{1,0:T(8,128)(2,1)} %collective-permute-done.18.refs_1_, ...), custom_call_target="tpu_custom_call" | custom-call | flops 2147483648 | bytes 14680064 | tf_op jit(solution)/shard_map/up/pallas_call | solution.py:68
  188.6 3.4 all-to-all-start.2
  207.5 6.6 %inner_back.1 = (f32[256,2048]{1,0:T(8,128)S(1)}, bf16[256,2048]{1,0:T(8,128)(2,1)S(1)}, bf16[512,1024]{1,0:T(8,128)(2,1)}) custom-call(s32[4]{0:T(128)S(1)} %pad_add_fusion.ids, f32[512,1024]{1,0:T(8,128)S(1)} %copy-done.23, f32[512,1024]{1,0:T(8,128)S(1)} %copy-done.25, f32[512,1024]{1,0:T(8,128)S(1)} %copy-done.27, ...), custom_call_target="tpu_custom_call" | custom-call | flops 2147483648 | bytes 14680064 | tf_op jit(solution)/shard_map/inner_back/pallas_call | solution.py:68
  225.2 8.1 %mlp_grad.1 = bf16[2048,2048]{1,0:T(8,128)(2,1)} custom-call(bf16[512,2048]{1,0:T(8,128)(2,1)S(1)} %copy-done.71, bf16[512,1024]{1,0:T(8,128)(2,1)S(1)} %copy-done.65, bf16[512,2048]{1,0:T(8,128)(2,1)S(1)} %copy-done.63, bf16[512,1024]{1,0:T(8,128)(2,1)S(1)} %copy-done.67), custom_call_target="tpu_custom_call" | custom-call | flops 4294967296 | bytes 14680064 | tf_op jit(solution)/shard_map/mlp_grad/pallas_call | solution.py:577
  243.3 5.4 %down.1 = (f32[256,2048]{1,0:T(8,128)S(1)}, bf16[256,2048]{1,0:T(8,128)(2,1)}) custom-call(s32[4]{0:T(128)S(1)} %pad_add_fusion.ids, bf16[512,1024]{1,0:T(8,128)(2,1)S(1)} %copy-done.66, bf16[2048,1024]{1,0:T(8,128)(2,1)S(1)} %copy-done.9), custom_call_target="tpu_custom_call" | custom-call | flops 2147483648 | bytes 8388608 | tf_op jit(solution)/shard_map/down/pallas_call | solution.py:68
  256.0 4.1 out_back.1
  261.6 4.9 %all-to-all-start.3 = ((f32[8,8,512]{2,1,0:T(8,128)}), f32[8,8,512]{2,1,0:T(8,128)S(1)}, u32[]{:S(2)}, u32[]{:S(2)}) async-start(f32[8,8,512]{2,1,0:T(8,128)} %copy-done.51), calls=%async_computation.3 | async-start | bytes 262144 | tf_op jit(solution)/shard_map/all_to_all | solution.py:1035
  274.9 3.7 all-to-all-start.4
  294.2 12.8 %attend_back.1 = bf16[16,3,64,128]{3,2,1,0:T(8,128)(2,1)} custom-call(bf16[16,3,64,128]{3,2,1,0:T(8,128)(2,1)} %all-to-all-done.qkv_ref, bf16[16,64,128]{2,1,0:T(8,128)(2,1)S(1)} %all-to-all-done.4.do_ref, f32[16,64,128]{2,1,0:T(8,128)S(1)} %copy-done.72, f32[1,2048]{1,0:T(1,128)S(1)} %copy-done.74, s32[1,2048]{1,0:T(1,128)S(1)} %bitcast.80, ...), custom_call_target="tpu_custom_call" | custom-call | flops 6000000000 | bytes 6000000 | tf_op jit(solution)/shard_map/attend_back/pallas_call | solution.py:226
  307.1 18.5 %all_to_all.40.dqkv_ref = bf16[16,3,64,128]{3,2,1,0:T(8,128)(2,1)S(1)} all-to-all(bf16[16,3,64,128]{3,2,1,0:T(8,128)(2,1)} %attend_back.1), channel_id=1, replica_groups=mesh['seq_0'=4,'seq_1'=4,'seq_2'=2,'ffn_0'=2,'ffn_1'=2] {'seq_0','seq_1'}, dimensions={0} | all-to-all | bytes 1572864 | tf_op jit(solution)/shard_map/all_to_all | solution.py:1035
  325.7 6.3 %in_grad.1 = (bf16[272,1024]{1,0:T(8,128)(2,1)}, bf16[272,1024]{1,0:T(8,128)(2,1)}, bf16[144,1024]{1,0:T(8,128)(2,1)}, bf16[128,1024]{1,0:T(8,128)(2,1)}, bf16[2...) custom-call(s32[4]{0:T(128)S(1)} %pad_add_fusion.ids, ...), custom_call_target="tpu_custom_call" | custom-call | flops 1610612736 | bytes 13631488 | tf_op jit(solution)/shard_map/in_grad/pallas_call | solution.py:68
  338.6 3.1 collective-permute-done.43.refs_6_
  347.3 2.7 collective-permute-start.46
  352.6 3.9 in_back.1
  360.6 5.3 %collective-permute-start.55 = (bf16[256,2048]{1,0:T(8,128)(2,1)}, bf16[256,2048]{1,0:T(8,128)(2,1)S(1)}, u32[]{:S(2)}, u32[]{:S(2)}) collective-permute-start(bf16[256,2048]{1,0:T(8,128)(2,1)} %copy-done.64), channel_id=1, source_target_pairs={{0,1},{1,0},{2,3},{3,2},{4,5},{5,4},{6,7},{7,6},{8,9},{9,8},{10,11... | collective-permute-start | bytes 3145736 | tf_op jit(solution)/shard_map/ppermute | solution.py:985
  371.9 3.3 collective-permute-start.50
  390.0 6.6 %all-to-all-start.6 = ((bf16[8,8,2048]{2,1,0:T(8,128)(2,1)}), bf16[8,8,2048]{2,1,0:T(8,128)(2,1)S(1)}, u32[]{:S(2)}, u32[]{:S(2)}) async-start(bf16[8,8,2048]{2,1,0:T(8,128)(2,1)} %get-tuple-element.242), calls=%async_computation.7 | async-start | bytes 524288 | tf_op jit(solution)/shard_map/all_to_all | solution.py:1035
  400.1 4.0 collective-permute-start.60
  406.3 4.7 %all-to-all-start.7 = ((f32[16,8,128]{2,1,0:T(8,128)}), f32[16,8,128]{2,1,0:T(8,128)S(1)}, u32[]{:S(2)}, u32[]{:S(2)}) async-start(f32[16,8,128]{2,1,0:T(8,128)} %get-tuple-element.260), calls=%async_computation.8 | async-start | bytes 131072 | tf_op jit(solution)/shard_map/all_to_all | solution.py:1035
  413.4 4.1 all-to-all-done.7.norm_part
  418.2 6.4 %adam.1 = (f32[3,64,512]{2,1,0:T(8,128)}, f32[3,64,512]{2,1,0:T(8,128)}, f32[3,64,512]{2,1,0:T(8,128)}, f32[64,512]{1,0:T(8,128)}, f32[64,512]{1,0:T(8,128)}, /*...) custom-call(s32[4]{0:T(128)} %copy-done.55, ...), custom_call_target="tpu_custom_call" | custom-call | bytes 12582912 | tf_op jit(solution)/shard_map/adam/pallas_call | solution.py:953
  (379 shorter events, 163.9 us)
Async XLA Ops:
  7.2 64.8 %all-gather.3.cloned.1.call-start = ((), (), s32[]{:S(2)}) async-start(), calls=%async_computation.9 | async-start | bytes 4456448 | tf_op jit(solution)/shard_map/all_gather | solution.py:1094
  17.0 146.0 %all-gather.5.cloned.1.call-start = ((), (), s32[]{:S(2)}) async-start(), calls=%async_computation.10 | async-start | bytes 8912896 | tf_op jit(solution)/shard_map/all_gather | solution.py:1097
  26.3 12.3 %collective-permute-start = (bf16[4,32,2048]{2,1,0:T(8,128)(2,1)S(1)}, bf16[4,32,2048]{2,1,0:T(8,128)(2,1)S(1)}, u32[]{:S(2)}, u32[]{:S(2)}) collective-permute-start(bf16[4,32,2048]{2,1,0:T(8,128)(2,1)S(1)} %constant_dynamic-slice_fusion.8), channel_id=1, source_target_pairs={{0,6},{2,4},{4,2},{6,0},{1,7},{3,5},{5,3},{7,1},{8,14},{10,12},{12... | collective-permute-start | bytes 1572872 | tf_op jit(solution)/shard_map/ppermute | solution.py:1113
  38.7 12.1 %collective-permute-start.5 = (bf16[64,2048]{1,0:T(8,128)(2,1)S(1)}, bf16[64,2048]{1,0:T(8,128)(2,1)S(1)}, u32[]{:S(2)}, u32[]{:S(2)}) collective-permute-start(bf16[64,2048]{1,0:T(8,128)(2,1)S(1)} %multiply_convert_fusion.refs_0_), channel_id=1, source_target_pairs={{0,4},{2,6},{4,0},{6,2},{1,5},{3,7},{5,1},{7,3},{8,12},{10,14},{12... | collective-permute-start | bytes 786440 | tf_op jit(solution)/shard_map/ppermute | solution.py:973
  42.4 13.4 %collective-permute-start.7 = (bf16[64,2048]{1,0:T(8,128)(2,1)S(1)}, bf16[64,2048]{1,0:T(8,128)(2,1)}, u32[]{:S(2)}, u32[]{:S(2)}) collective-permute-start(bf16[64,2048]{1,0:T(8,128)(2,1)S(1)} %multiply_convert_fusion.refs_0_), channel_id=1, source_target_pairs={{0,6},{2,4},{4,2},{6,0},{1,7},{3,5},{5,3},{7,1},{8,14},{10,12},{12... | collective-permute-start | bytes 786440 | tf_op jit(solution)/shard_map/ppermute | solution.py:973
  42.5 17.1 %collective-permute-start.1 = (bf16[4,32,2048]{2,1,0:T(8,128)(2,1)S(1)}, bf16[4,32,2048]{2,1,0:T(8,128)(2,1)S(1)}, u32[]{:S(2)}, u32[]{:S(2)}) collective-permute-start(bf16[4,32,2048]{2,1,0:T(8,128)(2,1)S(1)} %collective-permute-done.near_ref), channel_id=1, source_target_pairs={{0,1},{1,0},{2,3},{3,2},{4,5},{5,4},{6,7},{7,6},{8,9},{9,8},{10,11... | collective-permute-start | bytes 1572872 | tf_op jit(solution)/shard_map/ppermute | solution.py:1114
  46.6 12.4 %collective-permute-start.2 = (bf16[64,2048]{1,0:T(8,128)(2,1)S(1)}, bf16[64,2048]{1,0:T(8,128)(2,1)}, u32[]{:S(2)}, u32[]{:S(2)}) collective-permute-start(bf16[64,2048]{1,0:T(8,128)(2,1)S(1)} %multiply_convert_fusion.refs_0_), channel_id=1, source_target_pairs={{0,1},{1,0},{2,3},{3,2},{4,5},{5,4},{6,7},{7,6},{8,9},{9,8},{10,11... | collective-permute-start | bytes 786440 | tf_op jit(solution)/shard_map/ppermute | solution.py:979
  46.6 12.3 %collective-permute-start.4 = (bf16[64,2048]{1,0:T(8,128)(2,1)S(1)}, bf16[64,2048]{1,0:T(8,128)(2,1)}, u32[]{:S(2)}, u32[]{:S(2)}) collective-permute-start(bf16[64,2048]{1,0:T(8,128)(2,1)S(1)} %collective-permute-done.3.refs_2_), channel_id=1, source_target_pairs={{0,1},{1,0},{2,3},{3,2},{4,5},{5,4},{6,7},{7,6},{8,9},{9,8},{10,11... | collective-permute-start | bytes 786440 | tf_op jit(solution)/shard_map/ppermute | solution.py:979
  78.8 23.6 %all-to-all-start = ((bf16[16,3,64,128]{3,2,1,0:T(8,128)(2,1)}), bf16[16,3,64,128]{3,2,1,0:T(8,128)(2,1)}, u32[]{:S(2)}, u32[]{:S(2)}) async-start(bf16[16,3,64,128]{3,2,1,0:T(8,128)(2,1)} %get-tuple-element.154), calls=%async_computation | async-start | bytes 1572864 | tf_op jit(solution)/shard_map/all_to_all | solution.py:1035
  109.4 11.8 %all-to-all-start.1 = ((bf16[16,64,128]{2,1,0:T(8,128)(2,1)}), bf16[16,64,128]{2,1,0:T(8,128)(2,1)S(1)}, u32[]{:S(2)}, u32[]{:S(2)}) async-start(bf16[16,64,128]{2,1,0:T(8,128)(2,1)} %get-tuple-element.158), calls=%async_computation.1 | async-start | bytes 524288 | tf_op jit(solution)/shard_map/all_to_all | solution.py:1035
  136.3 15.2 %collective-permute-start.16 = (bf16[64,2176]{1,0:T(8,128)(2,1)}, bf16[64,2176]{1,0:T(8,128)(2,1)}, u32[]{:S(2)}, u32[]{:S(2)}) collective-permute-start(bf16[64,2176]{1,0:T(8,128)(2,1)} %get-tuple-element.163), channel_id=1, source_target_pairs={{0,4},{2,6},{4,0},{6,2},{1,5},{3,7},{5,1},{7,3},{8,12},{10,14},{12... | collective-permute-start | bytes 835592 | tf_op jit(solution)/shard_map/ppermute | solution.py:996
  138.8 14.7 %collective-permute-start.17 = (bf16[64,2176]{1,0:T(8,128)(2,1)}, bf16[64,2176]{1,0:T(8,128)(2,1)}, u32[]{:S(2)}, u32[]{:S(2)}) collective-permute-start(bf16[64,2176]{1,0:T(8,128)(2,1)} %get-tuple-element.164), channel_id=1, source_target_pairs={{0,6},{2,4},{4,2},{6,0},{1,7},{3,5},{5,3},{7,1},{8,14},{10,12},{12... | collective-permute-start | bytes 835592 | tf_op jit(solution)/shard_map/ppermute | solution.py:996
  157.0 18.6 %collective-permute-start.24 = (bf16[64,2048]{1,0:T(8,128)(2,1)}, bf16[64,2048]{1,0:T(8,128)(2,1)}, u32[]{:S(2)}, u32[]{:S(2)}) collective-permute-start(bf16[64,2048]{1,0:T(8,128)(2,1)} %get-tuple-element.165.refs_0_), channel_id=1, source_target_pairs={{0,6},{2,4},{4,2},{6,0},{1,7},{3,5},{5,3},{7,1},{8,14},{10,12},{12... | collective-permute-start | bytes 786440 | tf_op jit(solution)/shard_map/ppermute | solution.py:973
  157.3 18.4 %collective-permute-start.22 = (bf16[64,2048]{1,0:T(8,128)(2,1)}, bf16[64,2048]{1,0:T(8,128)(2,1)}, u32[]{:S(2)}, u32[]{:S(2)}) collective-permute-start(bf16[64,2048]{1,0:T(8,128)(2,1)} %get-tuple-element.165.refs_0_), channel_id=1, source_target_pairs={{0,4},{2,6},{4,0},{6,2},{1,5},{3,7},{5,1},{7,3},{8,12},{10,14},{12... | collective-permute-start | bytes 786440 | tf_op jit(solution)/shard_map/ppermute | solution.py:973
  157.3 18.9 %collective-permute-start.19 = (bf16[64,2048]{1,0:T(8,128)(2,1)}, bf16[64,2048]{1,0:T(8,128)(2,1)}, u32[]{:S(2)}, u32[]{:S(2)}) collective-permute-start(bf16[64,2048]{1,0:T(8,128)(2,1)} %get-tuple-element.165.refs_0_), channel_id=1, source_target_pairs={{0,2},{2,0},{4,6},{6,4},{1,3},{3,1},{5,7},{7,5},{8,10},{10,8},{12,... | collective-permute-start | bytes 786440 | tf_op jit(solution)/shard_map/ppermute | solution.py:973
  160.3 17.2 %collective-permute-start.18 = (bf16[64,2048]{1,0:T(8,128)(2,1)}, bf16[64,2048]{1,0:T(8,128)(2,1)}, u32[]{:S(2)}, u32[]{:S(2)}) collective-permute-start(bf16[64,2048]{1,0:T(8,128)(2,1)} %get-tuple-element.165.refs_0_), channel_id=1, source_target_pairs={{0,1},{1,0},{2,3},{3,2},{4,5},{5,4},{6,7},{7,6},{8,9},{9,8},{10,11... | collective-permute-start | bytes 786440 | tf_op jit(solution)/shard_map/ppermute | solution.py:979
  188.6 12.0 %all-to-all-start.2 = ((f32[8,8,512]{2,1,0:T(8,128)}), f32[8,8,512]{2,1,0:T(8,128)S(1)}, u32[]{:S(2)}, u32[]{:S(2)}) async-start(f32[8,8,512]{2,1,0:T(8,128)} %copy-done.52), calls=%async_computation.2 | async-start | bytes 262144 | tf_op jit(solution)/shard_map/all_to_all | solution.py:1035
  192.0 165.5 %reduce-scatter.2.cloned.1.call-start = ((), (), s32[]{:S(2)}) async-start(), calls=%async_computation.11 | async-start | bytes 8912896 | tf_op jit(solution)/shard_map/reduce_scatter | solution.py:1232
  217.8 15.5 %collective-permute-start.29 = (bf16[64,2048]{1,0:T(8,128)(2,1)}, bf16[64,2048]{1,0:T(8,128)(2,1)}, u32[]{:S(2)}, u32[]{:S(2)}) collective-permute-start(bf16[64,2048]{1,0:T(8,128)(2,1)} %get-tuple-element.194), channel_id=1, source_target_pairs={{0,6},{2,4},{4,2},{6,0},{1,7},{3,5},{5,3},{7,1},{8,14},{10,12},{12... | collective-permute-start | bytes 786440 | tf_op jit(solution)/shard_map/ppermute | solution.py:996
  220.4 12.9 %collective-permute-start.28 = (bf16[64,2048]{1,0:T(8,128)(2,1)}, bf16[64,2048]{1,0:T(8,128)(2,1)}, u32[]{:S(2)}, u32[]{:S(2)}) collective-permute-start(bf16[64,2048]{1,0:T(8,128)(2,1)} %get-tuple-element.192), channel_id=1, source_target_pairs={{0,4},{2,6},{4,0},{6,2},{1,5},{3,7},{5,1},{7,3},{8,12},{10,14},{12... | collective-permute-start | bytes 786440 | tf_op jit(solution)/shard_map/ppermute | solution.py:996
  221.0 12.4 %collective-permute-start.27 = (bf16[64,2048]{1,0:T(8,128)(2,1)}, bf16[64,2048]{1,0:T(8,128)(2,1)}, u32[]{:S(2)}, u32[]{:S(2)}) collective-permute-start(bf16[64,2048]{1,0:T(8,128)(2,1)} %get-tuple-element.185), channel_id=1, source_target_pairs={{0,2},{2,0},{4,6},{6,4},{1,3},{3,1},{5,7},{7,5},{8,10},{10,8},{12,... | collective-permute-start | bytes 786440 | tf_op jit(solution)/shard_map/ppermute | solution.py:996
  237.8 13.9 %collective-permute-start.35 = (bf16[64,2048]{1,0:T(8,128)(2,1)S(1)}, bf16[64,2048]{1,0:T(8,128)(2,1)S(1)}, u32[]{:S(2)}, u32[]{:S(2)}) collective-permute-start(bf16[64,2048]{1,0:T(8,128)(2,1)S(1)} %get-tuple-element.197.refs_0_), channel_id=1, source_target_pairs={{0,6},{2,4},{4,2},{6,0},{1,7},{3,5},{5,3},{7,1},{8,14},{10,12},{12... | collective-permute-start | bytes 786440 | tf_op jit(solution)/shard_map/ppermute | solution.py:973
  240.5 12.9 %collective-permute-start.33 = (bf16[64,2048]{1,0:T(8,128)(2,1)S(1)}, bf16[64,2048]{1,0:T(8,128)(2,1)S(1)}, u32[]{:S(2)}, u32[]{:S(2)}) collective-permute-start(bf16[64,2048]{1,0:T(8,128)(2,1)S(1)} %get-tuple-element.197.refs_0_), channel_id=1, source_target_pairs={{0,4},{2,6},{4,0},{6,2},{1,5},{3,7},{5,1},{7,3},{8,12},{10,14},{12... | collective-permute-start | bytes 786440 | tf_op jit(solution)/shard_map/ppermute | solution.py:973
  241.0 12.5 %collective-permute-start.31 = (bf16[64,2048]{1,0:T(8,128)(2,1)S(1)}, bf16[64,2048]{1,0:T(8,128)(2,1)S(1)}, u32[]{:S(2)}, u32[]{:S(2)}) collective-permute-start(bf16[64,2048]{1,0:T(8,128)(2,1)S(1)} %get-tuple-element.197.refs_0_), channel_id=1, source_target_pairs={{0,2},{2,0},{4,6},{6,4},{1,3},{3,1},{5,7},{7,5},{8,10},{10,8},{12,... | collective-permute-start | bytes 786440 | tf_op jit(solution)/shard_map/ppermute | solution.py:973
  255.3 27.4 %collective-permute-start.37 = (bf16[256,2048]{1,0:T(8,128)(2,1)}, bf16[256,2048]{1,0:T(8,128)(2,1)}, u32[]{:S(2)}, u32[]{:S(2)}) collective-permute-start(bf16[256,2048]{1,0:T(8,128)(2,1)} %get-tuple-element.201), channel_id=1, source_target_pairs={{0,1},{1,0},{2,3},{3,2},{4,5},{5,4},{6,7},{7,6},{8,9},{9,8},{10,11... | collective-permute-start | bytes 3145736 | tf_op jit(solution)/shard_map/ppermute | solution.py:985
  261.6 12.4 %all-to-all-start.3 = ((f32[8,8,512]{2,1,0:T(8,128)}), f32[8,8,512]{2,1,0:T(8,128)S(1)}, u32[]{:S(2)}, u32[]{:S(2)}) async-start(f32[8,8,512]{2,1,0:T(8,128)} %copy-done.51), calls=%async_computation.3 | async-start | bytes 262144 | tf_op jit(solution)/shard_map/all_to_all | solution.py:1035
  274.9 14.4 %all-to-all-start.4 = ((bf16[16,64,128]{2,1,0:T(8,128)(2,1)}), bf16[16,64,128]{2,1,0:T(8,128)(2,1)S(1)}, u32[]{:S(2)}, u32[]{:S(2)}) async-start(bf16[16,64,128]{2,1,0:T(8,128)(2,1)} %head_grad.1), calls=%async_computation.4 | async-start | bytes 524288 | tf_op jit(solution)/shard_map/all_to_all | solution.py:1035
  289.3 17.8 %collective-permute-start.38 = (bf16[64,2048]{1,0:T(8,128)(2,1)}, bf16[64,2048]{1,0:T(8,128)(2,1)S(1)}, u32[]{:S(2)}, u32[]{:S(2)}) collective-permute-start(bf16[64,2048]{1,0:T(8,128)(2,1)} %copy-done.70), channel_id=1, source_target_pairs={{0,2},{2,0},{4,6},{6,4},{1,3},{3,1},{5,7},{7,5},{8,10},{10,8},{12,... | collective-permute-start | bytes 786440 | tf_op jit(solution)/shard_map/ppermute | solution.py:996
  290.4 16.6 %collective-permute-start.39 = (bf16[64,2048]{1,0:T(8,128)(2,1)}, bf16[64,2048]{1,0:T(8,128)(2,1)S(1)}, u32[]{:S(2)}, u32[]{:S(2)}) collective-permute-start(bf16[64,2048]{1,0:T(8,128)(2,1)} %copy-done.69), channel_id=1, source_target_pairs={{0,4},{2,6},{4,0},{6,2},{1,5},{3,7},{5,1},{7,3},{8,12},{10,14},{12... | collective-permute-start | bytes 786440 | tf_op jit(solution)/shard_map/ppermute | solution.py:996
  293.1 14.0 %collective-permute-start.40 = (bf16[64,2048]{1,0:T(8,128)(2,1)}, bf16[64,2048]{1,0:T(8,128)(2,1)S(1)}, u32[]{:S(2)}, u32[]{:S(2)}) collective-permute-start(bf16[64,2048]{1,0:T(8,128)(2,1)} %copy-done.68), channel_id=1, source_target_pairs={{0,6},{2,4},{4,2},{6,0},{1,7},{3,5},{5,3},{7,1},{8,14},{10,12},{12... | collective-permute-start | bytes 786440 | tf_op jit(solution)/shard_map/ppermute | solution.py:996
  332.0 9.6 %collective-permute-start.41 = (bf16[144,1024]{1,0:T(8,128)(2,1)}, bf16[144,1024]{1,0:T(8,128)(2,1)S(1)}, u32[]{:S(2)}, u32[]{:S(2)}) collective-permute-start(bf16[144,1024]{1,0:T(8,128)(2,1)} %get-tuple-element.219), channel_id=1, source_target_pairs={{0,8},{8,16},{16,24},{24,0},{1,9},{9,17},{17,25},{25,1},{2,10},{10... | collective-permute-start | bytes 884744 | tf_op jit(solution)/shard_map/ppermute | solution.py:1025
  347.3 13.3 %collective-permute-start.45 = (bf16[272,1024]{1,0:T(8,128)(2,1)}, bf16[272,1024]{1,0:T(8,128)(2,1)S(1)}, u32[]{:S(2)}, u32[]{:S(2)}) collective-permute-start(bf16[272,1024]{1,0:T(8,128)(2,1)} %get-tuple-element.225), channel_id=1, source_target_pairs={{0,8},{8,16},{16,24},{24,0},{1,9},{9,17},{17,25},{25,1},{2,10},{10... | collective-permute-start | bytes 1671176 | tf_op jit(solution)/shard_map/ppermute | solution.py:1029
  347.3 13.3 %collective-permute-start.46 = (bf16[272,1024]{1,0:T(8,128)(2,1)}, bf16[272,1024]{1,0:T(8,128)(2,1)}, u32[]{:S(2)}, u32[]{:S(2)}) collective-permute-start(bf16[272,1024]{1,0:T(8,128)(2,1)} %get-tuple-element.226), channel_id=1, source_target_pairs={{0,24},{8,0},{16,8},{24,16},{1,25},{9,1},{17,9},{25,17},{2,26},{10... | collective-permute-start | bytes 1671176 | tf_op jit(solution)/shard_map/ppermute | solution.py:1029
  349.9 10.6 %collective-permute-start.47 = (bf16[256,1024]{1,0:T(8,128)(2,1)}, bf16[256,1024]{1,0:T(8,128)(2,1)}, u32[]{:S(2)}, u32[]{:S(2)}) collective-permute-start(bf16[256,1024]{1,0:T(8,128)(2,1)} %get-tuple-element.228), channel_id=1, source_target_pairs={{0,32},{32,64},{64,96},{96,0},{1,33},{33,65},{65,97},{97,1},{2,34}... | collective-permute-start | bytes 1572872 | tf_op jit(solution)/shard_map/ppermute | solution.py:1029
  349.9 10.6 %collective-permute-start.48 = (bf16[256,1024]{1,0:T(8,128)(2,1)}, bf16[256,1024]{1,0:T(8,128)(2,1)}, u32[]{:S(2)}, u32[]{:S(2)}) collective-permute-start(bf16[256,1024]{1,0:T(8,128)(2,1)} %get-tuple-element.229), channel_id=1, source_target_pairs={{0,96},{32,0},{64,32},{96,64},{1,97},{33,1},{65,33},{97,65},{2,98}... | collective-permute-start | bytes 1572872 | tf_op jit(solution)/shard_map/ppermute | solution.py:1029
  360.6 11.4 %collective-permute-start.55 = (bf16[256,2048]{1,0:T(8,128)(2,1)}, bf16[256,2048]{1,0:T(8,128)(2,1)S(1)}, u32[]{:S(2)}, u32[]{:S(2)}) collective-permute-start(bf16[256,2048]{1,0:T(8,128)(2,1)} %copy-done.64), channel_id=1, source_target_pairs={{0,1},{1,0},{2,3},{3,2},{4,5},{5,4},{6,7},{7,6},{8,9},{9,8},{10,11... | collective-permute-start | bytes 3145736 | tf_op jit(solution)/shard_map/ppermute | solution.py:985
  368.7 14.9 %collective-permute-start.49 = (bf16[80,1024]{1,0:T(8,128)(2,1)S(1)}, bf16[80,1024]{1,0:T(8,128)(2,1)S(1)}, u32[]{:S(2)}, u32[]{:S(2)}) collective-permute-start(bf16[80,1024]{1,0:T(8,128)(2,1)S(1)} %get-tuple-element.231), channel_id=1, source_target_pairs={{0,32},{32,64},{64,96},{96,0},{1,33},{33,65},{65,97},{97,1},{2,34}... | collective-permute-start | bytes 491528 | tf_op jit(solution)/shard_map/ppermute | solution.py:1015
  369.2 11.4 %collective-permute-start.53 = (bf16[64,1024]{1,0:T(8,128)(2,1)S(1)}, bf16[64,1024]{1,0:T(8,128)(2,1)S(1)}, u32[]{:S(2)}, u32[]{:S(2)}) collective-permute-start(bf16[64,1024]{1,0:T(8,128)(2,1)S(1)} %get-tuple-element.236), channel_id=1, source_target_pairs={{0,16},{8,24},{16,0},{24,8},{1,17},{9,25},{17,1},{25,9},{2,18},{10... | collective-permute-start | bytes 393224 | tf_op jit(solution)/shard_map/ppermute | solution.py:1016
  370.6 10.9 %collective-permute-start.54 = (bf16[64,1024]{1,0:T(8,128)(2,1)S(1)}, bf16[64,1024]{1,0:T(8,128)(2,1)S(1)}, u32[]{:S(2)}, u32[]{:S(2)}) collective-permute-start(bf16[64,1024]{1,0:T(8,128)(2,1)S(1)} %get-tuple-element.237), channel_id=1, source_target_pairs={{0,24},{8,0},{16,8},{24,16},{1,25},{9,1},{17,9},{25,17},{2,26},{10... | collective-permute-start | bytes 393224 | tf_op jit(solution)/shard_map/ppermute | solution.py:1016
  371.9 12.0 %collective-permute-start.50 = (bf16[80,1024]{1,0:T(8,128)(2,1)S(1)}, bf16[80,1024]{1,0:T(8,128)(2,1)S(1)}, u32[]{:S(2)}, u32[]{:S(2)}) collective-permute-start(bf16[80,1024]{1,0:T(8,128)(2,1)S(1)} %get-tuple-element.232), channel_id=1, source_target_pairs={{0,64},{32,96},{64,0},{96,32},{1,65},{33,97},{65,1},{97,33},{2,66}... | collective-permute-start | bytes 491528 | tf_op jit(solution)/shard_map/ppermute | solution.py:1015
  378.1 19.7 %collective-permute-start.59 = (bf16[64,2048]{1,0:T(8,128)(2,1)}, bf16[64,2048]{1,0:T(8,128)(2,1)S(1)}, u32[]{:S(2)}, u32[]{:S(2)}) collective-permute-start(bf16[64,2048]{1,0:T(8,128)(2,1)} %get-tuple-element.256), channel_id=1, source_target_pairs={{0,6},{2,4},{4,2},{6,0},{1,7},{3,5},{5,3},{7,1},{8,14},{10,12},{12... | collective-permute-start | bytes 786440 | tf_op jit(solution)/shard_map/ppermute | solution.py:996
  380.7 17.1 %collective-permute-start.57 = (bf16[64,2048]{1,0:T(8,128)(2,1)}, bf16[64,2048]{1,0:T(8,128)(2,1)S(1)}, u32[]{:S(2)}, u32[]{:S(2)}) collective-permute-start(bf16[64,2048]{1,0:T(8,128)(2,1)} %get-tuple-element.251), channel_id=1, source_target_pairs={{0,4},{4,0},{1,5},{5,1},{2,6},{6,2},{3,7},{7,3},{8,12},{12,8},{9,1... | collective-permute-start | bytes 786440 | tf_op jit(solution)/shard_map/ppermute | solution.py:1307
  381.6 16.2 %collective-permute-start.58 = (bf16[64,2048]{1,0:T(8,128)(2,1)}, bf16[64,2048]{1,0:T(8,128)(2,1)S(1)}, u32[]{:S(2)}, u32[]{:S(2)}) collective-permute-start(bf16[64,2048]{1,0:T(8,128)(2,1)} %get-tuple-element.253), channel_id=1, source_target_pairs={{0,4},{2,6},{4,0},{6,2},{1,5},{3,7},{5,1},{7,3},{8,12},{10,14},{12... | collective-permute-start | bytes 786440 | tf_op jit(solution)/shard_map/ppermute | solution.py:996
  383.6 14.2 %collective-permute-start.56 = (bf16[64,2048]{1,0:T(8,128)(2,1)}, bf16[64,2048]{1,0:T(8,128)(2,1)S(1)}, u32[]{:S(2)}, u32[]{:S(2)}) collective-permute-start(bf16[64,2048]{1,0:T(8,128)(2,1)} %get-tuple-element.249), channel_id=1, source_target_pairs={{0,2},{2,0},{4,6},{6,4},{1,3},{3,1},{5,7},{7,5},{8,10},{10,8},{12,... | collective-permute-start | bytes 786440 | tf_op jit(solution)/shard_map/ppermute | solution.py:996
  390.0 15.6 %all-to-all-start.6 = ((bf16[8,8,2048]{2,1,0:T(8,128)(2,1)}), bf16[8,8,2048]{2,1,0:T(8,128)(2,1)S(1)}, u32[]{:S(2)}, u32[]{:S(2)}) async-start(bf16[8,8,2048]{2,1,0:T(8,128)(2,1)} %get-tuple-element.242), calls=%async_computation.7 | async-start | bytes 524288 | tf_op jit(solution)/shard_map/all_to_all | solution.py:1035
  398.3 26.2 %collective-permute-start.61 = (bf16[4,16,2048]{2,1,0:T(8,128)(2,1)S(1)}, bf16[4,16,2048]{2,1,0:T(8,128)(2,1)S(1)}, u32[]{:S(2)}, u32[]{:S(2)}) collective-permute-start(bf16[4,16,2048]{2,1,0:T(8,128)(2,1)S(1)} %bitcast.72), channel_id=1, source_target_pairs={{0,2},{2,0},{1,3},{3,1},{4,6},{6,4},{5,7},{7,5},{8,10},{10,8},{9,1... | collective-permute-start | bytes 786440 | tf_op jit(solution)/shard_map/ppermute | solution.py:1337
  400.1 26.2 %collective-permute-start.60 = (bf16[4,16,2048]{2,1,0:T(8,128)(2,1)S(1)}, bf16[4,16,2048]{2,1,0:T(8,128)(2,1)S(1)}, u32[]{:S(2)}, u32[]{:S(2)}) collective-permute-start(bf16[4,16,2048]{2,1,0:T(8,128)(2,1)S(1)} %bitcast.73), channel_id=1, source_target_pairs={{0,1},{1,0},{2,3},{3,2},{4,5},{5,4},{6,7},{7,6},{8,9},{9,8},{10,11... | collective-permute-start | bytes 786440 | tf_op jit(solution)/shard_map/ppermute | solution.py:1338
  406.3 11.2 %all-to-all-start.7 = ((f32[16,8,128]{2,1,0:T(8,128)}), f32[16,8,128]{2,1,0:T(8,128)S(1)}, u32[]{:S(2)}, u32[]{:S(2)}) async-start(f32[16,8,128]{2,1,0:T(8,128)} %get-tuple-element.260), calls=%async_computation.8 | async-start | bytes 131072 | tf_op jit(solution)/shard_map/all_to_all | solution.py:1035
  (124 other events, 1338.0 us)
Sparse Core Ops, SparseCore 0:
  17.1 54.9 all-gather.2
  74.8 79.5 all-gather.4
  233.5 84.6 reduce-scatter.1
